TPU v7x, 128 devices: a whole 4x4x4 slice. The times are simulated.
128 devices in a mesh: lon: 8 (over x, y_lo), lat: 16 (over z, y_hi, core).
Axes of the slice: x: 4, y: 4 (y_hi: 2, y_lo: 2; y = y_hi * 2 + y_lo), z: 4, core: 2. Of those that a mesh axis runs over, the one named last changes fastest.
Arguments:
- fields: bfloat16 [768, 1024, 128], P('lon', 'lat'), may hold values from -6 to 6
- land_sea: int32 [768, 1024], P('lon', 'lat'), may hold values 0 or 1
- tile_list: int32 [8, 16, 72], P('lon', 'lat'), may hold values from -1 to 95, as said below
- upstream: bfloat16 [768, 1024, 128], P('lon', 'lat'), may hold values from -6 to 6
- dw_weight: float32 [49, 128], replicated, may hold values from -0.875 to 0.875
- dw_bias: float32 [128], replicated, may hold values from -3 to 3
- ln_gain: float32 [128], replicated, may hold values from 0.1 to 1.9
- ln_bias: float32 [128], replicated, may hold values from -3 to 3
- w_in: bfloat16 [128, 512], replicated, may hold values from -0.5 to 0.5
- b_in: float32 [512], replicated, may hold values from -3 to 3
- w_out: bfloat16 [512, 128], replicated, may hold values from -0.25 to 0.25
- b_out: float32 [128], replicated, may hold values from -3 to 3
- layer_scale: float32 [128], replicated, may hold values from 0.3 to 1.5
Outputs:
- mixed: bfloat16 [768, 1024, 128], P('lon', 'lat')
- grad_input: bfloat16 [768, 1024, 128], P('lon', 'lat')
- grad_w_in: float32 [128, 512], P(None, 'lat')
- grad_w_out: float32 [512, 128], P('lat')
- grad_dw: float32 [49, 128], P(None, 'lat')
- grad_channel: float32 [5, 128], P(None, 'lat')
- grad_b_in: float32 [512], P('lat')
Inputs may be any that keep to these rules, and one draw needn't show every extreme that they name: `tile_list`: each device's 72 entries hold distinct tile numbers of its block, followed by -1 in unused slots; at least 24 entries are used, and some device uses all 72.
All inputs are finite; a program needn't handle non-finite values. No bound on the sum of `land_sea` on one device may be relied on, other than what follows from the above.
Results may differ from a plain program's by a relative error of at most 0.0064.
Values may be sent and summed in bfloat16 or wider, within the bound.
A program may use at most 128 MiB of HBM per device.

v0:
```python
import math

import jax
import jax.numpy as jnp
from jax import lax
from jax.sharding import PartitionSpec as P

LN_EPSILON = 1e-06


def with_halo(cells, sides, width):
    for axis, dim in sides:
        count = lax.axis_size(axis)
        head = lax.slice_in_dim(cells, 0, width, axis=dim)
        tail = lax.slice_in_dim(cells, cells.shape[dim] - width, cells.shape[dim], axis=dim)
        cells = jnp.concatenate(
            [
                lax.ppermute(tail, axis, [(i, (i + 1) % count) for i in range(count)]),
                cells,
                lax.ppermute(head, axis, [((i + 1) % count, i) for i in range(count)]),
            ],
            axis=dim,
        )
    return cells


def conv_taps(padded, weight, lon_cells, lat_cells):
    running = jnp.zeros((lon_cells, lat_cells, padded.shape[2]), jnp.float32)
    for a in range(7):
        for b in range(7):
            running = (
                running
                + padded[a : a + lon_cells, b : b + lat_cells].astype(jnp.float32)
                * weight[a * 7 + b]
            )
    return running


def backward_taps(grad_pad, padded, weight, lon_cells, lat_cells):
    running = jnp.zeros((lon_cells, lat_cells, padded.shape[2]), jnp.float32)
    d_conv = grad_pad[3 : 3 + lon_cells, 3 : 3 + lat_cells].astype(jnp.float32)
    tap_sums = []
    for a in range(7):
        for b in range(7):
            running = (
                running
                + grad_pad[6 - a : 6 - a + lon_cells, 6 - b : 6 - b + lat_cells].astype(jnp.float32)
                * weight[a * 7 + b]
            )
            tap_sums.append(
                jnp.sum(
                    padded[a : a + lon_cells, b : b + lat_cells].astype(jnp.float32) * d_conv,
                    axis=(0, 1),
                )
            )
    return (running, jnp.stack(tap_sums))


def to_tiles(cell_grid):
    shape_in = cell_grid.shape
    trailing = shape_in[2:]
    r = cell_grid.reshape((shape_in[0] // 8, 8, shape_in[1] // 8, 8) + trailing)
    r = jnp.swapaxes(r, 1, 2)
    return r.reshape((shape_in[0] // 8 * (shape_in[1] // 8), 64) + trailing)


def from_tiles(tile_stack, lon_cells, lat_cells):
    trailing = tile_stack.shape[2:]
    r = tile_stack.reshape((lon_cells // 8, lat_cells // 8, 8, 8) + trailing)
    r = jnp.swapaxes(r, 1, 2)
    return r.reshape((lon_cells, lat_cells) + trailing)


def gelu_slope(hidden):
    normal_cdf = 0.5 * (1.0 + lax.erf(hidden * (1.0 / math.sqrt(2.0))))
    normal_pdf = jnp.exp(-0.5 * hidden * hidden) * (1.0 / math.sqrt(2.0 * math.pi))
    return normal_cdf + hidden * normal_pdf


def contract_rows(first_op, second_op):
    return lax.dot_general(
        first_op, second_op, (((0,), (0,)), ((), ())), preferred_element_type=jnp.float32
    )


def contract_cols(first_op, second_op):
    return lax.dot_general(
        first_op, second_op, (((1,), (1,)), ((), ())), preferred_element_type=jnp.float32
    )


def cell_rows(conv_rows, active, up_rows, params):
    ln_gain, ln_bias, w_in, b_in, w_out, b_out, layer_scale = params
    center = conv_rows - jnp.mean(conv_rows, axis=-1, keepdims=True)
    variance = jnp.mean(center * center, axis=-1, keepdims=True)
    inv_std = lax.rsqrt(variance + LN_EPSILON)
    normed = center * inv_std
    normed_b = (normed * ln_gain + ln_bias).astype(jnp.bfloat16)
    hidden = jnp.dot(normed_b, w_in, preferred_element_type=jnp.float32) + b_in
    activated = jax.nn.gelu(hidden, approximate=False).astype(jnp.bfloat16)
    output = jnp.dot(activated, w_out, preferred_element_type=jnp.float32) + b_out
    branch = active[:, None] * layer_scale * output
    up_float = up_rows.astype(jnp.float32)
    d_out = active[:, None] * layer_scale * up_float
    d_out_b = d_out.astype(jnp.bfloat16)
    g_wout = contract_rows(activated, d_out_b)
    g_scale = jnp.sum(active[:, None] * output * up_float, axis=0)
    d_hidden = contract_cols(d_out_b, w_out) * gelu_slope(hidden)
    d_hidden_b = d_hidden.astype(jnp.bfloat16)
    g_win = contract_rows(normed_b, d_hidden_b)
    d_norm = contract_cols(d_hidden_b, w_in)
    d_scaled = d_norm * ln_gain
    d_conv = inv_std * (
        d_scaled
        - jnp.mean(d_scaled, axis=-1, keepdims=True)
        - normed * jnp.mean(d_scaled * normed, axis=-1, keepdims=True)
    )
    channel_sums = jnp.stack(
        [
            jnp.sum(d_conv, axis=0),
            jnp.sum(d_norm * normed, axis=0),
            jnp.sum(d_norm, axis=0),
            jnp.sum(d_out, axis=0),
            g_scale,
        ]
    )
    grad_terms = (g_win, g_wout, jnp.sum(d_hidden, axis=0), channel_sums)
    return (branch, d_conv.astype(jnp.bfloat16), grad_terms)


def listed_rows(conv_out, land_float, up_grid, tile_ids, params):
    lon_cells, lat_cells, channels = conv_out.shape
    tile_count = lon_cells // 8 * (lat_cells // 8)
    slot_count = tile_ids.shape[0]
    slot_tile = jnp.maximum(tile_ids, 0)
    slot_live = (tile_ids >= 0).astype(jnp.float32)
    conv_rows = to_tiles(conv_out)[slot_tile].reshape(-1, channels)
    active = (to_tiles(land_float)[slot_tile] * slot_live[:, None]).reshape(-1)
    up_rows = to_tiles(up_grid)[slot_tile].reshape(-1, channels)
    branch, d_conv_b, grad_terms = cell_rows(conv_rows, active, up_rows, params)
    branch_tiles = (
        jnp.zeros((tile_count, 64, channels), jnp.float32)
        .at[slot_tile]
        .add(branch.reshape(slot_count, 64, channels))
    )
    d_conv_tiles = (
        jnp.zeros((tile_count, 64, channels), jnp.bfloat16)
        .at[slot_tile]
        .add(d_conv_b.reshape(slot_count, 64, channels))
    )
    return (
        from_tiles(branch_tiles, lon_cells, lat_cells),
        from_tiles(d_conv_tiles, lon_cells, lat_cells),
        grad_terms,
    )


def lat_keep(lat_cells, width, lat_place, lat_count):
    edge_pos = jnp.arange(lat_cells + 2 * width)
    outside = (edge_pos < width) & (lat_place == 0) | (edge_pos >= lat_cells + width) & (
        lat_place == lat_count - 1
    )
    return jnp.logical_not(outside)


def per_device(
    fields,
    land_sea,
    tile_list,
    upstream,
    dw_weight,
    dw_bias,
    ln_gain,
    ln_bias,
    w_in,
    b_in,
    w_out,
    b_out,
    layer_scale,
):
    lon_cells, lat_cells, channels = fields.shape
    params = (ln_gain, ln_bias, w_in, b_in, w_out, b_out, layer_scale)
    lat_place = lax.axis_index("lat")
    lat_count = lax.axis_size("lat")
    rim_keep = lat_keep(lat_cells, 3, lat_place, lat_count).astype(jnp.bfloat16)[None, :, None]
    land_float = land_sea.astype(jnp.float32)
    masked = fields * land_sea.astype(jnp.bfloat16)[:, :, None]
    tile_ids = tile_list.reshape(-1)
    padded = with_halo(masked, (("lon", 0), ("lat", 1)), 3) * rim_keep
    conv_out = conv_taps(padded, dw_weight, lon_cells, lat_cells) + dw_bias
    branch_grid, d_conv_grid, grad_terms = listed_rows(
        conv_out, land_float, upstream, tile_ids, params
    )
    mixed = (fields.astype(jnp.float32) + branch_grid).astype(jnp.bfloat16)
    grad_pad = with_halo(d_conv_grid, (("lon", 0), ("lat", 1)), 3) * rim_keep
    masked_grad, tap_sums = backward_taps(grad_pad, padded, dw_weight, lon_cells, lat_cells)
    grad_input = (upstream.astype(jnp.float32) + land_float[:, :, None] * masked_grad).astype(
        jnp.bfloat16
    )
    grad_scale = 1.0 / math.sqrt(lon_cells * lax.axis_size("lon") * lat_cells * lat_count)
    g_win, g_wout, g_bin, channel_sums = grad_terms
    part_win = g_win * grad_scale
    part_wout = g_wout * grad_scale
    part_taps = tap_sums * grad_scale
    part_chan = channel_sums * grad_scale
    part_bin = g_bin * grad_scale
    whole_win, whole_wout, whole_taps, whole_chan, whole_bin = lax.psum(
        (part_win, part_wout, part_taps, part_chan, part_bin), "lon"
    )
    share_win, share_wout, share_taps, share_chan, share_bin = (
        lax.psum_scatter(whole_win, "lat", scatter_dimension=1, tiled=True),
        lax.psum_scatter(whole_wout, "lat", scatter_dimension=0, tiled=True),
        lax.psum_scatter(whole_taps, "lat", scatter_dimension=1, tiled=True),
        lax.psum_scatter(whole_chan, "lat", scatter_dimension=1, tiled=True),
        lax.psum_scatter(whole_bin, "lat", scatter_dimension=0, tiled=True),
    )
    return (mixed, grad_input, share_win, share_wout, share_taps, share_chan, share_bin)


def solution(mesh):
    return jax.shard_map(
        per_device,
        mesh=mesh,
        in_specs=(
            P("lon", "lat", None),
            P("lon", "lat"),
            P("lon", "lat", None),
            P("lon", "lat", None),
            P(),
            P(),
            P(),
            P(),
            P(),
            P(),
            P(),
            P(),
            P(),
        ),
        out_specs=(
            P("lon", "lat", None),
            P("lon", "lat", None),
            P(None, "lat"),
            P("lat", None),
            P(None, "lat"),
            P(None, "lat"),
            P("lat"),
        ),
        check_vma=False,
    )
```

profile of v0, /device:TPU:0, one launch (start us, length us, event | category | flops | bytes accessed | tf_op | source)
XLA Modules:
  0.0 339.9 jit_solution(5862877423233817542)
XLA Ops:
  7.3 0.9 fusion.153
  8.3 2.1 broadcast_multiply_fusion
  11.1 1.7 collective-permute-start
  12.8 2.5 collective-permute-start.1
  17.3 0.9 reshape.208
  18.2 1.8 copy.39
  20.0 1.2 reshape.209
  21.2 1.6 copy.44
  23.4 2.2 gather_fusion.2
  25.7 1.4 fusion.139
  29.3 5.7 %collective-permute-start.3 = (bf16[102,3,128]{2,1,0:T(4,128)(2,1)S(1)}, bf16[102,3,128]{2,1,0:T(4,128)(2,1)S(1)}, u32[]{:S(2)}, u32[]{:S(2)}) collective-permute-start(bf16[102,3,128]{2,1,0:T(4,128)(2,1)S(1)} %get-tuple-element.107), channel_id=1, source_target_pairs={{1,0},{2,1},{3,2},{4,3},{5,4},{6,5},{7,6},{8,7},{9,8},{10,9},{11,1... | collective-permute-start | bytes 235016 | tf_op jit(solution)/shard_map/ppermute | solution.py:20
  35.0 2.3 collective-permute-done.2
  37.3 2.4 maximum_multiply_fusion
  39.8 23.5 %fusion.137 = f32[96,64,128]{2,1,0:T(8,128)S(1)} fusion(f32[128]{0:T(128)} %param.18, f32[128]{0:T(128)} %get-tuple-element.162, f32[128]{0:T(128)} %get-tuple-element.163, f32[128]{0:T(128)S(1)} %get-tuple-element.116, f32[128]{0:T(128)S(1)} %copy-done.11, f32[128]{0:T(128)S(1)} %copy-done.12, f32[128]{0:T(128)S(1)} %copy-done.14, f32[128]{0:T(128)S(1)} %copy-done.16, ...), kind=kLoop, calls=%fused_computation.256 | loop fusion | flops 115605504 | bytes 80241664 | tf_op jit(solution)/shard_map/add | solution.py:190
  63.3 2.1 copy.41
  65.4 4.1 %gather_fusion.1 = f32[72,64,128]{2,1,0:T(8,128)} fusion(f32[96,64,128]{2,1,0:T(8,128)} %bitcast.219, s32[1024]{0:T(1024)S(1)} %pad_clamp_fusion), kind=kCustom, calls=%fused_computation.1 | custom fusion | bytes 4718880 | tf_op jit(solution)/shard_map/gather | solution.py:137
  69.5 2.4 reduce_sum.531
  71.9 2.9 multiply_reduce_fusion.2
  74.9 3.9 %add_convert_fusion.2 = bf16[4608,128]{1,0:T(8,128)(2,1)S(1)} fusion(f32[72,64,128]{2,1,0:T(8,128)} %gather_fusion.1, f32[128]{0:T(128)S(1)} %copy-done.61, f32[128]{0:T(128)S(1)} %copy-done.59, f32[4608]{0:T(1024)S(1)} %rsqrt.12, f32[4608]{0:T(1024)S(1)} %div.15), kind=kLoop, calls=%fused_computation.271 | loop fusion | flops 2949120 | bytes 3576832 | tf_op jit(solution)/shard_map/convert_element_type | solution.py:98
  78.9 22.9 %fusion.2 = (bf16[4608,512]{1,0:T(8,128)(2,1)S(1)}, f32[4608,512]{1,0:T(8,128)}) fusion(f32[512]{0:T(512)S(1)} %copy-done.66, bf16[4608,128]{1,0:T(8,128)(2,1)S(1)} %add_convert_fusion.2, bf16[128,512]{1,0:T(8,128)(2,1)S(1)} %copy-done), kind=kOutput, calls=%fused_computation.59 | convolution fusion | flops 759693312 | bytes 15468544 | tf_op jit(solution)/shard_map/dot_general | solution.py:99
  101.8 3.2 fusion.140
  105.0 1.0 copy-done.9
  106.1 2.1 convolution_multiply_fusion
  108.2 7.6 %fusion.154 = (f32[512]{0:T(512)S(1)}, bf16[4608,512]{1,0:T(8,128)(2,1)S(1)}) fusion(f32[4608,512]{1,0:T(8,128)} %get-tuple-element.165, f32[512]{0:T(512)S(1)} %copy-done.66, bf16[4608,128]{1,0:T(8,128)(2,1)} %copy-done.9, bf16[512,128]{1,0:T(8,128)(2,1)S(1)} %copy-done.65), kind=kOutput, calls=%fused_computation.353 | convolution fusion | flops 632290816 | bytes 15470592 | tf_op jit(solution)/shard_map/dot_general | solution.py:87
  115.8 4.7 %multiply_reduce_fusion = (f32[128]{0:T(128)S(1)}, f32[4608]{0:T(1024)S(1)}, f32[4608]{0:T(1024)S(1)}, f32[128]{0:T(128)S(1)}, f32[4608,128]{1,0:T(8,128)}) fusion(f32[72,64,128]{2,1,0:T(8,128)S(1)} %copy-done.1, f32[4608]{0:T(1024)S(1)} %rsqrt.12, f32[4608]{0:T(1024)S(1)} %div.15, f32[128]{0:T(128)S(1)} %copy-done.59, bf16[128,512]{1,0:T(8,128)(2,1)S(1)} %copy-done, ...), kind=kOutput, calls=%fused_computation.264 | convolution fusion | flops 609278720 | bytes 9643520 | tf_op jit(solution)/shard_map/dot_general | solution.py:87
  120.6 2.7 fusion.146
  123.3 5.7 %fusion.150 = (f32[128]{0:T(128)S(1)}, bf16[4608,128]{1,0:T(8,128)(2,1)S(1)}) fusion(f32[4608]{0:T(1024)S(1)} %get-tuple-element.169, f32[4608]{0:T(1024)S(1)} %div.15, f32[72,64,128]{2,1,0:T(8,128)} %gather_fusion.1, f32[4608]{0:T(1024)S(1)} %get-tuple-element.170, f32[4608,128]{1,0:T(8,128)} %get-tuple-element.166, f32[128]{0:T(128)S(1)} %copy-done.59, ...), kind=kLoop, calls=%fused_computation.349 | loop fusion | flops 5308288 | bytes 5972992 | tf_op jit(solution)/shard_map/reduce_sum | solution.py:120
  129.0 1.5 broadcast_in_dim.5
  130.5 12.6 %scatter_fusion.1 = bf16[96,64,128]{2,1,0:T(8,128)(2,1)} fusion(bf16[96,64,128]{2,1,0:T(8,128)(2,1)} %broadcast_in_dim.5, s32[72]{0:T(128)S(1)} %copy-done.58, bf16[72,64,128]{2,1,0:T(8,128)(2,1)S(1)} %bitcast.222), kind=kCustom, calls=%fused_computation.4 | custom fusion | flops 589824 | bytes 3539232 | tf_op jit(solution)/shard_map/scatter-add | solution.py:149
  143.1 1.8 copy.45
  145.0 1.1 copy-done.3
  146.2 4.1 %collective-permute-start.5 = (bf16[3,64,128]{2,1,0:T(8,128)(2,1)S(1)}, bf16[3,64,128]{2,1,0:T(8,128)(2,1)S(1)}, u32[]{:S(2)}, u32[]{:S(2)}) collective-permute-start(bf16[3,64,128]{2,1,0:T(8,128)(2,1)S(1)} %get-tuple-element.109), channel_id=1, source_target_pairs={{16,0},{32,16},{48,32},{64,48},{80,64},{96,80},{112,96},{0,112},{1... | collective-permute-start | bytes 147464 | tf_op jit(solution)/shard_map/ppermute | solution.py:20
  150.4 2.1 broadcast_in_dim.4
  152.5 12.8 %scatter_fusion = f32[96,64,128]{2,1,0:T(8,128)} fusion(f32[96,64,128]{2,1,0:T(8,128)} %broadcast_in_dim.4, s32[72]{0:T(128)S(1)} %copy-done.58, f32[72,64,128]{2,1,0:T(8,128)} %bitcast.223), kind=kCustom, calls=%fused_computation.3 | custom fusion | flops 589824 | bytes 7078176 | tf_op jit(solution)/shard_map/scatter-add | solution.py:144
  165.3 2.5 copy.42
  167.7 1.7 add_convert_fusion.1
  169.5 1.1 pad_maximum_fusion.2
  170.7 5.3 %collective-permute-start.7 = (bf16[102,3,128]{2,1,0:T(4,128)(2,1)S(1)}, bf16[102,3,128]{2,1,0:T(4,128)(2,1)S(1)}, u32[]{:S(2)}, u32[]{:S(2)}) collective-permute-start(bf16[102,3,128]{2,1,0:T(4,128)(2,1)S(1)} %get-tuple-element.105), channel_id=1, source_target_pairs={{1,0},{2,1},{3,2},{4,3},{5,4},{6,5},{7,6},{8,7},{9,8},{10,9},{11,1... | collective-permute-start | bytes 235016 | tf_op jit(solution)/shard_map/ppermute | solution.py:20
  176.1 2.3 collective-permute-done.6
  178.4 2.4 maximum_multiply_fusion.1
  180.8 4.8 %fusion.127 = (f32[128]{0:T(128)S(1)}, f32[128]{0:T(128)S(1)}, f32[128]{0:T(128)S(1)}, f32[128]{0:T(128)S(1)}, f32[128]{0:T(128)S(1)}, /*index=5*/f32[128]{0:T(1...) fusion(bf16[102,70,128]{2,1,0:T(8,128)(2,1)S(1)} %maximum_multiply_fusion, ...), kind=kLoop, calls=%fused_computation.244 | loop fusion | flops 22018944 | bytes 15733248 | tf_op jit(solution)/shard_map/reduce_sum | solution.py:51
  185.6 4.5 %fusion.118 = (f32[128]{0:T(128)S(1)}, f32[128]{0:T(128)S(1)}, f32[128]{0:T(128)S(1)}, f32[128]{0:T(128)S(1)}, f32[128]{0:T(128)S(1)}, /*index=5*/f32[128]{0:T(1...) fusion(bf16[102,70,128]{2,1,0:T(8,128)(2,1)S(1)} %maximum_multiply_fusion, ...), kind=kLoop, calls=%fused_computation.235 | loop fusion | flops 22018944 | bytes 15733248 | tf_op jit(solution)/shard_map/reduce_sum | solution.py:51
  190.1 4.3 %fusion.109 = (f32[128]{0:T(128)S(1)}, f32[128]{0:T(128)S(1)}, f32[128]{0:T(128)S(1)}, f32[128]{0:T(128)S(1)}, f32[128]{0:T(128)S(1)}, /*index=5*/f32[128]{0:T(1...) fusion(bf16[102,70,128]{2,1,0:T(8,128)(2,1)S(1)} %maximum_multiply_fusion, ...), kind=kLoop, calls=%fused_computation.226 | loop fusion | flops 22018944 | bytes 15733248 | tf_op jit(solution)/shard_map/reduce_sum | solution.py:51
  194.4 4.3 %fusion.100 = (f32[128]{0:T(128)S(1)}, f32[128]{0:T(128)S(1)}, f32[128]{0:T(128)S(1)}, f32[128]{0:T(128)S(1)}, f32[128]{0:T(128)S(1)}, /*index=5*/f32[128]{0:T(1...) fusion(bf16[102,70,128]{2,1,0:T(8,128)(2,1)S(1)} %maximum_multiply_fusion, ...), kind=kLoop, calls=%fused_computation.217 | loop fusion | flops 22018944 | bytes 15733248 | tf_op jit(solution)/shard_map/reduce_sum | solution.py:51
  199.2 6.2 %fusion.136 = (f32[128]{0:T(128)S(1)}, f32[128]{0:T(128)S(1)}, f32[128]{0:T(128)S(1)}, f32[128]{0:T(128)S(1)}, f32[128]{0:T(128)S(1)}, /*index=5*/f32[128]{0:T(1...) fusion(bf16[102,70,128]{2,1,0:T(8,128)(2,1)S(1)} %maximum_multi, ...), kind=kLoop, calls=%fused_computation.253 | loop fusion | flops 31455616 | bytes 22026752 | tf_op jit(solution)/shard_map/reduce_sum | solution.py:51
  205.7 23.6 %add_convert_fusion = bf16[96,64,128]{2,1,0:T(8,128)(2,1)} fusion(bf16[96,64,128]{2,1,0:T(8,128)(2,1)S(1)} %copy-done.6, bf16[102,70,128]{2,1,0:T(8,128)(2,1)S(1)} %maximum_multiply_fusion.1, f32[96,64]{1,0:T(8,128)S(1)} %copy.38, f32[128]{0:T(128)} %get-tuple-element.162, f32[128]{0:T(128)} %get-tuple-element.163, f32[128]{0:T(128)S(1)} %get-tuple-element.116, ...), kind=kLoop, calls=%fused_computation.254 | loop fusion | flops 117964800 | bytes 80265728 | tf_op jit(solution)/shard_map/convert_element_type | solution.py:197
  229.5 70.2 %all-reduce.3 = (f32[49,128]{1,0:T(8,128)S(1)}, f32[5,128]{1,0:T(8,128)S(1)}, f32[512]{0:T(512)S(1)}) all-reduce(f32[49,128]{1,0:T(8,128)S(1)} %broadcast_multiply_fusion.3, f32[5,128]{1,0:T(8,128)S(1)} %broadcast_multiply_fusion.6, f32[512]{0:T(512)S(1)} %broadcast_multiply_fusion.7), channel_id=4, replica_groups=mesh['lon'=8,'lat'=16] {'lat'}, use_global_device_ids=true, to_apply=%region_60.0.clone | all-reduce | flops 7424 | bytes 59392
  299.9 32.5 %all-reduce.4 = (f32[128,32]{0,1:T(8,128)}, f32[32,128]{1,0:T(8,128)}, f32[49,8]{1,0:T(8,128)S(1)}, f32[5,8]{1,0:T(8,128)}, f32[32]{0:T(128)}) all-reduce(f32[128,32]{0,1:T(8,128)} %reduce-scatter.5.cloned.1.call-done, f32[32,128]{1,0:T(8,128)} %reduce-scatter.7.cloned.1.call-done, ...), channel_id=1, replica_groups=mesh['lon'=8,'lat'=16] {'lon'}, use_global_device_ids=true, to_apply=%region_6.0 | all-reduce | flops 8656 | bytes 69248 | tf_op jit(solution)/shard_map/psum | solution.py:207
  (183 shorter events, 6.2 us)
Async XLA Ops:
  7.2 71.7 %copy-start = (bf16[128,512]{1,0:T(8,128)(2,1)S(1)}, bf16[128,512]{1,0:T(8,128)(2,1)}, u32[]{:S(2)}) copy-start(bf16[128,512]{1,0:T(8,128)(2,1)} %param.21) | copy-start | bytes 393220
  7.2 8.1 %copy-start.10 = (f32[49,128]{1,0:T(8,128)S(1)}, f32[49,128]{1,0:T(8,128)}, u32[]{:S(2)}) copy-start(f32[49,128]{1,0:T(8,128)} %param.17) | copy-start | bytes 75268
  7.2 10.0 %copy-start.67 = (s32[1,1,72]{2,1,0:T(1,128)S(1)}, s32[1,1,72]{2,1,0:T(1,128)}, u32[]{:S(2)}) copy-start(s32[1,1,72]{2,1,0:T(1,128)} %param.15) | copy-start | bytes 868
  7.2 14.0 %copy-start.5 = (bf16[96,64,128]{2,1,0:T(8,128)(2,1)S(1)}, bf16[96,64,128]{2,1,0:T(8,128)(2,1)}, u32[]{:S(2)}) copy-start(bf16[96,64,128]{2,1,0:T(8,128)(2,1)} %param.16) | copy-start | bytes 4718596
  7.2 292.6 %reduce-scatter.7.cloned.1.call-start = ((), (), s32[]{:S(2)}) async-start(), calls=%async_computation.3 | async-start | bytes 278528 | tf_op jit(solution)/shard_map/reduce_scatter | solution.py:212
  10.4 18.7 %copy-start.2 = (bf16[96,64,128]{2,1,0:T(8,128)(2,1)}, bf16[96,64,128]{2,1,0:T(8,128)(2,1)S(1)}, u32[]{:S(2)}) copy-start(bf16[96,64,128]{2,1,0:T(8,128)(2,1)S(1)} %broadcast_multiply_fusion) | copy-start | bytes 4718596
  11.1 18.0 %collective-permute-start = (bf16[3,64,128]{2,1,0:T(8,128)(2,1)}, bf16[3,64,128]{2,1,0:T(8,128)(2,1)S(1)}, u32[]{:S(2)}, u32[]{:S(2)}) collective-permute-start(bf16[3,64,128]{2,1,0:T(8,128)(2,1)} %get-tuple-element.110), channel_id=1, source_target_pairs={{0,16},{16,32},{32,48},{48,64},{64,80},{80,96},{96,112},{112,0},{1... | collective-permute-start | bytes 147464 | tf_op jit(solution)/shard_map/ppermute | solution.py:18
  12.8 16.3 %collective-permute-start.1 = (bf16[3,64,128]{2,1,0:T(8,128)(2,1)S(1)}, bf16[3,64,128]{2,1,0:T(8,128)(2,1)S(1)}, u32[]{:S(2)}, u32[]{:S(2)}) collective-permute-start(bf16[3,64,128]{2,1,0:T(8,128)(2,1)S(1)} %get-tuple-element.111), channel_id=1, source_target_pairs={{16,0},{32,16},{48,32},{64,48},{80,64},{96,80},{112,96},{0,112},{1... | collective-permute-start | bytes 147464 | tf_op jit(solution)/shard_map/ppermute | solution.py:20
  17.2 8.4 %copy-start.57 = (s32[72]{0:T(128)}, s32[72]{0:T(128)S(1)}, u32[]{:S(2)}) copy-start(s32[72]{0:T(128)S(1)} %maximum_bitcast_fusion) | copy-start | bytes 868
  27.1 12.6 %copy-start.11 = (f32[128]{0:T(128)S(1)}, f32[128]{0:T(128)}, u32[]{:S(2)}) copy-start(f32[128]{0:T(128)} %get-tuple-element.117) | copy-start | bytes 1540
  27.1 12.6 %copy-start.12 = (f32[128]{0:T(128)S(1)}, f32[128]{0:T(128)}, u32[]{:S(2)}) copy-start(f32[128]{0:T(128)} %get-tuple-element.118) | copy-start | bytes 1540
  27.1 12.6 %copy-start.14 = (f32[128]{0:T(128)S(1)}, f32[128]{0:T(128)}, u32[]{:S(2)}) copy-start(f32[128]{0:T(128)} %get-tuple-element.119) | copy-start | bytes 1540
  27.1 12.6 %copy-start.16 = (f32[128]{0:T(128)S(1)}, f32[128]{0:T(128)}, u32[]{:S(2)}) copy-start(f32[128]{0:T(128)} %get-tuple-element.120) | copy-start | bytes 1540
  27.1 12.7 %copy-start.18 = (f32[128]{0:T(128)S(1)}, f32[128]{0:T(128)}, u32[]{:S(2)}) copy-start(f32[128]{0:T(128)} %get-tuple-element.121) | copy-start | bytes 1540
  27.1 12.7 %copy-start.20 = (f32[128]{0:T(128)S(1)}, f32[128]{0:T(128)}, u32[]{:S(2)}) copy-start(f32[128]{0:T(128)} %get-tuple-element.122) | copy-start | bytes 1540
  27.1 12.7 %copy-start.22 = (f32[128]{0:T(128)S(1)}, f32[128]{0:T(128)}, u32[]{:S(2)}) copy-start(f32[128]{0:T(128)} %get-tuple-element.123) | copy-start | bytes 1540
  29.2 8.1 %collective-permute-start.2 = (bf16[102,3,128]{2,1,0:T(4,128)(2,1)S(1)}, bf16[102,3,128]{2,1,0:T(4,128)(2,1)S(1)}, u32[]{:S(2)}, u32[]{:S(2)}) collective-permute-start(bf16[102,3,128]{2,1,0:T(4,128)(2,1)S(1)} %get-tuple-element.106), channel_id=1, source_target_pairs={{0,1},{1,2},{2,3},{3,4},{4,5},{5,6},{6,7},{7,8},{8,9},{9,10},{10,1... | collective-permute-start | bytes 235016 | tf_op jit(solution)/shard_map/ppermute | solution.py:18
  29.3 8.0 %collective-permute-start.3 = (bf16[102,3,128]{2,1,0:T(4,128)(2,1)S(1)}, bf16[102,3,128]{2,1,0:T(4,128)(2,1)S(1)}, u32[]{:S(2)}, u32[]{:S(2)}) collective-permute-start(bf16[102,3,128]{2,1,0:T(4,128)(2,1)S(1)} %get-tuple-element.107), channel_id=1, source_target_pairs={{1,0},{2,1},{3,2},{4,3},{5,4},{6,5},{7,6},{8,7},{9,8},{10,9},{11,1... | collective-permute-start | bytes 235016 | tf_op jit(solution)/shard_map/ppermute | solution.py:20
  71.8 7.0 %copy-start.66 = (f32[512]{0:T(512)S(1)}, f32[512]{0:T(512)}, u32[]{:S(2)}) copy-start(f32[512]{0:T(512)} %param.22) | copy-start | bytes 6148
  78.9 23.0 %copy-start.7 = (bf16[4608,128]{1,0:T(8,128)(2,1)}, bf16[4608,128]{1,0:T(8,128)(2,1)S(1)}, u32[]{:S(2)}) copy-start(bf16[4608,128]{1,0:T(8,128)(2,1)S(1)} %add_convert_fusion.2) | copy-start | bytes 3538948
  78.9 23.0 %copy-start.63 = (f32[128]{0:T(128)S(1)}, f32[128]{0:T(128)}, u32[]{:S(2)}) copy-start(f32[128]{0:T(128)} %param.25) | copy-start | bytes 1540
  78.9 23.0 %copy-start.64 = (bf16[512,128]{1,0:T(8,128)(2,1)S(1)}, bf16[512,128]{1,0:T(8,128)(2,1)}, u32[]{:S(2)}) copy-start(bf16[512,128]{1,0:T(8,128)(2,1)} %param.23) | copy-start | bytes 393220
  78.9 22.9 %copy-start.68 = (f32[128]{0:T(128)S(1)}, f32[128]{0:T(128)}, u32[]{:S(2)}) copy-start(f32[128]{0:T(128)} %param.24) | copy-start | bytes 1540
  108.2 7.7 %copy-start.1 = (f32[72,64,128]{2,1,0:T(8,128)S(1)}, f32[72,64,128]{2,1,0:T(8,128)}, u32[]{:S(2)}) copy-start(f32[72,64,128]{2,1,0:T(8,128)} %gather_fusion.1) | copy-start | bytes 7077892
  123.3 7.2 %copy-start.58 = (s32[72]{0:T(128)S(1)}, s32[72]{0:T(128)}, u32[]{:S(2)}) copy-start(s32[72]{0:T(128)} %copy-done.57) | copy-start | bytes 868
  146.1 23.3 %collective-permute-start.4 = (bf16[3,64,128]{2,1,0:T(8,128)(2,1)S(1)}, bf16[3,64,128]{2,1,0:T(8,128)(2,1)S(1)}, u32[]{:S(2)}, u32[]{:S(2)}) collective-permute-start(bf16[3,64,128]{2,1,0:T(8,128)(2,1)S(1)} %get-tuple-element.108), channel_id=1, source_target_pairs={{0,16},{16,32},{32,48},{48,64},{64,80},{80,96},{96,112},{112,0},{1... | collective-permute-start | bytes 147464 | tf_op jit(solution)/shard_map/ppermute | solution.py:18
  146.2 23.3 %collective-permute-start.5 = (bf16[3,64,128]{2,1,0:T(8,128)(2,1)S(1)}, bf16[3,64,128]{2,1,0:T(8,128)(2,1)S(1)}, u32[]{:S(2)}, u32[]{:S(2)}) collective-permute-start(bf16[3,64,128]{2,1,0:T(8,128)(2,1)S(1)} %get-tuple-element.109), channel_id=1, source_target_pairs={{16,0},{32,16},{48,32},{64,48},{80,64},{96,80},{112,96},{0,112},{1... | collective-permute-start | bytes 147464 | tf_op jit(solution)/shard_map/ppermute | solution.py:20
  150.4 149.5 %reduce-scatter.5.cloned.1.call-start = ((), (), s32[]{:S(2)}) async-start(), calls=%async_computation.2 | async-start | bytes 278528 | tf_op jit(solution)/shard_map/reduce_scatter | solution.py:211
  170.6 7.8 %collective-permute-start.6 = (bf16[102,3,128]{2,1,0:T(4,128)(2,1)S(1)}, bf16[102,3,128]{2,1,0:T(4,128)(2,1)S(1)}, u32[]{:S(2)}, u32[]{:S(2)}) collective-permute-start(bf16[102,3,128]{2,1,0:T(4,128)(2,1)S(1)} %get-tuple-element.104), channel_id=1, source_target_pairs={{0,1},{1,2},{2,3},{3,4},{4,5},{5,6},{6,7},{7,8},{8,9},{9,10},{10,1... | collective-permute-start | bytes 235016 | tf_op jit(solution)/shard_map/ppermute | solution.py:18
  170.7 7.7 %collective-permute-start.7 = (bf16[102,3,128]{2,1,0:T(4,128)(2,1)S(1)}, bf16[102,3,128]{2,1,0:T(4,128)(2,1)S(1)}, u32[]{:S(2)}, u32[]{:S(2)}) collective-permute-start(bf16[102,3,128]{2,1,0:T(4,128)(2,1)S(1)} %get-tuple-element.105), channel_id=1, source_target_pairs={{1,0},{2,1},{3,2},{4,3},{5,4},{6,5},{7,6},{8,7},{9,8},{10,9},{11,1... | collective-permute-start | bytes 235016 | tf_op jit(solution)/shard_map/ppermute | solution.py:20
  198.7 6.6 %copy-start.6 = (bf16[96,64,128]{2,1,0:T(8,128)(2,1)S(1)}, bf16[96,64,128]{2,1,0:T(8,128)(2,1)}, u32[]{:S(2)}) copy-start(bf16[96,64,128]{2,1,0:T(8,128)(2,1)} %param.16) | copy-start | bytes 4718596
  198.8 6.6 %copy-start.13 = (f32[128]{0:T(128)S(1)}, f32[128]{0:T(128)}, u32[]{:S(2)}) copy-start(f32[128]{0:T(128)} %get-tuple-element.118) | copy-start | bytes 1540
  198.8 6.6 %copy-start.15 = (f32[128]{0:T(128)S(1)}, f32[128]{0:T(128)}, u32[]{:S(2)}) copy-start(f32[128]{0:T(128)} %get-tuple-element.119) | copy-start | bytes 1540
  198.8 6.6 %copy-start.17 = (f32[128]{0:T(128)S(1)}, f32[128]{0:T(128)}, u32[]{:S(2)}) copy-start(f32[128]{0:T(128)} %get-tuple-element.120) | copy-start | bytes 1540
  198.8 6.6 %copy-start.19 = (f32[128]{0:T(128)S(1)}, f32[128]{0:T(128)}, u32[]{:S(2)}) copy-start(f32[128]{0:T(128)} %get-tuple-element.121) | copy-start | bytes 1540
  198.8 6.6 %copy-start.21 = (f32[128]{0:T(128)S(1)}, f32[128]{0:T(128)}, u32[]{:S(2)}) copy-start(f32[128]{0:T(128)} %get-tuple-element.122) | copy-start | bytes 1540
  198.8 6.6 %copy-start.23 = (f32[128]{0:T(128)S(1)}, f32[128]{0:T(128)}, u32[]{:S(2)}) copy-start(f32[128]{0:T(128)} %get-tuple-element.123) | copy-start | bytes 1540
  198.8 6.6 %copy-start.24 = (f32[128]{0:T(128)S(1)}, f32[128]{0:T(128)}, u32[]{:S(2)}) copy-start(f32[128]{0:T(128)} %get-tuple-element.124) | copy-start | bytes 1540
  198.8 6.6 %copy-start.25 = (f32[128]{0:T(128)S(1)}, f32[128]{0:T(128)}, u32[]{:S(2)}) copy-start(f32[128]{0:T(128)} %get-tuple-element.125) | copy-start | bytes 1540
  198.8 6.6 %copy-start.26 = (f32[128]{0:T(128)S(1)}, f32[128]{0:T(128)}, u32[]{:S(2)}) copy-start(f32[128]{0:T(128)} %get-tuple-element.126) | copy-start | bytes 1540
  198.8 6.6 %copy-start.27 = (f32[128]{0:T(128)S(1)}, f32[128]{0:T(128)}, u32[]{:S(2)}) copy-start(f32[128]{0:T(128)} %get-tuple-element.127) | copy-start | bytes 1540
  198.9 6.6 %copy-start.28 = (f32[128]{0:T(128)S(1)}, f32[128]{0:T(128)}, u32[]{:S(2)}) copy-start(f32[128]{0:T(128)} %get-tuple-element.128) | copy-start | bytes 1540
  198.9 6.6 %copy-start.29 = (f32[128]{0:T(128)S(1)}, f32[128]{0:T(128)}, u32[]{:S(2)}) copy-start(f32[128]{0:T(128)} %get-tuple-element.129) | copy-start | bytes 1540
  198.9 6.6 %copy-start.30 = (f32[128]{0:T(128)S(1)}, f32[128]{0:T(128)}, u32[]{:S(2)}) copy-start(f32[128]{0:T(128)} %get-tuple-element.130) | copy-start | bytes 1540
  198.9 6.6 %copy-start.31 = (f32[128]{0:T(128)S(1)}, f32[128]{0:T(128)}, u32[]{:S(2)}) copy-start(f32[128]{0:T(128)} %get-tuple-element.131) | copy-start | bytes 1540
  198.9 6.6 %copy-start.32 = (f32[128]{0:T(128)S(1)}, f32[128]{0:T(128)}, u32[]{:S(2)}) copy-start(f32[128]{0:T(128)} %get-tuple-element.132) | copy-start | bytes 1540
  198.9 6.6 %copy-start.33 = (f32[128]{0:T(128)S(1)}, f32[128]{0:T(128)}, u32[]{:S(2)}) copy-start(f32[128]{0:T(128)} %get-tuple-element.133) | copy-start | bytes 1540
  198.9 6.6 %copy-start.34 = (f32[128]{0:T(128)S(1)}, f32[128]{0:T(128)}, u32[]{:S(2)}) copy-start(f32[128]{0:T(128)} %get-tuple-element.134) | copy-start | bytes 1540
  (32 other events, 179.6 us)
Sparse Core Ops, SparseCore 0:
  150.5 64.2 reduce-scatter.6
  218.4 64.1 reduce-scatter.4
where the time goes:
time: 341 us; the launch traced here: 340 us
  other arithmetic  124 us (36%)
  blocking collectives  103 us (30%)
  matrix products  43.3 us (13%)
  local copies, waits for them, and re-layouts  29.5 us (9%)
  starting transfers between devices  19.6 us (6%)
  between operations  16.5 us (5%)
  waiting for transfers between devices  4.66 us (1%)
    unnamed x1, blocking collectives  70.2 us
    psum x1, blocking collectives, per_device(): lax.psum((part_win, part_wout, part_taps, part_chan, part_bin), 'lon')  32.5 us
    reduce_sum x5, other arithmetic, backward_taps(): jnp.sum(padded[a:a + lon_cells, b:b + lat_cells].astype(jnp.float32) * d_...  24.1 us
    convert_element_type x1, other arithmetic, per_device(): (upstream.astype(jnp.float32) + land_float[:, :, None] * masked_grad).ast...  23.6 us
    add x1, other arithmetic, per_device(): conv_out = conv_taps(padded, dw_weight, lon_cells, lat_cells) + dw_bias  23.5 us
    dot_general x1, matrix products, cell_rows(): hidden = jnp.dot(normed_b, w_in, preferred_element_type=jnp.float32) + b_in  22.9 us
    ppermute x4, starting transfers between devices, with_halo(): lax.ppermute(head, axis, [((i + 1) % count, i) for i in range(count)])  17.6 us
    scatter-add x1, other arithmetic, listed_rows(): branch_tiles = jnp.zeros((tile_count, 64, channels), jnp.float32).at[slot...  12.8 us
  transfers between devices with their start and end apart: 10, of which 2 were waited for; matrix products, arithmetic and copies ran while one was open for 24% of the time, Pallas kernels for 0%

commit v1 on v0

v1 whole, which is shorter than its diff:
```python
import functools
import math

import jax
import jax.numpy as jnp
from jax import lax
from jax.experimental import pallas as pl
from jax.experimental.pallas import tpu as pltpu
from jax.sharding import PartitionSpec as P

LN_EPSILON = 1e-06
MESH = pl.DeviceIdType.MESH
F32 = jnp.float32
BF16 = jnp.bfloat16
CLON, CLAT, C, FF = 96, 64, 128, 512
NI, NJ = CLON // 8, CLAT // 8
TILES = NI * NJ
TCAP = 72
NG = 8
ZR = 80
N_LON, N_LAT = 8, 16
SHIFTS = (-4, -2, 0, 2)
GRAD_SCALE = 1.0 / math.sqrt(768 * 1024)
VMEM_LIMIT = 56 * 1024 * 1024
ERF_COEFS = (0.7978822019328625, 0.03634471964933557, -4.4922105999092954e-05,
             -5.0349129465290195e-05, 3.0967343000773035e-06, -6.63025075261232e-08)


def iota(shape, dim):
    return lax.broadcasted_iota(jnp.int32, shape, dim)


def block_transpose(rows):
    block = iota(rows[0].shape, 1) // 16
    turned = [r if n == 0 else pltpu.roll(r, 16 * n, axis=1) for n, r in enumerate(rows)]
    u = [turned[(-n) % 8] for n in range(8)]
    for s in (1, 2, 4):
        bit = (block & s) != 0
        u = [jnp.where(bit, u[(m - s) % 8], u[m]) for m in range(8)]
    return [r if m == 0 else pltpu.roll(r, 128 - 16 * m, axis=1) for m, r in enumerate(u)]


def build_weights(w_ref, W, flip):
    q_row, q_col = iota((56, 49), 0), iota((56, 49), 1)
    a, b = q_row // 8, q_row % 8
    tap = (6 - a) * 7 + (6 - b) if flip else a * 7 + b
    pick = jnp.where((q_col == tap) & (b < 7), 1.0, 0.0).astype(BF16)
    taps = jnp.dot(pick, w_ref[...].astype(BF16), preferred_element_type=F32).astype(BF16)
    lane_i = iota((8, 128), 1) // 16
    same = (iota((16, 128), 0) == iota((16, 128), 1) % 16).astype(F32)

    def group(g, carry):
        spread = jnp.where(iota((128, 128), 0) == 16 * g + iota((128, 128), 1) % 16, 1.0, 0.0).astype(BF16)
        rep = jnp.dot(taps, spread, preferred_element_type=F32)
        for i_in in range(16):
            v = jnp.zeros((8, 128), F32)
            for a in range(7):
                if 0 <= i_in - 1 - a < 8:
                    v = jnp.where(lane_i == i_in - 1 - a, rep[8 * a : 8 * a + 8], v)
            base = (i_in // 8) * 512 + (i_in % 8) * 16
            W[g, base : base + 16, 0:128] = jnp.zeros((16, 128), BF16)
            for b in range(7):
                parity = (b + 1) % 2
                e = (b - 3 - parity + 4) // 2
                row = jnp.broadcast_to(v[b : b + 1], (16, 128)) * same
                W[g, base + 128 * e : base + 128 * e + 16, 128 * parity : 128 * parity + 128] = row.astype(BF16)
        return carry

    lax.fori_loop(0, NG, group, 0)


def pack_edges(X, EL, ER, first):
    low = iota((8, 128), 0) < 4

    def block(n, carry):
        left = X[first + n * NJ].astype(F32)
        right = X[first + n * NJ + NJ - 1].astype(F32)
        el, er = [], []
        for m in range(4):
            even, odd = left[16 * m : 16 * m + 8], left[16 * m + 8 : 16 * m + 16]
            el.append(jnp.where(low, even, pltpu.roll(odd, 4, axis=0)))
            even, odd = right[16 * m : 16 * m + 8], right[16 * m + 8 : 16 * m + 16]
            er.append(jnp.where(low, pltpu.roll(even, 4, axis=0), odd))
        EL[n] = jnp.concatenate(el, axis=0).astype(BF16)
        ER[n] = jnp.concatenate(er, axis=0).astype(BF16)
        return carry

    lax.fori_loop(0, NI, block, 0)


def halo_copies(X, EL, ER, LH, RH, send, recv, lon, lat):
    up, down = lax.rem(lon + 1, N_LON), lax.rem(lon + N_LON - 1, N_LON)
    east, west = lax.rem(lat + 1, N_LAT), lax.rem(lat + N_LAT - 1, N_LAT)
    plan = (
        (EL, RH.at[pl.ds(1, NI)], (lon, west)),
        (ER, LH.at[pl.ds(1, NI)], (lon, east)),
        (X.at[pl.ds(NJ, NJ), pl.ds(0, 32)], X.at[pl.ds(13 * NJ, NJ), pl.ds(0, 32)], (down, lat)),
        (X.at[pl.ds(12 * NJ, NJ), pl.ds(32, 32)], X.at[pl.ds(0, NJ), pl.ds(32, 32)], (up, lat)),
        (EL.at[0, pl.ds(0, 16)], RH.at[13, pl.ds(0, 16)], (down, west)),
        (EL.at[NI - 1, pl.ds(16, 16)], RH.at[0, pl.ds(16, 16)], (up, west)),
        (ER.at[0, pl.ds(0, 16)], LH.at[13, pl.ds(0, 16)], (down, east)),
        (ER.at[NI - 1, pl.ds(16, 16)], LH.at[0, pl.ds(16, 16)], (up, east)),
    )
    return [
        pltpu.make_async_remote_copy(
            src_ref=src, dst_ref=dst, send_sem=send.at[n], recv_sem=recv.at[n], device_id=where, device_id_type=MESH
        )
        for n, (src, dst, where) in enumerate(plan)
    ]


def neighbours(lon, lat):
    up, down = lax.rem(lon + 1, N_LON), lax.rem(lon + N_LON - 1, N_LON)
    east, west = lax.rem(lat + 1, N_LAT), lax.rem(lat + N_LAT - 1, N_LAT)
    return [(lon, west), (lon, east), (down, lat), (up, lat), (down, west), (up, west), (down, east), (up, east)]


def greet(places):
    barrier = pltpu.get_barrier_semaphore()
    for place in places:
        pl.semaphore_signal(barrier, inc=1, device_id=place, device_id_type=MESH)
    pl.semaphore_wait(barrier, len(places))


def spread_blocks(X, LH, RH, PS, Z, keep_left, keep_right):
    PS[:, 0:8] = jnp.zeros((NG, 8, 128), F32)
    PS[:, 88:104] = jnp.zeros((NG, 16, 128), F32)

    def block(k, carry):
        def put(rows, at):
            for g, r in enumerate(block_transpose(rows)):
                PS[g, at : at + rows[0].shape[0]] = r

        for t in range(NJ):
            lower = X[k * NJ + t, 32:64].astype(F32)
            upper = X[(k + 1) * NJ + t, 0:32].astype(F32)
            rows = [lower[8 * i : 8 * i + 8] for i in range(4)] + [upper[8 * i : 8 * i + 8] for i in range(4)]
            put(rows, 16 + 8 * t)
        for H, keep, at, flip in ((LH, keep_left, 8, 0), (RH, keep_right, 80, 1)):
            pairs = []
            for edge in (H[k, 16:32].astype(F32) * keep, H[k + 1, 0:16].astype(F32) * keep):
                pairs += [edge[0:8], edge[8:16]]
            rows = []
            for pair in pairs:
                other = pltpu.roll(pair, 4, axis=0)
                rows += [pair, other] if flip else [other, pair]
            put(rows, at)
        for g in range(NG):
            for e, shift in enumerate(SHIFTS):
                Z[g, k, :, 128 * e : 128 * e + 128] = PS[g, 16 + shift : 16 + shift + ZR].astype(BF16)
        return carry

    lax.fori_loop(0, NI + 1, block, 0)


def banded_conv(Z, W, AB, S):
    def group(g, carry):
        lhs = jnp.concatenate([Z[g, 0:NI].reshape(NI * ZR, 512), Z[g, 1 : NI + 1].reshape(NI * ZR, 512)], axis=1)
        both = jnp.dot(lhs, W[g], preferred_element_type=F32)
        AB[...] = both[:, 128:256]
        for n in range(NI):
            S[g, n] = both[n * ZR : n * ZR + 64, 0:128] + AB[n * ZR + 1 : n * ZR + 65]
        return carry

    lax.fori_loop(0, NG, group, 0)


def conv_kernel(fields, land, w, bias, conv_out, masked_out, X, EL, ER, LH, RH, PS, Z, W, AB, S, land_pad, send, recv):
    lon, lat = lax.axis_index("lon"), lax.axis_index("lat")
    land_pad[...] = jnp.zeros((128, 128), F32)
    land_pad[0:CLON, 0:CLAT] = land[...].astype(F32)
    land_t = land_pad[...].T[0:CLAT]

    def mask_block(n, carry):
        turned = pltpu.roll(land_t, lax.rem(128 - 8 * n, 128), axis=1)
        for m in range(4):
            pair = []
            for i in (2 * m, 2 * m + 1):
                keep = jnp.broadcast_to(turned[:, i : i + 1], (CLAT, C))
                pair.append(fields[8 * n + i].astype(F32) * keep)
            for t in range(NJ):
                both = jnp.concatenate([pair[0][8 * t : 8 * t + 8], pair[1][8 * t : 8 * t + 8]], axis=0)
                X[(n + 1) * NJ + t, 16 * m : 16 * m + 16] = both.astype(BF16)
        return carry

    lax.fori_loop(0, NI, mask_block, 0)
    pack_edges(X, EL, ER, NJ)
    greet(neighbours(lon, lat))
    copies = halo_copies(X, EL, ER, LH, RH, send, recv, lon, lat)
    for copy in copies:
        copy.start()
    build_weights(w, W, False)
    masked_out[...] = X[NJ : NJ + TILES]
    for copy in copies:
        copy.wait()
    keep_left = jnp.where(lat > 0, 1.0, 0.0)
    keep_right = jnp.where(lat < N_LAT - 1, 1.0, 0.0)
    spread_blocks(X, LH, RH, PS, Z, keep_left, keep_right)
    banded_conv(Z, W, AB, S)
    offset = jnp.broadcast_to(bias[...], (8, C))

    def back(n, carry):
        for t in range(NJ):
            rows = block_transpose([S[g, n, 8 * t : 8 * t + 8] for g in range(NG)])
            for i in range(8):
                conv_out[n * NJ + t, 8 * i : 8 * i + 8] = rows[i] + offset
        return carry

    lax.fori_loop(0, NI, back, 0)


def vmem(n):
    return [pl.BlockSpec(memory_space=pltpu.VMEM)] * n


def halo_scratch():
    return [
        pltpu.VMEM((14 * NJ, 64, C), BF16),
        pltpu.VMEM((NI, 32, C), BF16),
        pltpu.VMEM((NI, 32, C), BF16),
        pltpu.VMEM((14, 32, C), BF16),
        pltpu.VMEM((14, 32, C), BF16),
        pltpu.VMEM((NG, 104, 128), F32),
        pltpu.VMEM((NG, NI + 1, ZR, 512), BF16),
        pltpu.VMEM((NG, 1024, 256), BF16),
        pltpu.VMEM((NI * ZR, 128), F32),
        pltpu.VMEM((NG, NI, 64, 128), F32),
    ]


def forward_conv(fields, land, w, bias):
    return pl.pallas_call(
        conv_kernel,
        name="forward_conv",
        out_shape=(jax.ShapeDtypeStruct((TILES, 64, C), F32), jax.ShapeDtypeStruct((TILES, 64, C), BF16)),
        in_specs=vmem(4),
        out_specs=tuple(vmem(2)),
        scratch_shapes=halo_scratch()
        + [pltpu.VMEM((128, 128), F32), pltpu.SemaphoreType.DMA((8,)), pltpu.SemaphoreType.DMA((8,))],
        compiler_params=pltpu.CompilerParams(collective_id=0, has_side_effects=True, vmem_limit_bytes=VMEM_LIMIT),
    )(fields, land, w, bias)


def transposed_land(land, land_pad):
    land_pad[...] = jnp.zeros((128, 128), F32)
    land_pad[0:CLON, 0:CLAT] = land[...].astype(F32)
    return land_pad[...].T[0:CLAT]


def normal_cdf(h, square):
    q = jnp.full(h.shape, ERF_COEFS[-1], F32)
    for coef in ERF_COEFS[-2::-1]:
        q = q * square + coef
    return 0.5 + 0.5 * jnp.tanh(h * q)


def mlp_kernel(tile_ids, conv, fields, upstream, land, gain, shift, w_in, b_in, w_out, b_out, scale,
               mixed, d_conv_out, shares, branch, w_in_t, w_out_t, g_in, g_out, g_bin, sums, land_pad, land_tr):
    slots = 4
    rows = slots * 64
    land_tr[...] = transposed_land(land, land_pad)
    w_in_t[...] = w_in[...].astype(F32).T.astype(BF16)
    w_out_t[...] = w_out[...].astype(F32).T.astype(BF16)
    branch[...] = jnp.zeros(branch.shape, F32)
    d_conv_out[...] = jnp.zeros(d_conv_out.shape, BF16)
    for acc in (g_in, g_out, g_bin, sums):
        acc[...] = jnp.zeros(acc.shape, F32)
    gain_row, shift_row, scale_row = gain[...], shift[...], scale[...]

    def step(n, carry):
        ids = [tile_ids[slots * n + q] for q in range(slots)]
        tiles = [jnp.maximum(t, 0) for t in ids]
        conv_parts, up_parts, active_parts = [], [], []
        for q in range(slots):
            t = tiles[q]
            big, small = t // NJ, lax.rem(t, NJ)
            conv_parts.append(conv[t])
            pair = upstream[pl.ds(8 * big, 8), pl.ds(16 * (small // 2), 16), :].astype(F32)
            odd = lax.rem(small, 2) == 1
            up_parts.append(jnp.where(odd, pair[:, 8:16], pair[:, 0:8]).reshape(64, C))
            strip = pltpu.roll(land_tr[pl.ds(8 * small, 8), :], lax.rem(128 - 8 * big, 128), axis=1)
            live = jnp.where(ids[q] >= 0, 1.0, 0.0)
            strip = strip * live
            active_parts += [jnp.broadcast_to(strip[:, i : i + 1], (8, C)) for i in range(8)]
        conv_rows = jnp.concatenate(conv_parts, axis=0)
        up = jnp.concatenate(up_parts, axis=0)
        active = jnp.concatenate(active_parts, axis=0)
        center = conv_rows - jnp.mean(conv_rows, axis=-1, keepdims=True)
        inv_std = lax.rsqrt(jnp.mean(center * center, axis=-1, keepdims=True) + LN_EPSILON)
        normed = center * inv_std
        normed_b = (normed * gain_row + shift_row).astype(BF16)
        hidden = jnp.dot(normed_b, w_in[...], preferred_element_type=F32) + b_in[...]
        bounded = jnp.clip(hidden, -5.0, 5.0)
        square = bounded * bounded
        cdf = normal_cdf(bounded, square)
        activated = (hidden * cdf).astype(BF16)
        output = jnp.dot(activated, w_out[...], preferred_element_type=F32) + b_out[...]
        gate = active * scale_row
        branch_rows = gate * output
        d_out = gate * up
        d_out_b = d_out.astype(BF16)
        g_out[...] += lax.dot_general(d_out_b, activated, (((0,), (0,)), ((), ())), preferred_element_type=F32)
        pdf = jnp.exp(-0.5 * (hidden * hidden)) * (1.0 / math.sqrt(2.0 * math.pi))
        d_hidden = jnp.dot(d_out_b, w_out_t[...], preferred_element_type=F32) * (cdf + hidden * pdf)
        d_hidden_b = d_hidden.astype(BF16)
        g_in[...] += lax.dot_general(normed_b, d_hidden_b, (((0,), (0,)), ((), ())), preferred_element_type=F32)
        g_bin[...] += jnp.sum(d_hidden.reshape(rows // 8, 8, FF), axis=0)
        d_norm = jnp.dot(d_hidden_b, w_in_t[...], preferred_element_type=F32)
        d_scaled = d_norm * gain_row
        d_conv = inv_std * (
            d_scaled
            - jnp.mean(d_scaled, axis=-1, keepdims=True)
            - normed * jnp.mean(d_scaled * normed, axis=-1, keepdims=True)
        )
        for k, term in enumerate((d_conv, d_norm * normed, d_norm, d_out, active * output * up)):
            sums[k] += jnp.sum(term.reshape(rows // 8, 8, C), axis=0)
        d_conv_b = d_conv.astype(BF16)
        for q in range(slots):

            @pl.when(ids[q] >= 0)
            def _(q=q):
                branch[tiles[q]] = branch_rows[64 * q : 64 * q + 64]
                d_conv_out[tiles[q]] = d_conv_b[64 * q : 64 * q + 64]

        return carry

    lax.fori_loop(0, TCAP // slots, step, 0)

    def mix(n, carry):
        for i in range(8):
            rows_i = jnp.concatenate([branch[n * NJ + t, 8 * i : 8 * i + 8] for t in range(NJ)], axis=0)
            mixed[8 * n + i] = (fields[8 * n + i].astype(F32) + rows_i).astype(BF16)
        return carry

    lax.fori_loop(0, NI, mix, 0)
    bin_row = jnp.sum(g_bin[...], axis=0, keepdims=True)
    tail = jnp.concatenate([jnp.sum(sums[k], axis=0, keepdims=True) for k in range(5)], axis=0)
    for n in range(4):
        turned_in = g_in[:, 128 * n : 128 * n + 128].T
        turned_out = g_out[:, 128 * n : 128 * n + 128].T
        for m in range(4):
            q = 4 * n + m
            shares[q, 0:32] = turned_in[32 * m : 32 * m + 32]
            shares[q, 32:64] = turned_out[32 * m : 32 * m + 32]
            shares[q, 64:65] = bin_row[:, 128 * n : 128 * n + 128]
            shares[q, 65:70] = tail
            shares[q, 70:72] = jnp.zeros((2, 128), F32)


def listed_mlp(tile_ids, conv, fields, upstream, land, gain, shift, w_in, b_in, w_out, b_out, scale):
    return pl.pallas_call(
        mlp_kernel,
        name="listed_mlp",
        out_shape=(
            jax.ShapeDtypeStruct((CLON, CLAT, C), BF16),
            jax.ShapeDtypeStruct((TILES, 64, C), BF16),
            jax.ShapeDtypeStruct((N_LAT, 72, 128), F32),
        ),
        in_specs=[pl.BlockSpec(memory_space=pltpu.SMEM)] + vmem(11),
        out_specs=tuple(vmem(3)),
        scratch_shapes=[
            pltpu.VMEM((TILES, 64, C), F32),
            pltpu.VMEM((FF, C), BF16),
            pltpu.VMEM((C, FF), BF16),
            pltpu.VMEM((C, FF), F32),
            pltpu.VMEM((C, FF), F32),
            pltpu.VMEM((8, FF), F32),
            pltpu.VMEM((5, 8, C), F32),
            pltpu.VMEM((128, 128), F32),
            pltpu.VMEM((CLAT, 128), F32),
        ],
        compiler_params=pltpu.CompilerParams(vmem_limit_bytes=VMEM_LIMIT),
    )(tile_ids, conv, fields, upstream, land, gain, shift, w_in, b_in, w_out, b_out, scale)


def spread_masked(masked, PS, MP):
    PS[:, 0:8] = jnp.zeros((NG, 8, 128), F32)
    PS[:, 72:104] = jnp.zeros((NG, 32, 128), F32)

    def block(n, carry):
        for t in range(NJ):
            tile = masked[n * NJ + t].astype(F32)
            rows = block_transpose([tile[8 * i : 8 * i + 8] for i in range(8)])
            for g in range(NG):
                PS[g, 8 + 8 * t : 16 + 8 * t] = rows[g]
        for g in range(NG):
            MP[g, n, :, 0:128] = PS[g, 8 : 8 + ZR].astype(BF16)
            MP[g, n, :, 128:256] = PS[g, 7 : 7 + ZR].astype(BF16)
        return carry

    lax.fori_loop(0, NI, block, 0)


def tap_gradients(Z, MP, G, taps):
    lane = iota((16, 128), 1)
    same = (iota((16, 128), 0) == lane % 16).astype(F32)
    block = lane // 16
    taps[...] = jnp.zeros(taps.shape, F32)

    def group(g, carry):
        lhs = MP[g].reshape(NI * ZR, 256)
        for half in range(2):
            rhs = Z[g, half : half + NI].reshape(NI * ZR, 512)
            G[half] = lax.dot_general(lhs, rhs, (((0,), (0,)), ((), ())), preferred_element_type=F32)
        for e in range(4):
            for parity in range(2):
                b = 3 - SHIFTS[e] - parity
                if not 0 <= b < 7:
                    continue
                for a in range(7):
                    total = None
                    for i_out in range(8):
                        half, k = divmod(i_out + 7 - a, 8)
                        at = 128 * parity + 16 * i_out
                        piece = G[half, at : at + 16, 128 * e : 128 * e + 128]
                        total = piece if total is None else jnp.where(block == k, piece, total)
                    taps[g, 7 * a + b : 7 * a + b + 1] = jnp.sum(total * same, axis=0, keepdims=True)
        return carry

    lax.fori_loop(0, NG, group, 0)


def gather_taps(taps, square, tap_shares):
    total = jnp.zeros((56, 128), F32)
    for g in range(NG):
        row, col = iota((128, 128), 0), iota((128, 128), 1)
        pick = jnp.where((col // 16 == g) & (row % 16 == col % 16), 1.0, 0.0).astype(BF16)
        value = taps[g]
        head = value.astype(BF16)
        tail = (value - head.astype(F32)).astype(BF16)
        total += jnp.dot(head, pick, preferred_element_type=F32) + jnp.dot(tail, pick, preferred_element_type=F32)
    square[...] = jnp.zeros((128, 128), F32)
    square[0:56] = total
    turned = square[...].T
    for q in range(N_LAT):
        tap_shares[q] = turned[8 * q : 8 * q + 8]


def grad_kernel(d_conv, masked, upstream, land, w, shares,
                grad_input, out_win, out_wout, out_dw, out_channel, out_bin,
                X, EL, ER, LH, RH, PS, Z, W, AB, S, MP, G, taps, square, tap_shares, parts, tap_parts, mine, whole,
                send, recv, send_one, recv_one, send_tap, recv_tap, send_two, recv_two):
    lon, lat = lax.axis_index("lon"), lax.axis_index("lat")
    X[NJ : NJ + TILES] = d_conv[...]
    pack_edges(X, EL, ER, NJ)
    around = neighbours(lon, lat)
    others = [(lon, lax.rem(lat + d, N_LAT)) for d in range(2, N_LAT - 1)]
    others += [(lax.rem(lon + d, N_LON), lat) for d in range(2, N_LON - 1)]
    greet(around + others)
    copies = halo_copies(X, EL, ER, LH, RH, send, recv, lon, lat)
    for copy in copies:
        copy.start()
    share_copies, tap_copies = [], []
    for d in range(1, N_LAT):
        to = lax.rem(lat + d, N_LAT)
        share_copies.append(pltpu.make_async_remote_copy(
            src_ref=shares.at[to], dst_ref=parts.at[d], send_sem=send_one.at[d], recv_sem=recv_one.at[d],
            device_id=(lon, to), device_id_type=MESH))
        tap_copies.append(pltpu.make_async_remote_copy(
            src_ref=tap_shares.at[to], dst_ref=tap_parts.at[d], send_sem=send_tap.at[d], recv_sem=recv_tap.at[d],
            device_id=(lon, to), device_id_type=MESH))
    for copy in share_copies:
        copy.start()
    build_weights(w, W, True)
    spread_masked(masked, PS, MP)
    for copy in copies:
        copy.wait()
    keep_left = jnp.where(lat > 0, 1.0, 0.0)
    keep_right = jnp.where(lat < N_LAT - 1, 1.0, 0.0)
    spread_blocks(X, LH, RH, PS, Z, keep_left, keep_right)
    tap_gradients(Z, MP, G, taps)
    gather_taps(taps, square, tap_shares)
    for copy in tap_copies:
        copy.start()
    banded_conv(Z, W, AB, S)
    for copy in share_copies:
        copy.wait()
    for copy in tap_copies:
        copy.wait()
    total = shares[lat]
    tap_total = tap_shares[lat]
    for d in range(1, N_LAT):
        total += parts[d]
        tap_total += tap_parts[d]
    mine[0:72] = total * GRAD_SCALE
    mine[72:80] = tap_total * GRAD_SCALE
    last_copies = [
        pltpu.make_async_remote_copy(
            src_ref=mine, dst_ref=whole.at[d], send_sem=send_two.at[d], recv_sem=recv_two.at[d],
            device_id=(lax.rem(lon + d, N_LON), lat), device_id_type=MESH)
        for d in range(1, N_LON)
    ]
    for copy in last_copies:
        copy.start()
    square[...] = jnp.zeros((128, 128), F32)
    square[0:CLON, 0:CLAT] = land[...].astype(F32)
    land_t = square[...].T[0:CLAT]

    def back(n, carry):
        turned = pltpu.roll(land_t, lax.rem(128 - 8 * n, 128), axis=1)
        for t in range(NJ // 2):
            low = block_transpose([S[g, n, 16 * t : 16 * t + 8] for g in range(NG)])
            high = block_transpose([S[g, n, 16 * t + 8 : 16 * t + 16] for g in range(NG)])
            for i in range(8):
                keep = jnp.broadcast_to(turned[16 * t : 16 * t + 16, i : i + 1], (16, C))
                value = jnp.concatenate([low[i], high[i]], axis=0) * keep
                up = upstream[8 * n + i, 16 * t : 16 * t + 16].astype(F32)
                grad_input[8 * n + i, 16 * t : 16 * t + 16] = (up + value).astype(BF16)
        return carry

    lax.fori_loop(0, NI, back, 0)
    for copy in last_copies:
        copy.wait()
    total = mine[...]
    for d in range(1, N_LON):
        total += whole[d]
    square[...] = jnp.zeros((128, 128), F32)
    square[0:32] = total[0:32]
    out_win[...] = square[...].T[:, 0:32]
    out_wout[...] = total[32:64]
    small = total[64:72]
    out_bin[...] = pltpu.roll(small, lax.rem(128 - 32 * lax.rem(lat, 4), 128), axis=1)[0:1, 0:32]
    out_channel[...] = pltpu.roll(small, lax.rem(128 - 8 * lat, 128), axis=1)[1:6, 0:8]
    square[0:8] = total[72:80]
    out_dw[...] = square[...].T[0:49, 0:8]


def backward_conv(d_conv, masked, upstream, land, w, shares):
    dma = pltpu.SemaphoreType.DMA
    return pl.pallas_call(
        grad_kernel,
        name="backward_conv",
        out_shape=(
            jax.ShapeDtypeStruct((CLON, CLAT, C), BF16),
            jax.ShapeDtypeStruct((C, 32), F32),
            jax.ShapeDtypeStruct((32, C), F32),
            jax.ShapeDtypeStruct((49, 8), F32),
            jax.ShapeDtypeStruct((5, 8), F32),
            jax.ShapeDtypeStruct((1, 32), F32),
        ),
        in_specs=vmem(6),
        out_specs=tuple(vmem(6)),
        scratch_shapes=halo_scratch()
        + [
            pltpu.VMEM((NG, NI, ZR, 256), BF16),
            pltpu.VMEM((2, 256, 512), F32),
            pltpu.VMEM((NG, 56, 128), F32),
            pltpu.VMEM((128, 128), F32),
            pltpu.VMEM((N_LAT, 8, 128), F32),
            pltpu.VMEM((N_LAT, 72, 128), F32),
            pltpu.VMEM((N_LAT, 8, 128), F32),
            pltpu.VMEM((80, 128), F32),
            pltpu.VMEM((N_LON, 80, 128), F32),
            dma((8,)), dma((8,)), dma((N_LAT,)), dma((N_LAT,)), dma((N_LAT,)), dma((N_LAT,)), dma((N_LON,)), dma((N_LON,)),
        ],
        compiler_params=pltpu.CompilerParams(collective_id=1, has_side_effects=True, vmem_limit_bytes=VMEM_LIMIT),
    )(d_conv, masked, upstream, land, w, shares)


def per_device(fields, land_sea, tile_list, upstream, dw_weight, dw_bias, ln_gain, ln_bias, w_in, b_in, w_out, b_out,
               layer_scale):
    def row(v):
        return v.reshape(1, -1)

    conv, masked = forward_conv(fields, land_sea, dw_weight, row(dw_bias))
    mixed, d_conv, shares = listed_mlp(
        tile_list.reshape(-1), conv, fields, upstream, land_sea, row(ln_gain), row(ln_bias), w_in, row(b_in), w_out,
        row(b_out), row(layer_scale))
    grad_input, g_win, g_wout, g_dw, g_channel, g_bin = backward_conv(
        d_conv, masked, upstream, land_sea, dw_weight, shares)
    return mixed, grad_input, g_win, g_wout, g_dw, g_channel, g_bin.reshape(-1)


def solution(mesh):
    cells = P("lon", "lat", None)
    return jax.shard_map(
        per_device,
        mesh=mesh,
        in_specs=(cells, P("lon", "lat"), cells, cells) + (P(),) * 9,
        out_specs=(cells, cells, P(None, "lat"), P("lat", None), P(None, "lat"), P(None, "lat"), P("lat")),
        check_vma=False,
    )
```

time: 341 us -> 121 us (0.35)
  other arithmetic: 124 us -> 0 us
  Pallas kernels: 0 us -> 111 us
  blocking collectives: 103 us -> 0 us
  matrix products: 43.3 us -> 0 us
  local copies, waits for them, and re-layouts: 29.5 us -> 8.8 us
  starting transfers between devices: 19.6 us -> 0 us
  between operations: 16.5 us -> 0.65 us
  waiting for transfers between devices: 4.66 us -> 0 us
    pallas_call x0 -> x3, Pallas kernels: none -> 111 us  [the longest x1 45.1 us: backward_conv(): pl.pallas_call(grad_kernel, name='backward_conv', out_shape=(jax.ShapeDty...]
    unnamed x1 -> x0, blocking collectives: 70.2 us -> none
    dot_general x6 -> x0, matrix products: 43.3 us -> none  [the longest x1 22.9 us: cell_rows(): hidden = jnp.dot(normed_b, w_in, preferred_element_type=jnp.float32) + b_in]
    reduce_sum x9 -> x0, other arithmetic: 36.4 us -> none  [the longest x5 24.1 us: backward_taps(): jnp.sum(padded[a:a + lon_cells, b:b + lat_cells].astype(jnp.float32) * d_...]
    psum x1 -> x0, blocking collectives: 32.5 us -> none  [per_device(): lax.psum((part_win, part_wout, part_taps, part_chan, part_bin), 'lon')]
    convert_element_type x6 -> x0, other arithmetic: 30.1 us -> none  [the longest x1 23.6 us: per_device(): (upstream.astype(jnp.float32) + land_float[:, :, None] * masked_grad).ast...]
    scatter-add x2 -> x0, other arithmetic: 25.4 us -> none  [the longest x1 12.8 us: listed_rows(): branch_tiles = jnp.zeros((tile_count, 64, channels), jnp.float32).at[slot...]
    add x1 -> x0, other arithmetic: 23.5 us -> none  [per_device(): conv_out = conv_taps(padded, dw_weight, lon_cells, lat_cells) + dw_bias]
  transfers between devices with their start and end apart: 10 -> 0, of which waited for: 2 -> 0; matrix products, arithmetic and copies ran while one was open for 24% -> 0% of each run, Pallas kernels for 0% -> 0%
where the time goes in v1:
time: 121 us; the launch traced here: 120 us
  Pallas kernels  111 us (92%)
  local copies, waits for them, and re-layouts  8.8 us (7%)
    pallas_call x1, Pallas kernels, backward_conv(): pl.pallas_call(grad_kernel, name='backward_conv', out_shape=(jax.ShapeDty...  45.1 us
    pallas_call x1, Pallas kernels, forward_conv(): pl.pallas_call(conv_kernel, name='forward_conv', out_shape=(jax.ShapeDtyp...  36.9 us
    pallas_call x1, Pallas kernels, listed_mlp(): pl.pallas_call(mlp_kernel, name='listed_mlp', out_shape=(jax.ShapeDtypeSt...  28.9 us
    unnamed x13, local copies, waits for them, and re-layouts  8.8 us

profile of v1, /device:TPU:0, one launch (start us, length us, event | category | flops | bytes accessed | tf_op | source)
XLA Modules:
  0.0 120.4 jit_solution(18205280813859275211)
XLA Ops:
  0.6 1.5 %copy.20.land = s32[96,64]{1,0:T(8,128)} copy(s32[96,64]{0,1:T(8,128)} %param.14) | data formatting | bytes 49152 | tf_op args[1]
  2.1 36.9 %forward_conv.1 = (f32[96,64,128]{2,1,0:T(8,128)}, bf16[96,64,128]{2,1,0:T(8,128)(2,1)}) custom-call(bf16[96,64,128]{2,1,0:T(8,128)(2,1)} %fields.3, s32[96,64]{1,0:T(8,128)} %copy.20.land, f32[49,128]{1,0:T(8,128)} %w.3, f32[1,128]{1,0:T(1,128)} %bitcast.9), custom_call_target="tpu_custom_call" | custom-call | tf_op jit(solution)/shard_map/forward_conv/pallas_call | solution.py:232
  39.0 28.9 %listed_mlp.1 = (bf16[96,64,128]{2,1,0:T(8,128)(2,1)}, bf16[96,64,128]{2,1,0:T(8,128)(2,1)}, f32[16,72,128]{2,1,0:T(8,128)}) custom-call(s32[72]{0:T(128)} %bitcast.10, f32[96,64,128]{2,1,0:T(8,128)} %get-tuple-element.18.conv, bf16[96,64,128]{2,1,0:T(8,128)(2,1)} %fields.3, bf16[96,64,128]{2,1,0:T(8,128)(2,1)} %upstream.3, s32[96,64]{1,0:T(8,128)} %copy.20.land, ...), custom_call_target="tpu_custom_call" | custom-call | tf_op jit(solution)/shard_map/listed_mlp/pallas_call | solution.py:351
  67.9 45.1 %backward_conv.1 = (bf16[96,64,128]{2,1,0:T(8,128)(2,1)}, f32[128,32]{1,0:T(8,128)}, f32[32,128]{1,0:T(8,128)}, f32[49,8]{1,0:T(8,128)}, f32[5,8]{1,0:T(8,128)}, /*index=5*/f32[1,32]{1,0:T(1,128)}) custom-call(bf16[96,64,128]{2,1,0:T(8,128)(2,1)} %get-tuple-element.20.d_conv, bf16[96,64,128]{2,1,0:T(8,128)(2,1)} %get-tuple-element.21.masked, ...), custom_call_target="tpu_custom_call" | custom-call | tf_op jit(solution)/shard_map/backward_conv/pallas_call | solution.py:530
  113.0 1.4 %copy.24 = f32[49,8]{0,1:T(8,128)} copy(f32[49,8]{1,0:T(8,128)} %get-tuple-element.33) | data formatting | bytes 3136
  114.4 1.5 %copy.23 = f32[128,32]{0,1:T(8,128)} copy(f32[128,32]{1,0:T(8,128)} %get-tuple-element.31) | data formatting | bytes 32768
  116.0 0.0 copy-start
  116.0 0.0 copy-start.1
  116.0 0.0 copy-start.2
  116.0 2.7 %copy.29 = bf16[96,64,128]{2,1,0:T(8,128)(2,1)} copy(bf16[96,64,128]{2,1,0:T(8,128)(2,1)} %get-tuple-element.44) | data formatting | bytes 3145728
  118.7 0.0 copy-done
  118.7 0.6 copy.30
  119.3 0.0 copy-done.1
  119.3 0.6 copy.31
  119.9 0.0 copy-done.2
  119.9 0.5 copy.32
Async XLA Ops:
  116.0 2.7 %copy-start = (f32[32,128]{1,0:T(8,128)S(1)}, f32[32,128]{1,0:T(8,128)}, u32[]{:S(2)}) copy-start(f32[32,128]{1,0:T(8,128)} %get-tuple-element.46) | copy-start | bytes 49156
  116.0 3.3 %copy-start.1 = (f32[5,8]{1,0:T(8,128)S(1)}, f32[5,8]{1,0:T(8,128)}, u32[]{:S(2)}) copy-start(f32[5,8]{1,0:T(8,128)} %get-tuple-element.48) | copy-start | bytes 484
  116.0 3.9 %copy-start.2 = (f32[1,32]{1,0:T(1,128)S(1)}, f32[1,32]{1,0:T(1,128)}, u32[]{:S(2)}) copy-start(f32[1,32]{1,0:T(1,128)} %get-tuple-element.28) | copy-start | bytes 388

commit v2 on v1

--- a/solution.py
+++ b/solution.py
@@ -69,20 +69,51 @@
     lax.fori_loop(0, NG, group, 0)
 
 
-def pack_edges(X, EL, ER, first):
+def build_permutation(PM):
+    def clear(n, carry):
+        PM[pl.ds(pl.multiple_of(64 * n, 64), 64), :] = jnp.zeros((64, 1024), BF16)
+        return carry
+
+    lax.fori_loop(0, 16, clear, 0)
+    row, lane = iota((16, 128), 0), iota((16, 128), 1)
+    for p in range(8):
+        unit = jnp.where(lane == 16 * p + row, 1.0, 0.0).astype(BF16)
+        for q in range(8):
+            PM[128 * p + 16 * q : 128 * p + 16 * q + 16, 128 * q : 128 * q + 128] = unit
+
+
+def expand_mask(land_ext, M, count):
+    value = land_ext.astype(BF16)
+    row, block = iota((128, 128), 0), iota((128, 128), 1) // 16
+
+    def one(k, carry):
+        pick = jnp.where(row == 8 * k + block, 1.0, 0.0).astype(BF16)
+        M[k] = jnp.dot(value, pick, preferred_element_type=F32)
+        return carry
+
+    lax.fori_loop(0, count, one, 0)
+
+
+def pack_edges(X, EL, ER, masks):
     low = iota((8, 128), 0) < 4
 
     def block(n, carry):
-        left = X[first + n * NJ].astype(F32)
-        right = X[first + n * NJ + NJ - 1].astype(F32)
-        el, er = [], []
-        for m in range(4):
-            even, odd = left[16 * m : 16 * m + 8], left[16 * m + 8 : 16 * m + 16]
-            el.append(jnp.where(low, even, pltpu.roll(odd, 4, axis=0)))
-            even, odd = right[16 * m : 16 * m + 8], right[16 * m + 8 : 16 * m + 16]
-            er.append(jnp.where(low, pltpu.roll(even, 4, axis=0), odd))
-        EL[n] = jnp.concatenate(el, axis=0).astype(BF16)
-        ER[n] = jnp.concatenate(er, axis=0).astype(BF16)
+        for east, E in ((0, EL), (1, ER)):
+            out = []
+            keep = None if masks is None else pltpu.roll(masks[east], lax.rem(128 - 8 * n, 128), axis=1)
+            for m in range(4):
+                pair = []
+                for i in (2 * m, 2 * m + 1):
+                    cells = X[1 + 2 * n + i // 4, i % 4, 48 * east : 48 * east + 16].astype(F32)
+                    pair.append(cells[8 * east : 8 * east + 8])
+                if east:
+                    value = jnp.where(low, pltpu.roll(pair[0], 4, axis=0), pair[1])
+                else:
+                    value = jnp.where(low, pair[0], pltpu.roll(pair[1], 4, axis=0))
+                if keep is not None:
+                    value = value * jnp.broadcast_to(keep[:, 2 * m : 2 * m + 1], (8, 128))
+                out.append(value)
+            E[n] = jnp.concatenate(out, axis=0).astype(BF16)
         return carry
 
     lax.fori_loop(0, NI, block, 0)
@@ -94,8 +125,8 @@
     plan = (
         (EL, RH.at[pl.ds(1, NI)], (lon, west)),
         (ER, LH.at[pl.ds(1, NI)], (lon, east)),
-        (X.at[pl.ds(NJ, NJ), pl.ds(0, 32)], X.at[pl.ds(13 * NJ, NJ), pl.ds(0, 32)], (down, lat)),
-        (X.at[pl.ds(12 * NJ, NJ), pl.ds(32, 32)], X.at[pl.ds(0, NJ), pl.ds(32, 32)], (up, lat)),
+        (X.at[1], X.at[25], (down, lat)),
+        (X.at[24], X.at[0], (up, lat)),
         (EL.at[0, pl.ds(0, 16)], RH.at[13, pl.ds(0, 16)], (down, west)),
         (EL.at[NI - 1, pl.ds(16, 16)], RH.at[0, pl.ds(16, 16)], (up, west)),
         (ER.at[0, pl.ds(0, 16)], LH.at[13, pl.ds(0, 16)], (down, east)),
@@ -119,84 +150,139 @@
     barrier = pltpu.get_barrier_semaphore()
     for place in places:
         pl.semaphore_signal(barrier, inc=1, device_id=place, device_id_type=MESH)
-    pl.semaphore_wait(barrier, len(places))
-
-
-def spread_blocks(X, LH, RH, PS, Z, keep_left, keep_right):
-    PS[:, 0:8] = jnp.zeros((NG, 8, 128), F32)
-    PS[:, 88:104] = jnp.zeros((NG, 16, 128), F32)
-
+
+
+def greeted(places):
+    pl.semaphore_wait(pltpu.get_barrier_semaphore(), len(places))
+
+
+def clear_margins(PS):
     def block(k, carry):
-        def put(rows, at):
-            for g, r in enumerate(block_transpose(rows)):
-                PS[g, at : at + rows[0].shape[0]] = r
-
-        for t in range(NJ):
-            lower = X[k * NJ + t, 32:64].astype(F32)
-            upper = X[(k + 1) * NJ + t, 0:32].astype(F32)
-            rows = [lower[8 * i : 8 * i + 8] for i in range(4)] + [upper[8 * i : 8 * i + 8] for i in range(4)]
-            put(rows, 16 + 8 * t)
-        for H, keep, at, flip in ((LH, keep_left, 8, 0), (RH, keep_right, 80, 1)):
-            pairs = []
-            for edge in (H[k, 16:32].astype(F32) * keep, H[k + 1, 0:16].astype(F32) * keep):
-                pairs += [edge[0:8], edge[8:16]]
-            rows = []
-            for pair in pairs:
-                other = pltpu.roll(pair, 4, axis=0)
-                rows += [pair, other] if flip else [other, pair]
-            put(rows, at)
+        PS[:, k, 8:16] = jnp.zeros((NG, 8, 128), F32)
+        PS[:, k, 80:104] = jnp.zeros((NG, 24, 128), F32)
+        return carry
+
+    lax.fori_loop(0, NI + 1, block, 0)
+
+
+def group_blocks(cells, blocks, PM, PS, M):
+    rows = len(blocks) * 64
+    lhs = jnp.concatenate([jnp.concatenate([cells(k, i) for k in blocks], axis=0) for i in range(8)], axis=1)
+
+    def pair(n, carry):
+        both = jnp.dot(lhs, PM[:, pl.ds(pl.multiple_of(256 * n, 256), 256)], preferred_element_type=F32)
+        for h in range(2):
+            for m, k in enumerate(blocks):
+                part = both[64 * m : 64 * m + 64, 128 * h : 128 * h + 128]
+                PS[2 * n + h, k, 16:80] = part if M is None else part * M[k]
+        return carry
+
+    lax.fori_loop(0, NG // 2, pair, 0)
+
+
+def group_halos(LH, RH, EH, PM, PS, lat):
+    low = iota((8, 128), 0) < 4
+    keep = jnp.where(low, jnp.where(lat < N_LAT - 1, 1.0, 0.0), jnp.where(lat > 0, 1.0, 0.0))
+
+    def rows_of(k):
+        rows = []
+        for m in range(4):
+            at = (16, 24, 0, 8)[m]
+            left = LH[k + m // 2, at // 16 * 16 : at // 16 * 16 + 16].astype(F32)[at % 16 : at % 16 + 8]
+            right = RH[k + m // 2, at // 16 * 16 : at // 16 * 16 + 16].astype(F32)[at % 16 : at % 16 + 8]
+            rows.append(jnp.where(low, right, pltpu.roll(left, 4, axis=0)) * keep)
+            rows.append(jnp.where(low, pltpu.roll(right, 4, axis=0), left) * keep)
+        return rows
+
+    for n in range(7):
+        first = rows_of(2 * n)
+        second = rows_of(2 * n + 1) if 2 * n + 1 <= NI else first
+        for i in range(8):
+            EH[n, :, 128 * i : 128 * i + 128] = jnp.concatenate([first[i], second[i]], axis=0).astype(BF16)
+
+    def pair(n, carry):
+        both = jnp.dot(EH[...].reshape(112, 1024), PM[:, pl.ds(pl.multiple_of(256 * n, 256), 256)],
+                       preferred_element_type=F32)
+        for h in range(2):
+            for k in range(NI + 1):
+                part = both[8 * k : 8 * k + 8, 128 * h : 128 * h + 128]
+                PS[2 * n + h, k, 8:16] = part
+                PS[2 * n + h, k, 80:88] = part
+        return carry
+
+    lax.fori_loop(0, NG // 2, pair, 0)
+
+
+def shift_blocks(PS, Z):
+    def block(k, carry):
         for g in range(NG):
             for e, shift in enumerate(SHIFTS):
-                Z[g, k, :, 128 * e : 128 * e + 128] = PS[g, 16 + shift : 16 + shift + ZR].astype(BF16)
+                Z[g, k, :, 128 * e : 128 * e + 128] = PS[g, k, 16 + shift : 16 + shift + ZR].astype(BF16)
         return carry
 
     lax.fori_loop(0, NI + 1, block, 0)
 
 
-def banded_conv(Z, W, AB, S):
+INNER = ((1, 2, 3, 4), (5, 6, 7, 8), (9, 10, 11))
+
+
+def banded_conv(Z, W, AB, S, M):
     def group(g, carry):
         lhs = jnp.concatenate([Z[g, 0:NI].reshape(NI * ZR, 512), Z[g, 1 : NI + 1].reshape(NI * ZR, 512)], axis=1)
         both = jnp.dot(lhs, W[g], preferred_element_type=F32)
         AB[...] = both[:, 128:256]
         for n in range(NI):
-            S[g, n] = both[n * ZR : n * ZR + 64, 0:128] + AB[n * ZR + 1 : n * ZR + 65]
+            value = both[n * ZR : n * ZR + 64, 0:128] + AB[n * ZR + 1 : n * ZR + 65]
+            S[g, n] = value if M is None else (value * M[n]).astype(S.dtype)
         return carry
 
     lax.fori_loop(0, NG, group, 0)
 
 
-def conv_kernel(fields, land, w, bias, conv_out, masked_out, X, EL, ER, LH, RH, PS, Z, W, AB, S, land_pad, send, recv):
+def conv_kernel(fields, land, w, bias, conv_out, X, EL, ER, LH, RH, EH, PS, Z, W, PM, AB, S, M, land_pad, send, recv,
+                load):
     lon, lat = lax.axis_index("lon"), lax.axis_index("lat")
-    land_pad[...] = jnp.zeros((128, 128), F32)
-    land_pad[0:CLON, 0:CLAT] = land[...].astype(F32)
-    land_t = land_pad[...].T[0:CLAT]
-
-    def mask_block(n, carry):
-        turned = pltpu.roll(land_t, lax.rem(128 - 8 * n, 128), axis=1)
-        for m in range(4):
-            pair = []
-            for i in (2 * m, 2 * m + 1):
-                keep = jnp.broadcast_to(turned[:, i : i + 1], (CLAT, C))
-                pair.append(fields[8 * n + i].astype(F32) * keep)
-            for t in range(NJ):
-                both = jnp.concatenate([pair[0][8 * t : 8 * t + 8], pair[1][8 * t : 8 * t + 8]], axis=0)
-                X[(n + 1) * NJ + t, 16 * m : 16 * m + 16] = both.astype(BF16)
-        return carry
-
-    lax.fori_loop(0, NI, mask_block, 0)
-    pack_edges(X, EL, ER, NJ)
-    greet(neighbours(lon, lat))
+    around = neighbours(lon, lat)
+    greet(around)
+    copy_in = pltpu.make_async_copy(fields, X.at[pl.ds(1, 24)], load)
+    copy_in.start()
+    land_pad[...] = jnp.zeros((CLAT, 128), F32)
+    land_pad[:, 0:CLON] = land[...].astype(F32)
+    land_t = land_pad[...]
+    lane = iota((CLAT, 128), 1)
+    expand_mask(jnp.where((lane < 4) | (lane >= CLON + 4), 1.0, pltpu.roll(land_t, 4, axis=1)), M, NI + 1)
+    low = iota((8, 128), 0) < 4
+    masks = []
+    for east in range(2):
+        edge = land_pad[56 * east : 56 * east + 8]
+        turned = pltpu.roll(edge, 4, axis=0)
+        edge = jnp.where(low, turned, edge) if east else jnp.where(low, edge, turned)
+        masks.append(jnp.where(low, edge, pltpu.roll(edge, 127, axis=1)))
+    copy_in.wait()
+    pack_edges(X, EL, ER, masks)
+    for at, first in ((1, 0), (24, CLON - 4)):
+        for i in range(4):
+            keep = jnp.broadcast_to(land_t[:, first + i : first + i + 1], (CLAT, C))
+            X[at, i] = (X[at, i].astype(F32) * keep).astype(BF16)
+    greeted(around)
     copies = halo_copies(X, EL, ER, LH, RH, send, recv, lon, lat)
     for copy in copies:
         copy.start()
+    build_permutation(PM)
+    clear_margins(PS)
+
+    def cells(k, i):
+        return X[2 * k + i // 4, i % 4]
+
+    for blocks in INNER:
+        group_blocks(cells, blocks, PM, PS, M)
     build_weights(w, W, False)
-    masked_out[...] = X[NJ : NJ + TILES]
     for copy in copies:
         copy.wait()
-    keep_left = jnp.where(lat > 0, 1.0, 0.0)
-    keep_right = jnp.where(lat < N_LAT - 1, 1.0, 0.0)
-    spread_blocks(X, LH, RH, PS, Z, keep_left, keep_right)
-    banded_conv(Z, W, AB, S)
+    group_blocks(cells, (0, NI), PM, PS, M)
+    group_halos(LH, RH, EH, PM, PS, lat)
+    shift_blocks(PS, Z)
+    banded_conv(Z, W, AB, S, None)
     offset = jnp.broadcast_to(bias[...], (8, C))
 
     def back(n, carry):
@@ -213,38 +299,40 @@
     return [pl.BlockSpec(memory_space=pltpu.VMEM)] * n
 
 
-def halo_scratch():
+def hbm(n):
+    return [pl.BlockSpec(memory_space=pl.ANY)] * n
+
+
+def halo_scratch(kind):
     return [
-        pltpu.VMEM((14 * NJ, 64, C), BF16),
+        pltpu.VMEM((26, 4, CLAT, C), BF16),
         pltpu.VMEM((NI, 32, C), BF16),
         pltpu.VMEM((NI, 32, C), BF16),
         pltpu.VMEM((14, 32, C), BF16),
         pltpu.VMEM((14, 32, C), BF16),
-        pltpu.VMEM((NG, 104, 128), F32),
+        pltpu.VMEM((7, 16, 1024), BF16),
+        pltpu.VMEM((NG, NI + 1, 104, 128), F32),
         pltpu.VMEM((NG, NI + 1, ZR, 512), BF16),
         pltpu.VMEM((NG, 1024, 256), BF16),
+        pltpu.VMEM((1024, 1024), BF16),
         pltpu.VMEM((NI * ZR, 128), F32),
-        pltpu.VMEM((NG, NI, 64, 128), F32),
+        pltpu.VMEM((NG, NI, 64, 128), kind),
+        pltpu.VMEM((NI + 1, 64, 128), F32),
+        pltpu.VMEM((CLAT, 128), F32),
     ]
 
 
 def forward_conv(fields, land, w, bias):
+    dma = pltpu.SemaphoreType.DMA
     return pl.pallas_call(
         conv_kernel,
         name="forward_conv",
-        out_shape=(jax.ShapeDtypeStruct((TILES, 64, C), F32), jax.ShapeDtypeStruct((TILES, 64, C), BF16)),
-        in_specs=vmem(4),
-        out_specs=tuple(vmem(2)),
-        scratch_shapes=halo_scratch()
-        + [pltpu.VMEM((128, 128), F32), pltpu.SemaphoreType.DMA((8,)), pltpu.SemaphoreType.DMA((8,))],
+        out_shape=jax.ShapeDtypeStruct((TILES, 64, C), F32),
+        in_specs=hbm(1) + vmem(3),
+        out_specs=vmem(1)[0],
+        scratch_shapes=halo_scratch(F32) + [dma((8,)), dma((8,)), dma],
         compiler_params=pltpu.CompilerParams(collective_id=0, has_side_effects=True, vmem_limit_bytes=VMEM_LIMIT),
     )(fields, land, w, bias)
-
-
-def transposed_land(land, land_pad):
-    land_pad[...] = jnp.zeros((128, 128), F32)
-    land_pad[0:CLON, 0:CLAT] = land[...].astype(F32)
-    return land_pad[...].T[0:CLAT]
 
 
 def normal_cdf(h, square):
@@ -255,14 +343,17 @@
 
 
 def mlp_kernel(tile_ids, conv, fields, upstream, land, gain, shift, w_in, b_in, w_out, b_out, scale,
-               mixed, d_conv_out, shares, branch, w_in_t, w_out_t, g_in, g_out, g_bin, sums, land_pad, land_tr):
+               mixed, d_conv_out, shares, branch, d_conv, w_in_t, w_out_t, g_in, g_out, g_bin, sums, land_tr, own, load):
     slots = 4
     rows = slots * 64
-    land_tr[...] = transposed_land(land, land_pad)
+    copy_in = pltpu.make_async_copy(fields, own, load)
+    copy_in.start()
+    land_tr[...] = jnp.zeros((CLAT, 128), F32)
+    land_tr[:, 0:CLON] = land[...].astype(F32)
     w_in_t[...] = w_in[...].astype(F32).T.astype(BF16)
     w_out_t[...] = w_out[...].astype(F32).T.astype(BF16)
     branch[...] = jnp.zeros(branch.shape, F32)
-    d_conv_out[...] = jnp.zeros(d_conv_out.shape, BF16)
+    d_conv[...] = jnp.zeros(d_conv.shape, F32)
     for acc in (g_in, g_out, g_bin, sums):
         acc[...] = jnp.zeros(acc.shape, F32)
     gain_row, shift_row, scale_row = gain[...], shift[...], scale[...]
@@ -307,29 +398,32 @@
         g_bin[...] += jnp.sum(d_hidden.reshape(rows // 8, 8, FF), axis=0)
         d_norm = jnp.dot(d_hidden_b, w_in_t[...], preferred_element_type=F32)
         d_scaled = d_norm * gain_row
-        d_conv = inv_std * (
+        d_cells = inv_std * (
             d_scaled
             - jnp.mean(d_scaled, axis=-1, keepdims=True)
             - normed * jnp.mean(d_scaled * normed, axis=-1, keepdims=True)
         )
-        for k, term in enumerate((d_conv, d_norm * normed, d_norm, d_out, active * output * up)):
+        for k, term in enumerate((d_cells, d_norm * normed, d_norm, d_out, active * output * up)):
             sums[k] += jnp.sum(term.reshape(rows // 8, 8, C), axis=0)
-        d_conv_b = d_conv.astype(BF16)
         for q in range(slots):
 
             @pl.when(ids[q] >= 0)
             def _(q=q):
                 branch[tiles[q]] = branch_rows[64 * q : 64 * q + 64]
-                d_conv_out[tiles[q]] = d_conv_b[64 * q : 64 * q + 64]
+                d_conv[tiles[q]] = d_cells[64 * q : 64 * q + 64]
 
         return carry
 
     lax.fori_loop(0, TCAP // slots, step, 0)
+
+    copy_in.wait()
 
     def mix(n, carry):
         for i in range(8):
             rows_i = jnp.concatenate([branch[n * NJ + t, 8 * i : 8 * i + 8] for t in range(NJ)], axis=0)
-            mixed[8 * n + i] = (fields[8 * n + i].astype(F32) + rows_i).astype(BF16)
+            mixed[8 * n + i] = (own[2 * n + i // 4, i % 4].astype(F32) + rows_i).astype(BF16)
+            rows_i = jnp.concatenate([d_conv[n * NJ + t, 8 * i : 8 * i + 8] for t in range(NJ)], axis=0)
+            d_conv_out[2 * n + i // 4, i % 4] = rows_i.astype(BF16)
         return carry
 
     lax.fori_loop(0, NI, mix, 0)
@@ -353,12 +447,13 @@
         name="listed_mlp",
         out_shape=(
             jax.ShapeDtypeStruct((CLON, CLAT, C), BF16),
-            jax.ShapeDtypeStruct((TILES, 64, C), BF16),
+            jax.ShapeDtypeStruct((24, 4, CLAT, C), BF16),
             jax.ShapeDtypeStruct((N_LAT, 72, 128), F32),
         ),
-        in_specs=[pl.BlockSpec(memory_space=pltpu.SMEM)] + vmem(11),
+        in_specs=[pl.BlockSpec(memory_space=pltpu.SMEM)] + vmem(1) + hbm(1) + vmem(9),
         out_specs=tuple(vmem(3)),
         scratch_shapes=[
+            pltpu.VMEM((TILES, 64, C), F32),
             pltpu.VMEM((TILES, 64, C), F32),
             pltpu.VMEM((FF, C), BF16),
             pltpu.VMEM((C, FF), BF16),
@@ -366,26 +461,19 @@
             pltpu.VMEM((C, FF), F32),
             pltpu.VMEM((8, FF), F32),
             pltpu.VMEM((5, 8, C), F32),
-            pltpu.VMEM((128, 128), F32),
             pltpu.VMEM((CLAT, 128), F32),
+            pltpu.VMEM((24, 4, CLAT, C), BF16),
+            pltpu.SemaphoreType.DMA,
         ],
         compiler_params=pltpu.CompilerParams(vmem_limit_bytes=VMEM_LIMIT),
     )(tile_ids, conv, fields, upstream, land, gain, shift, w_in, b_in, w_out, b_out, scale)
 
 
-def spread_masked(masked, PS, MP):
-    PS[:, 0:8] = jnp.zeros((NG, 8, 128), F32)
-    PS[:, 72:104] = jnp.zeros((NG, 32, 128), F32)
-
+def pair_masked(PS, MP):
     def block(n, carry):
-        for t in range(NJ):
-            tile = masked[n * NJ + t].astype(F32)
-            rows = block_transpose([tile[8 * i : 8 * i + 8] for i in range(8)])
-            for g in range(NG):
-                PS[g, 8 + 8 * t : 16 + 8 * t] = rows[g]
         for g in range(NG):
-            MP[g, n, :, 0:128] = PS[g, 8 : 8 + ZR].astype(BF16)
-            MP[g, n, :, 128:256] = PS[g, 7 : 7 + ZR].astype(BF16)
+            MP[g, n, :, 0:128] = PS[g, n, 16 : 16 + ZR].astype(BF16)
+            MP[g, n, :, 128:256] = PS[g, n, 15 : 15 + ZR].astype(BF16)
         return carry
 
     lax.fori_loop(0, NI, block, 0)
@@ -436,17 +524,25 @@
         tap_shares[q] = turned[8 * q : 8 * q + 8]
 
 
-def grad_kernel(d_conv, masked, upstream, land, w, shares,
+def grad_kernel(d_conv, fields, upstream, land, w, shares,
                 grad_input, out_win, out_wout, out_dw, out_channel, out_bin,
-                X, EL, ER, LH, RH, PS, Z, W, AB, S, MP, G, taps, square, tap_shares, parts, tap_parts, mine, whole,
-                send, recv, send_one, recv_one, send_tap, recv_tap, send_two, recv_two):
+                X, EL, ER, LH, RH, EH, PS, Z, W, PM, AB, S, M, land_pad,
+                own, up, MP, G, taps, square, tap_shares, parts, tap_parts, mine, whole,
+                send, recv, send_one, recv_one, send_tap, recv_tap, send_two, recv_two, load):
     lon, lat = lax.axis_index("lon"), lax.axis_index("lat")
-    X[NJ : NJ + TILES] = d_conv[...]
-    pack_edges(X, EL, ER, NJ)
     around = neighbours(lon, lat)
-    others = [(lon, lax.rem(lat + d, N_LAT)) for d in range(2, N_LAT - 1)]
-    others += [(lax.rem(lon + d, N_LON), lat) for d in range(2, N_LON - 1)]
-    greet(around + others)
+    around += [(lon, lax.rem(lat + d, N_LAT)) for d in range(2, N_LAT - 1)]
+    around += [(lax.rem(lon + d, N_LON), lat) for d in range(2, N_LON - 1)]
+    greet(around)
+    copy_in = pltpu.make_async_copy(d_conv, X.at[pl.ds(1, 24)], load.at[0])
+    copy_own = pltpu.make_async_copy(fields, own, load.at[1])
+    copy_up = pltpu.make_async_copy(upstream, up, load.at[2])
+    copy_in.start()
+    copy_own.start()
+    copy_up.start()
+    copy_in.wait()
+    pack_edges(X, EL, ER, None)
+    greeted(around)
     copies = halo_copies(X, EL, ER, LH, RH, send, recv, lon, lat)
     for copy in copies:
         copy.start()
@@ -461,18 +557,32 @@
             device_id=(lon, to), device_id_type=MESH))
     for copy in share_copies:
         copy.start()
+    build_permutation(PM)
+    clear_margins(PS)
+    land_pad[...] = jnp.zeros((CLAT, 128), F32)
+    land_pad[:, 0:CLON] = land[...].astype(F32)
+    expand_mask(land_pad[...], M, NI)
+    copy_own.wait()
+    for blocks in ((0, 1, 2, 3), (4, 5, 6, 7), (8, 9, 10, 11)):
+        group_blocks(lambda k, i: own[2 * k + i // 4, i % 4], blocks, PM, PS, M)
+    pair_masked(PS, MP)
     build_weights(w, W, True)
-    spread_masked(masked, PS, MP)
+
+    def cells(k, i):
+        return X[2 * k + i // 4, i % 4]
+
+    for blocks in INNER:
+        group_blocks(cells, blocks, PM, PS, None)
     for copy in copies:
         copy.wait()
-    keep_left = jnp.where(lat > 0, 1.0, 0.0)
-    keep_right = jnp.where(lat < N_LAT - 1, 1.0, 0.0)
-    spread_blocks(X, LH, RH, PS, Z, keep_left, keep_right)
+    group_blocks(cells, (0, NI), PM, PS, None)
+    group_halos(LH, RH, EH, PM, PS, lat)
+    shift_blocks(PS, Z)
     tap_gradients(Z, MP, G, taps)
     gather_taps(taps, square, tap_shares)
     for copy in tap_copies:
         copy.start()
-    banded_conv(Z, W, AB, S)
+    banded_conv(Z, W, AB, S, M)
     for copy in share_copies:
         copy.wait()
     for copy in tap_copies:
@@ -492,56 +602,53 @@
     ]
     for copy in last_copies:
         copy.start()
-    square[...] = jnp.zeros((128, 128), F32)
-    square[0:CLON, 0:CLAT] = land[...].astype(F32)
-    land_t = square[...].T[0:CLAT]
-
-    def back(n, carry):
-        turned = pltpu.roll(land_t, lax.rem(128 - 8 * n, 128), axis=1)
-        for t in range(NJ // 2):
-            low = block_transpose([S[g, n, 16 * t : 16 * t + 8] for g in range(NG)])
-            high = block_transpose([S[g, n, 16 * t + 8 : 16 * t + 16] for g in range(NG)])
-            for i in range(8):
-                keep = jnp.broadcast_to(turned[16 * t : 16 * t + 16, i : i + 1], (16, C))
-                value = jnp.concatenate([low[i], high[i]], axis=0) * keep
-                up = upstream[8 * n + i, 16 * t : 16 * t + 16].astype(F32)
-                grad_input[8 * n + i, 16 * t : 16 * t + 16] = (up + value).astype(BF16)
-        return carry
-
-    lax.fori_loop(0, NI, back, 0)
+    copy_up.wait()
+    for first in range(0, NI, 4):
+        rows = [S[g, first : first + 4].reshape(256, 128) for g in range(NG)]
+        lhs = jnp.concatenate(rows, axis=1)
+
+        def back(n, carry, lhs=lhs, first=first):
+            both = jnp.dot(lhs, PM[:, pl.ds(pl.multiple_of(256 * n, 256), 256)], preferred_element_type=F32)
+            for h in range(2):
+                for m in range(4):
+                    at = 8 * (first + m) + 2 * n + h
+                    value = up[at].astype(F32) + both[64 * m : 64 * m + 64, 128 * h : 128 * h + 128]
+                    grad_input[at] = value.astype(BF16)
+            return carry
+
+        lax.fori_loop(0, 4, back, 0)
     for copy in last_copies:
         copy.wait()
     total = mine[...]
     for d in range(1, N_LON):
         total += whole[d]
-    square[...] = jnp.zeros((128, 128), F32)
-    square[0:32] = total[0:32]
-    out_win[...] = square[...].T[:, 0:32]
+    out_win[...] = total[0:32]
     out_wout[...] = total[32:64]
     small = total[64:72]
     out_bin[...] = pltpu.roll(small, lax.rem(128 - 32 * lax.rem(lat, 4), 128), axis=1)[0:1, 0:32]
     out_channel[...] = pltpu.roll(small, lax.rem(128 - 8 * lat, 128), axis=1)[1:6, 0:8]
-    square[0:8] = total[72:80]
-    out_dw[...] = square[...].T[0:49, 0:8]
-
-
-def backward_conv(d_conv, masked, upstream, land, w, shares):
+    out_dw[...] = total[72:80, 0:49]
+
+
+def backward_conv(d_conv, fields, upstream, land, w, shares):
     dma = pltpu.SemaphoreType.DMA
     return pl.pallas_call(
         grad_kernel,
         name="backward_conv",
         out_shape=(
             jax.ShapeDtypeStruct((CLON, CLAT, C), BF16),
-            jax.ShapeDtypeStruct((C, 32), F32),
             jax.ShapeDtypeStruct((32, C), F32),
-            jax.ShapeDtypeStruct((49, 8), F32),
+            jax.ShapeDtypeStruct((32, C), F32),
+            jax.ShapeDtypeStruct((8, 49), F32),
             jax.ShapeDtypeStruct((5, 8), F32),
             jax.ShapeDtypeStruct((1, 32), F32),
         ),
-        in_specs=vmem(6),
+        in_specs=hbm(3) + vmem(3),
         out_specs=tuple(vmem(6)),
-        scratch_shapes=halo_scratch()
+        scratch_shapes=halo_scratch(BF16)
         + [
+            pltpu.VMEM((24, 4, CLAT, C), BF16),
+            pltpu.VMEM((CLON, CLAT, C), BF16),
             pltpu.VMEM((NG, NI, ZR, 256), BF16),
             pltpu.VMEM((2, 256, 512), F32),
             pltpu.VMEM((NG, 56, 128), F32),
@@ -551,10 +658,10 @@
             pltpu.VMEM((N_LAT, 8, 128), F32),
             pltpu.VMEM((80, 128), F32),
             pltpu.VMEM((N_LON, 80, 128), F32),
-            dma((8,)), dma((8,)), dma((N_LAT,)), dma((N_LAT,)), dma((N_LAT,)), dma((N_LAT,)), dma((N_LON,)), dma((N_LON,)),
+            dma((8,)), dma((8,)), dma((N_LAT,)), dma((N_LAT,)), dma((N_LAT,)), dma((N_LAT,)), dma((N_LON,)), dma((N_LON,)), dma((3,)),
         ],
         compiler_params=pltpu.CompilerParams(collective_id=1, has_side_effects=True, vmem_limit_bytes=VMEM_LIMIT),
-    )(d_conv, masked, upstream, land, w, shares)
+    )(d_conv, fields, upstream, land, w, shares)
 
 
 def per_device(fields, land_sea, tile_list, upstream, dw_weight, dw_bias, ln_gain, ln_bias, w_in, b_in, w_out, b_out,
@@ -562,13 +669,14 @@
     def row(v):
         return v.reshape(1, -1)
 
-    conv, masked = forward_conv(fields, land_sea, dw_weight, row(dw_bias))
+    fours = fields.reshape(24, 4, CLAT, C)
+    land = land_sea.T
+    conv = forward_conv(fours, land, dw_weight, row(dw_bias))
     mixed, d_conv, shares = listed_mlp(
-        tile_list.reshape(-1), conv, fields, upstream, land_sea, row(ln_gain), row(ln_bias), w_in, row(b_in), w_out,
+        tile_list.reshape(-1), conv, fours, upstream, land, row(ln_gain), row(ln_bias), w_in, row(b_in), w_out,
         row(b_out), row(layer_scale))
-    grad_input, g_win, g_wout, g_dw, g_channel, g_bin = backward_conv(
-        d_conv, masked, upstream, land_sea, dw_weight, shares)
-    return mixed, grad_input, g_win, g_wout, g_dw, g_channel, g_bin.reshape(-1)
+    grad_input, g_win, g_wout, g_dw, g_channel, g_bin = backward_conv(d_conv, fours, upstream, land, dw_weight, shares)
+    return mixed, grad_input, g_win.T, g_wout, g_dw.T, g_channel, g_bin.reshape(-1)
 
 
 def solution(mesh):

time: 121 us -> 106 us (0.88)
  Pallas kernels: 111 us -> 99.6 us
  local copies, waits for them, and re-layouts: 8.8 us -> 5.6 us
    pallas_call x1, Pallas kernels: 36.9 us -> 29 us  [forward_conv(): pl.pallas_call(conv_kernel, name='forward_conv', out_shape=jax.ShapeDtype...]
    unnamed x13 -> x16, local copies, waits for them, and re-layouts: 8.8 us -> 5.6 us
    pallas_call x1, Pallas kernels: 45.1 us -> 42 us  [backward_conv(): pl.pallas_call(grad_kernel, name='backward_conv', out_shape=(jax.ShapeDty...]
where the time goes in v2:
time: 106 us
  Pallas kernels  99.6 us (94%)
  local copies, waits for them, and re-layouts  5.6 us (5%)
    pallas_call x1, Pallas kernels, backward_conv(): pl.pallas_call(grad_kernel, name='backward_conv', out_shape=(jax.ShapeDty...  42 us
    pallas_call x1, Pallas kernels, forward_conv(): pl.pallas_call(conv_kernel, name='forward_conv', out_shape=jax.ShapeDtype...  29 us
    pallas_call x1, Pallas kernels, listed_mlp(): pl.pallas_call(mlp_kernel, name='listed_mlp', out_shape=(jax.ShapeDtypeSt...  28.6 us
    unnamed x16, local copies, waits for them, and re-layouts  5.6 us

profile of v2, /device:TPU:0, one launch (start us, length us, event | category | flops | bytes accessed | tf_op | source)
XLA Modules:
  0.0 105.9 jit_solution(4372958130070622327)
XLA Ops:
  0.6 29.0 %forward_conv.1.conv = f32[96,64,128]{2,1,0:T(8,128)} custom-call(bf16[24,4,64,128]{3,2,1,0:T(8,128)(2,1)} %bitcast.12, s32[64,96]{1,0:T(8,128)} %bitcast.15, f32[49,128]{1,0:T(8,128)} %w.3, f32[1,128]{1,0:T(1,128)} %bitcast.21), custom_call_target="tpu_custom_call" | custom-call | tf_op jit(solution)/shard_map/forward_conv/pallas_call | solution.py:327
  29.7 28.6 %listed_mlp.1 = (bf16[96,64,128]{2,1,0:T(8,128)(2,1)}, bf16[24,4,64,128]{3,2,1,0:T(8,128)(2,1)}, f32[16,72,128]{2,1,0:T(8,128)}) custom-call(s32[72]{0:T(128)} %bitcast.22, f32[96,64,128]{2,1,0:T(8,128)} %forward_conv.1.conv, bf16[24,4,64,128]{3,2,1,0:T(8,128)(2,1)} %bitcast.13, bf16[96,64,128]{2,1,0:T(8,128)(2,1)} %upstream.3, s32[64,96]{1,0:T(8,128)} %bitcast.16, ...), custom_call_target="tpu_custom_call" | custom-call | tf_op jit(solution)/shard_map/listed_mlp/pallas_call | solution.py:445
  58.3 42.0 %backward_conv.1 = (bf16[96,64,128]{2,1,0:T(8,128)(2,1)}, f32[32,128]{1,0:T(8,128)}, f32[32,128]{1,0:T(8,128)}, f32[8,49]{1,0:T(8,128)}, f32[5,8]{1,0:T(8,128)}, /*index=5*/f32[1,32]{1,0:T(1,128)}) custom-call(bf16[24,4,64,128]{3,2,1,0:T(8,128)(2,1)} %get-tuple-element.17.d_conv, bf16[24,4,64,128]{3,2,1,0:T(8,128)(2,1)} %bitcast.14, ...), custom_call_target="tpu_custom_call" | custom-call | tf_op jit(solution)/shard_map/backward_conv/pallas_call | solution.py:635
  100.3 0.0 copy-start.1
  100.3 0.0 copy-start
  100.3 0.0 copy-start.3
  100.3 0.0 copy-start.2
  100.3 0.0 copy-start.4
  100.3 2.7 %copy.26 = bf16[96,64,128]{2,1,0:T(8,128)(2,1)} copy(bf16[96,64,128]{2,1,0:T(8,128)(2,1)} %get-tuple-element.33) | data formatting | bytes 3145728
  103.0 0.0 copy-done.1
  103.0 0.6 copy.27
  103.6 0.0 copy-done
  103.6 0.6 copy.28
  104.2 0.0 copy-done.3
  104.2 0.6 copy.29
  104.8 0.0 copy-done.2
  104.8 0.6 copy.30
  105.4 0.0 copy-done.4
  105.4 0.5 copy.31
Async XLA Ops:
  100.3 2.7 %copy-start.1 = (f32[32,128]{1,0:T(8,128)S(1)}, f32[32,128]{1,0:T(8,128)}, u32[]{:S(2)}) copy-start(f32[32,128]{1,0:T(8,128)} %get-tuple-element.20) | copy-start | bytes 49156
  100.3 3.3 %copy-start = (f32[32,128]{1,0:T(8,128)S(1)}, f32[32,128]{1,0:T(8,128)}, u32[]{:S(2)}) copy-start(f32[32,128]{1,0:T(8,128)} %get-tuple-element.35) | copy-start | bytes 49156
  100.3 3.9 %copy-start.3 = (f32[8,49]{1,0:T(8,128)S(1)}, f32[8,49]{1,0:T(8,128)}, u32[]{:S(2)}) copy-start(f32[8,49]{1,0:T(8,128)} %get-tuple-element.22) | copy-start | bytes 4708
  100.3 4.5 %copy-start.2 = (f32[5,8]{1,0:T(8,128)S(1)}, f32[5,8]{1,0:T(8,128)}, u32[]{:S(2)}) copy-start(f32[5,8]{1,0:T(8,128)} %get-tuple-element.37) | copy-start | bytes 484
  100.3 5.1 %copy-start.4 = (f32[1,32]{1,0:T(1,128)S(1)}, f32[1,32]{1,0:T(1,128)}, u32[]{:S(2)}) copy-start(f32[1,32]{1,0:T(1,128)} %get-tuple-element.24) | copy-start | bytes 388

commit v3 on v2

--- a/solution.py
+++ b/solution.py
@@ -21,23 +21,13 @@
 N_LON, N_LAT = 8, 16
 SHIFTS = (-4, -2, 0, 2)
 GRAD_SCALE = 1.0 / math.sqrt(768 * 1024)
-VMEM_LIMIT = 56 * 1024 * 1024
+VMEM_LIMIT = 50 * 1024 * 1024
 ERF_COEFS = (0.7978822019328625, 0.03634471964933557, -4.4922105999092954e-05,
              -5.0349129465290195e-05, 3.0967343000773035e-06, -6.63025075261232e-08)
 
 
 def iota(shape, dim):
     return lax.broadcasted_iota(jnp.int32, shape, dim)
-
-
-def block_transpose(rows):
-    block = iota(rows[0].shape, 1) // 16
-    turned = [r if n == 0 else pltpu.roll(r, 16 * n, axis=1) for n, r in enumerate(rows)]
-    u = [turned[(-n) % 8] for n in range(8)]
-    for s in (1, 2, 4):
-        bit = (block & s) != 0
-        u = [jnp.where(bit, u[(m - s) % 8], u[m]) for m in range(8)]
-    return [r if m == 0 else pltpu.roll(r, 128 - 16 * m, axis=1) for m, r in enumerate(u)]
 
 
 def build_weights(w_ref, W, flip):
@@ -49,7 +39,7 @@
     lane_i = iota((8, 128), 1) // 16
     same = (iota((16, 128), 0) == iota((16, 128), 1) % 16).astype(F32)
 
-    def group(g, carry):
+    def group(g):
         spread = jnp.where(iota((128, 128), 0) == 16 * g + iota((128, 128), 1) % 16, 1.0, 0.0).astype(BF16)
         rep = jnp.dot(taps, spread, preferred_element_type=F32)
         for i_in in range(16):
@@ -64,9 +54,9 @@
                 e = (b - 3 - parity + 4) // 2
                 row = jnp.broadcast_to(v[b : b + 1], (16, 128)) * same
                 W[g, base + 128 * e : base + 128 * e + 16, 128 * parity : 128 * parity + 128] = row.astype(BF16)
-        return carry
-
-    lax.fori_loop(0, NG, group, 0)
+
+    for g in range(NG):
+        group(g)
 
 
 def build_permutation(PM):
@@ -86,12 +76,14 @@
     value = land_ext.astype(BF16)
     row, block = iota((128, 128), 0), iota((128, 128), 1) // 16
 
-    def one(k, carry):
+    for k in range(count):
         pick = jnp.where(row == 8 * k + block, 1.0, 0.0).astype(BF16)
         M[k] = jnp.dot(value, pick, preferred_element_type=F32)
-        return carry
-
-    lax.fori_loop(0, count, one, 0)
+
+
+def with_ones(land_t):
+    lane = iota((CLAT, 128), 1)
+    return jnp.where((lane < 4) | (lane >= CLON + 4), 1.0, pltpu.roll(land_t, 4, axis=1))
 
 
 def pack_edges(X, EL, ER, masks):
@@ -166,18 +158,14 @@
 
 
 def group_blocks(cells, blocks, PM, PS, M):
-    rows = len(blocks) * 64
     lhs = jnp.concatenate([jnp.concatenate([cells(k, i) for k in blocks], axis=0) for i in range(8)], axis=1)
 
-    def pair(n, carry):
-        both = jnp.dot(lhs, PM[:, pl.ds(pl.multiple_of(256 * n, 256), 256)], preferred_element_type=F32)
+    for n in range(NG // 2):
+        both = jnp.dot(lhs, PM[:, 256 * n : 256 * n + 256], preferred_element_type=F32)
         for h in range(2):
             for m, k in enumerate(blocks):
                 part = both[64 * m : 64 * m + 64, 128 * h : 128 * h + 128]
                 PS[2 * n + h, k, 16:80] = part if M is None else part * M[k]
-        return carry
-
-    lax.fori_loop(0, NG // 2, pair, 0)
 
 
 def group_halos(LH, RH, EH, PM, PS, lat):
@@ -200,46 +188,42 @@
         for i in range(8):
             EH[n, :, 128 * i : 128 * i + 128] = jnp.concatenate([first[i], second[i]], axis=0).astype(BF16)
 
-    def pair(n, carry):
-        both = jnp.dot(EH[...].reshape(112, 1024), PM[:, pl.ds(pl.multiple_of(256 * n, 256), 256)],
-                       preferred_element_type=F32)
+    edges = EH[...].reshape(112, 1024)
+    for n in range(NG // 2):
+        both = jnp.dot(edges, PM[:, 256 * n : 256 * n + 256], preferred_element_type=F32)
         for h in range(2):
             for k in range(NI + 1):
                 part = both[8 * k : 8 * k + 8, 128 * h : 128 * h + 128]
                 PS[2 * n + h, k, 8:16] = part
                 PS[2 * n + h, k, 80:88] = part
-        return carry
-
-    lax.fori_loop(0, NG // 2, pair, 0)
-
-
-def shift_blocks(PS, Z):
-    def block(k, carry):
-        for g in range(NG):
-            for e, shift in enumerate(SHIFTS):
-                Z[g, k, :, 128 * e : 128 * e + 128] = PS[g, k, 16 + shift : 16 + shift + ZR].astype(BF16)
-        return carry
-
-    lax.fori_loop(0, NI + 1, block, 0)
+
+
+def shift_blocks(PS, Z, g):
+    for k in range(NI + 1):
+        for e, shift in enumerate(SHIFTS):
+            Z[g, k, :, 128 * e : 128 * e + 128] = PS[g, k, 16 + shift : 16 + shift + ZR].astype(BF16)
 
 
 INNER = ((1, 2, 3, 4), (5, 6, 7, 8), (9, 10, 11))
 
 
-def banded_conv(Z, W, AB, S, M):
-    def group(g, carry):
-        lhs = jnp.concatenate([Z[g, 0:NI].reshape(NI * ZR, 512), Z[g, 1 : NI + 1].reshape(NI * ZR, 512)], axis=1)
-        both = jnp.dot(lhs, W[g], preferred_element_type=F32)
-        AB[...] = both[:, 128:256]
-        for n in range(NI):
-            value = both[n * ZR : n * ZR + 64, 0:128] + AB[n * ZR + 1 : n * ZR + 65]
-            S[g, n] = value if M is None else (value * M[n]).astype(S.dtype)
-        return carry
-
-    lax.fori_loop(0, NG, group, 0)
-
-
-def conv_kernel(fields, land, w, bias, conv_out, X, EL, ER, LH, RH, EH, PS, Z, W, PM, AB, S, M, land_pad, send, recv,
+def banded_conv(Z, W, AB, S, M, g):
+    lhs = jnp.concatenate([Z[g, 0:NI].reshape(NI * ZR, 512), Z[g, 1 : NI + 1].reshape(NI * ZR, 512)], axis=1)
+    both = jnp.dot(lhs, W[g], preferred_element_type=F32)
+    AB[g % 2] = both[:, 128:256]
+    for n in range(NI):
+        value = both[n * ZR : n * ZR + 64, 0:128] + AB[g % 2, n * ZR + 1 : n * ZR + 65]
+        S[g, n] = (value if M is None else value * M[n]).astype(BF16)
+
+
+def ungroup(S, PM, blocks, put):
+    rows = [jnp.concatenate([S[g, k] for k in blocks], axis=0) for g in range(NG)]
+    lhs = jnp.concatenate(rows, axis=1)
+    for n in range(NG // 2):
+        put(n, jnp.dot(lhs, PM[:, 256 * n : 256 * n + 256], preferred_element_type=F32))
+
+
+def conv_kernel(fields, land, w, conv_out, lon_halo, left_halo, right_halo, X, EL, ER, LH, RH, EH, PS, Z, W, PM, AB, S, M, land_pad, send, recv,
                 load):
     lon, lat = lax.axis_index("lon"), lax.axis_index("lat")
     around = neighbours(lon, lat)
@@ -249,8 +233,7 @@
     land_pad[...] = jnp.zeros((CLAT, 128), F32)
     land_pad[:, 0:CLON] = land[...].astype(F32)
     land_t = land_pad[...]
-    lane = iota((CLAT, 128), 1)
-    expand_mask(jnp.where((lane < 4) | (lane >= CLON + 4), 1.0, pltpu.roll(land_t, 4, axis=1)), M, NI + 1)
+    expand_mask(with_ones(land_t), M, NI + 1)
     low = iota((8, 128), 0) < 4
     masks = []
     for east in range(2):
@@ -279,20 +262,25 @@
     build_weights(w, W, False)
     for copy in copies:
         copy.wait()
+    lon_halo[0] = X[0]
+    lon_halo[1] = X[25]
+    left_halo[...] = LH[...]
+    right_halo[...] = RH[...]
     group_blocks(cells, (0, NI), PM, PS, M)
     group_halos(LH, RH, EH, PM, PS, lat)
-    shift_blocks(PS, Z)
-    banded_conv(Z, W, AB, S, None)
-    offset = jnp.broadcast_to(bias[...], (8, C))
-
-    def back(n, carry):
-        for t in range(NJ):
-            rows = block_transpose([S[g, n, 8 * t : 8 * t + 8] for g in range(NG)])
-            for i in range(8):
-                conv_out[n * NJ + t, 8 * i : 8 * i + 8] = rows[i] + offset
-        return carry
-
-    lax.fori_loop(0, NI, back, 0)
+    for g in range(NG):
+        shift_blocks(PS, Z, g)
+        banded_conv(Z, W, AB, S, None, g)
+    for first in range(0, NI, 4):
+
+        def put(n, both, first=first):
+            for m in range(4):
+                for t in range(NJ):
+                    at = 64 * m + 8 * t
+                    value = jnp.concatenate([both[at : at + 8, 0:128], both[at : at + 8, 128:256]], axis=0)
+                    conv_out[(first + m) * NJ + t, 16 * n : 16 * n + 16] = value.astype(BF16)
+
+        ungroup(S, PM, range(first, first + 4), put)
 
 
 def vmem(n):
@@ -303,7 +291,7 @@
     return [pl.BlockSpec(memory_space=pl.ANY)] * n
 
 
-def halo_scratch(kind):
+def halo_scratch():
     return [
         pltpu.VMEM((26, 4, CLAT, C), BF16),
         pltpu.VMEM((NI, 32, C), BF16),
@@ -315,24 +303,29 @@
         pltpu.VMEM((NG, NI + 1, ZR, 512), BF16),
         pltpu.VMEM((NG, 1024, 256), BF16),
         pltpu.VMEM((1024, 1024), BF16),
-        pltpu.VMEM((NI * ZR, 128), F32),
-        pltpu.VMEM((NG, NI, 64, 128), kind),
+        pltpu.VMEM((2, NI * ZR, 128), F32),
+        pltpu.VMEM((NG, NI, 64, 128), BF16),
         pltpu.VMEM((NI + 1, 64, 128), F32),
         pltpu.VMEM((CLAT, 128), F32),
     ]
 
 
-def forward_conv(fields, land, w, bias):
+def forward_conv(fields, land, w):
     dma = pltpu.SemaphoreType.DMA
     return pl.pallas_call(
         conv_kernel,
         name="forward_conv",
-        out_shape=jax.ShapeDtypeStruct((TILES, 64, C), F32),
-        in_specs=hbm(1) + vmem(3),
-        out_specs=vmem(1)[0],
-        scratch_shapes=halo_scratch(F32) + [dma((8,)), dma((8,)), dma],
+        out_shape=(
+            pltpu.VMEM((TILES, 64, C), BF16),
+            pltpu.VMEM((2, 4, CLAT, C), BF16),
+            pltpu.VMEM((14, 32, C), BF16),
+            pltpu.VMEM((14, 32, C), BF16),
+        ),
+        in_specs=hbm(1) + vmem(2),
+        out_specs=tuple(vmem(4)),
+        scratch_shapes=halo_scratch() + [dma((8,)), dma((8,)), dma],
         compiler_params=pltpu.CompilerParams(collective_id=0, has_side_effects=True, vmem_limit_bytes=VMEM_LIMIT),
-    )(fields, land, w, bias)
+    )(fields, land, w)
 
 
 def normal_cdf(h, square):
@@ -342,9 +335,9 @@
     return 0.5 + 0.5 * jnp.tanh(h * q)
 
 
-def mlp_kernel(tile_ids, conv, fields, upstream, land, gain, shift, w_in, b_in, w_out, b_out, scale,
+def mlp_kernel(tile_ids, conv, fields, upstream, land, offset, gain, shift, w_in, b_in, w_out, b_out, scale,
                mixed, d_conv_out, shares, branch, d_conv, w_in_t, w_out_t, g_in, g_out, g_bin, sums, land_tr, own, load):
-    slots = 4
+    slots = 18
     rows = slots * 64
     copy_in = pltpu.make_async_copy(fields, own, load)
     copy_in.start()
@@ -365,7 +358,7 @@
         for q in range(slots):
             t = tiles[q]
             big, small = t // NJ, lax.rem(t, NJ)
-            conv_parts.append(conv[t])
+            conv_parts.append(conv[t].astype(F32))
             pair = upstream[pl.ds(8 * big, 8), pl.ds(16 * (small // 2), 16), :].astype(F32)
             odd = lax.rem(small, 2) == 1
             up_parts.append(jnp.where(odd, pair[:, 8:16], pair[:, 0:8]).reshape(64, C))
@@ -373,7 +366,7 @@
             live = jnp.where(ids[q] >= 0, 1.0, 0.0)
             strip = strip * live
             active_parts += [jnp.broadcast_to(strip[:, i : i + 1], (8, C)) for i in range(8)]
-        conv_rows = jnp.concatenate(conv_parts, axis=0)
+        conv_rows = jnp.concatenate(conv_parts, axis=0) + offset[...]
         up = jnp.concatenate(up_parts, axis=0)
         active = jnp.concatenate(active_parts, axis=0)
         center = conv_rows - jnp.mean(conv_rows, axis=-1, keepdims=True)
@@ -434,23 +427,22 @@
         turned_out = g_out[:, 128 * n : 128 * n + 128].T
         for m in range(4):
             q = 4 * n + m
-            shares[q, 0:32] = turned_in[32 * m : 32 * m + 32]
-            shares[q, 32:64] = turned_out[32 * m : 32 * m + 32]
-            shares[q, 64:65] = bin_row[:, 128 * n : 128 * n + 128]
-            shares[q, 65:70] = tail
-            shares[q, 70:72] = jnp.zeros((2, 128), F32)
-
-
-def listed_mlp(tile_ids, conv, fields, upstream, land, gain, shift, w_in, b_in, w_out, b_out, scale):
+            shares[q, 0:32] = turned_in[32 * m : 32 * m + 32].astype(BF16)
+            shares[q, 32:64] = turned_out[32 * m : 32 * m + 32].astype(BF16)
+            rest = [bin_row[:, 128 * n : 128 * n + 128], tail, jnp.zeros((10, 128), F32)]
+            shares[q, 64:80] = jnp.concatenate(rest, axis=0).astype(BF16)
+
+
+def listed_mlp(tile_ids, conv, fields, upstream, land, offset, gain, shift, w_in, b_in, w_out, b_out, scale):
     return pl.pallas_call(
         mlp_kernel,
         name="listed_mlp",
         out_shape=(
             jax.ShapeDtypeStruct((CLON, CLAT, C), BF16),
-            jax.ShapeDtypeStruct((24, 4, CLAT, C), BF16),
-            jax.ShapeDtypeStruct((N_LAT, 72, 128), F32),
+            pltpu.VMEM((24, 4, CLAT, C), BF16),
+            pltpu.VMEM((N_LAT, 80, 128), BF16),
         ),
-        in_specs=[pl.BlockSpec(memory_space=pltpu.SMEM)] + vmem(1) + hbm(1) + vmem(9),
+        in_specs=[pl.BlockSpec(memory_space=pltpu.SMEM)] + vmem(1) + hbm(1) + vmem(10),
         out_specs=tuple(vmem(3)),
         scratch_shapes=[
             pltpu.VMEM((TILES, 64, C), F32),
@@ -466,46 +458,39 @@
             pltpu.SemaphoreType.DMA,
         ],
         compiler_params=pltpu.CompilerParams(vmem_limit_bytes=VMEM_LIMIT),
-    )(tile_ids, conv, fields, upstream, land, gain, shift, w_in, b_in, w_out, b_out, scale)
-
-
-def pair_masked(PS, MP):
-    def block(n, carry):
-        for g in range(NG):
+    )(tile_ids, conv, fields, upstream, land, offset, gain, shift, w_in, b_in, w_out, b_out, scale)
+
+
+def pair_rows(PS, MP):
+    for g in range(NG):
+        for n in range(NI):
             MP[g, n, :, 0:128] = PS[g, n, 16 : 16 + ZR].astype(BF16)
             MP[g, n, :, 128:256] = PS[g, n, 15 : 15 + ZR].astype(BF16)
-        return carry
-
-    lax.fori_loop(0, NI, block, 0)
-
-
-def tap_gradients(Z, MP, G, taps):
+
+
+def tap_gradients(Z, MP, G, taps, groups):
     lane = iota((16, 128), 1)
     same = (iota((16, 128), 0) == lane % 16).astype(F32)
     block = lane // 16
-    taps[...] = jnp.zeros(taps.shape, F32)
-
-    def group(g, carry):
+    for g in groups:
+        taps[g] = jnp.zeros(taps.shape[1:], F32)
         lhs = MP[g].reshape(NI * ZR, 256)
         for half in range(2):
             rhs = Z[g, half : half + NI].reshape(NI * ZR, 512)
-            G[half] = lax.dot_general(lhs, rhs, (((0,), (0,)), ((), ())), preferred_element_type=F32)
+            G[g % 2, half] = lax.dot_general(lhs, rhs, (((0,), (0,)), ((), ())), preferred_element_type=F32)
         for e in range(4):
             for parity in range(2):
-                b = 3 - SHIFTS[e] - parity
+                b = 3 + SHIFTS[e] + parity
                 if not 0 <= b < 7:
                     continue
                 for a in range(7):
                     total = None
                     for i_out in range(8):
-                        half, k = divmod(i_out + 7 - a, 8)
+                        half, k = divmod(i_out + a + 1, 8)
                         at = 128 * parity + 16 * i_out
-                        piece = G[half, at : at + 16, 128 * e : 128 * e + 128]
+                        piece = G[g % 2, half, at : at + 16, 128 * e : 128 * e + 128]
                         total = piece if total is None else jnp.where(block == k, piece, total)
                     taps[g, 7 * a + b : 7 * a + b + 1] = jnp.sum(total * same, axis=0, keepdims=True)
-        return carry
-
-    lax.fori_loop(0, NG, group, 0)
 
 
 def gather_taps(taps, square, tap_shares):
@@ -524,22 +509,25 @@
         tap_shares[q] = turned[8 * q : 8 * q + 8]
 
 
-def grad_kernel(d_conv, fields, upstream, land, w, shares,
-                grad_input, out_win, out_wout, out_dw, out_channel, out_bin,
-                X, EL, ER, LH, RH, EH, PS, Z, W, PM, AB, S, M, land_pad,
-                own, up, MP, G, taps, square, tap_shares, parts, tap_parts, mine, whole,
-                send, recv, send_one, recv_one, send_tap, recv_tap, send_two, recv_two, load):
+def grad_kernel(d_conv, fields, lon_halo, left_halo, right_halo, land, w, shares,
+                S, total_out,
+                X, EL, ER, LH, RH, EH, PS, Z, W, PM, AB, M, land_pad,
+                own, MP, G, taps, square, tap_shares, parts, tap_parts, mine, whole, tap_mine, tap_whole,
+                send, recv, send_one, recv_one, send_tap, recv_tap, send_two, recv_two, send_last, recv_last, load):
     lon, lat = lax.axis_index("lon"), lax.axis_index("lat")
     around = neighbours(lon, lat)
     around += [(lon, lax.rem(lat + d, N_LAT)) for d in range(2, N_LAT - 1)]
     around += [(lax.rem(lon + d, N_LON), lat) for d in range(2, N_LON - 1)]
     greet(around)
     copy_in = pltpu.make_async_copy(d_conv, X.at[pl.ds(1, 24)], load.at[0])
-    copy_own = pltpu.make_async_copy(fields, own, load.at[1])
-    copy_up = pltpu.make_async_copy(upstream, up, load.at[2])
+    copies_own = [
+        pltpu.make_async_copy(fields, own.at[pl.ds(1, 24)], load.at[1]),
+        pltpu.make_async_copy(lon_halo.at[0], own.at[0], load.at[2]),
+        pltpu.make_async_copy(lon_halo.at[1], own.at[25], load.at[3]),
+    ]
     copy_in.start()
-    copy_own.start()
-    copy_up.start()
+    for copy in copies_own:
+        copy.start()
     copy_in.wait()
     pack_edges(X, EL, ER, None)
     greeted(around)
@@ -561,12 +549,26 @@
     clear_margins(PS)
     land_pad[...] = jnp.zeros((CLAT, 128), F32)
     land_pad[:, 0:CLON] = land[...].astype(F32)
-    expand_mask(land_pad[...], M, NI)
-    copy_own.wait()
+    land_t = land_pad[...]
+    expand_mask(with_ones(land_t), M, NI + 1)
+    for copy in copies_own:
+        copy.wait()
+    for blocks in INNER + ((0, NI),):
+        group_blocks(lambda k, i: own[2 * k + i // 4, i % 4], blocks, PM, PS, M)
+    group_halos(left_halo, right_halo, EH, PM, PS, lat)
+    for g in range(NG):
+        shift_blocks(PS, Z, g)
+    clear_margins(PS)
     for blocks in ((0, 1, 2, 3), (4, 5, 6, 7), (8, 9, 10, 11)):
-        group_blocks(lambda k, i: own[2 * k + i // 4, i % 4], blocks, PM, PS, M)
-    pair_masked(PS, MP)
+        group_blocks(lambda k, i: X[1 + 2 * k + i // 4, i % 4], blocks, PM, PS, None)
+    pair_rows(PS, MP)
+    for g in range(NG):
+        tap_gradients(Z, MP, G, taps, (g,))
+    gather_taps(taps, square, tap_shares)
+    for copy in tap_copies:
+        copy.start()
     build_weights(w, W, True)
+    expand_mask(land_t, M, NI)
 
     def cells(k, i):
         return X[2 * k + i // 4, i % 4]
@@ -577,64 +579,120 @@
         copy.wait()
     group_blocks(cells, (0, NI), PM, PS, None)
     group_halos(LH, RH, EH, PM, PS, lat)
-    shift_blocks(PS, Z)
-    tap_gradients(Z, MP, G, taps)
-    gather_taps(taps, square, tap_shares)
-    for copy in tap_copies:
-        copy.start()
-    banded_conv(Z, W, AB, S, M)
     for copy in share_copies:
         copy.wait()
+    total = shares[lat].astype(F32)
+    for d in range(1, N_LAT):
+        total += parts[d].astype(F32)
+    mine[...] = total * GRAD_SCALE
+
+    def spread(block, parts, send_sem, recv_sem):
+        made = [
+            pltpu.make_async_remote_copy(
+                src_ref=block, dst_ref=parts.at[d], send_sem=send_sem.at[d], recv_sem=recv_sem.at[d],
+                device_id=(lax.rem(lon + d, N_LON), lat), device_id_type=MESH)
+            for d in range(1, N_LON)
+        ]
+        for copy in made:
+            copy.start()
+        return made
+
+    last_copies = spread(mine, whole, send_two, recv_two)
+    for g in range(NG // 2):
+        shift_blocks(PS, Z, g)
+        banded_conv(Z, W, AB, S, M, g)
     for copy in tap_copies:
         copy.wait()
-    total = shares[lat]
-    tap_total = tap_shares[lat]
+    total = tap_shares[lat]
     for d in range(1, N_LAT):
-        total += parts[d]
-        tap_total += tap_parts[d]
-    mine[0:72] = total * GRAD_SCALE
-    mine[72:80] = tap_total * GRAD_SCALE
-    last_copies = [
-        pltpu.make_async_remote_copy(
-            src_ref=mine, dst_ref=whole.at[d], send_sem=send_two.at[d], recv_sem=recv_two.at[d],
-            device_id=(lax.rem(lon + d, N_LON), lat), device_id_type=MESH)
-        for d in range(1, N_LON)
-    ]
-    for copy in last_copies:
-        copy.start()
-    copy_up.wait()
-    for first in range(0, NI, 4):
-        rows = [S[g, first : first + 4].reshape(256, 128) for g in range(NG)]
-        lhs = jnp.concatenate(rows, axis=1)
-
-        def back(n, carry, lhs=lhs, first=first):
-            both = jnp.dot(lhs, PM[:, pl.ds(pl.multiple_of(256 * n, 256), 256)], preferred_element_type=F32)
-            for h in range(2):
-                for m in range(4):
-                    at = 8 * (first + m) + 2 * n + h
-                    value = up[at].astype(F32) + both[64 * m : 64 * m + 64, 128 * h : 128 * h + 128]
-                    grad_input[at] = value.astype(BF16)
-            return carry
-
-        lax.fori_loop(0, 4, back, 0)
+        total += tap_parts[d]
+    tap_mine[...] = total * GRAD_SCALE
+    last_copies += spread(tap_mine, tap_whole, send_last, recv_last)
+    for g in range(NG // 2, NG):
+        shift_blocks(PS, Z, g)
+        banded_conv(Z, W, AB, S, M, g)
     for copy in last_copies:
         copy.wait()
-    total = mine[...]
+    total, tap_total = mine[...], tap_mine[...]
     for d in range(1, N_LON):
         total += whole[d]
+        tap_total += tap_whole[d]
+    total_out[0:80] = total
+    total_out[80:88] = tap_total
+
+
+def backward_conv(d_conv, fields, lon_halo, left_halo, right_halo, land, w, shares):
+    dma = pltpu.SemaphoreType.DMA
+    scratch = halo_scratch()
+    scratch.pop(11)
+    return pl.pallas_call(
+        grad_kernel,
+        name="backward_conv",
+        out_shape=(pltpu.VMEM((NG, NI, 64, 128), BF16), pltpu.VMEM((88, C), F32)),
+        in_specs=hbm(3) + vmem(5),
+        out_specs=tuple(vmem(2)),
+        scratch_shapes=scratch
+        + [
+            pltpu.VMEM((26, 4, CLAT, C), BF16),
+            pltpu.VMEM((NG, NI, ZR, 256), BF16),
+            pltpu.VMEM((2, 2, 256, 512), F32),
+            pltpu.VMEM((NG, 56, 128), F32),
+            pltpu.VMEM((128, 128), F32),
+            pltpu.VMEM((N_LAT, 8, 128), F32),
+            pltpu.VMEM((N_LAT, 80, 128), BF16),
+            pltpu.VMEM((N_LAT, 8, 128), F32),
+            pltpu.VMEM((80, 128), F32),
+            pltpu.VMEM((N_LON, 80, 128), F32),
+            pltpu.VMEM((8, 128), F32),
+            pltpu.VMEM((N_LON, 8, 128), F32),
+            dma((8,)), dma((8,)), dma((N_LAT,)), dma((N_LAT,)), dma((N_LAT,)), dma((N_LAT,)),
+            dma((N_LON,)), dma((N_LON,)), dma((N_LON,)), dma((N_LON,)), dma((4,)),
+        ],
+        compiler_params=pltpu.CompilerParams(collective_id=1, has_side_effects=True, vmem_limit_bytes=VMEM_LIMIT),
+    )(d_conv, fields, lon_halo, left_halo, right_halo, land, w, shares)
+
+
+def finish_kernel(place, S, up, total, grad_input, out_win, out_wout, out_dw, out_channel, out_bin,
+                  S_in, up_in, made, PM, load_s, load_up, store):
+    copies = []
+    for n in range(3):
+        copies.append((
+            pltpu.make_async_copy(S.at[:, pl.ds(4 * n, 4)], S_in.at[n], load_s.at[n]),
+            pltpu.make_async_copy(up.at[pl.ds(32 * n, 32)], up_in.at[n], load_up.at[n]),
+            pltpu.make_async_copy(made.at[n], grad_input.at[pl.ds(32 * n, 32)], store.at[n]),
+        ))
+        copies[n][0].start()
+        copies[n][1].start()
+    build_permutation(PM)
+    lat = place[0]
     out_win[...] = total[0:32]
     out_wout[...] = total[32:64]
     small = total[64:72]
     out_bin[...] = pltpu.roll(small, lax.rem(128 - 32 * lax.rem(lat, 4), 128), axis=1)[0:1, 0:32]
     out_channel[...] = pltpu.roll(small, lax.rem(128 - 8 * lat, 128), axis=1)[1:6, 0:8]
-    out_dw[...] = total[72:80, 0:49]
-
-
-def backward_conv(d_conv, fields, upstream, land, w, shares):
+    out_dw[...] = total[80:88, 0:49]
+    for chunk in range(3):
+        copies[chunk][0].wait()
+        copies[chunk][1].wait()
+
+        def put(n, both, chunk=chunk):
+            for m in range(4):
+                for h in range(2):
+                    at = 8 * m + 2 * n + h
+                    value = up_in[chunk, at].astype(F32) + both[64 * m : 64 * m + 64, 128 * h : 128 * h + 128]
+                    made[chunk, at] = value.astype(BF16)
+
+        ungroup(S_in.at[chunk], PM, range(4), put)
+        copies[chunk][2].start()
+    for chunk in range(3):
+        copies[chunk][2].wait()
+
+
+def finish(place, S, upstream, total):
     dma = pltpu.SemaphoreType.DMA
     return pl.pallas_call(
-        grad_kernel,
-        name="backward_conv",
+        finish_kernel,
+        name="finish",
         out_shape=(
             jax.ShapeDtypeStruct((CLON, CLAT, C), BF16),
             jax.ShapeDtypeStruct((32, C), F32),
@@ -643,25 +701,17 @@
             jax.ShapeDtypeStruct((5, 8), F32),
             jax.ShapeDtypeStruct((1, 32), F32),
         ),
-        in_specs=hbm(3) + vmem(3),
-        out_specs=tuple(vmem(6)),
-        scratch_shapes=halo_scratch(BF16)
-        + [
-            pltpu.VMEM((24, 4, CLAT, C), BF16),
-            pltpu.VMEM((CLON, CLAT, C), BF16),
-            pltpu.VMEM((NG, NI, ZR, 256), BF16),
-            pltpu.VMEM((2, 256, 512), F32),
-            pltpu.VMEM((NG, 56, 128), F32),
-            pltpu.VMEM((128, 128), F32),
-            pltpu.VMEM((N_LAT, 8, 128), F32),
-            pltpu.VMEM((N_LAT, 72, 128), F32),
-            pltpu.VMEM((N_LAT, 8, 128), F32),
-            pltpu.VMEM((80, 128), F32),
-            pltpu.VMEM((N_LON, 80, 128), F32),
-            dma((8,)), dma((8,)), dma((N_LAT,)), dma((N_LAT,)), dma((N_LAT,)), dma((N_LAT,)), dma((N_LON,)), dma((N_LON,)), dma((3,)),
+        in_specs=[pl.BlockSpec(memory_space=pltpu.SMEM)] + hbm(2) + vmem(1),
+        out_specs=tuple(hbm(1) + vmem(5)),
+        scratch_shapes=[
+            pltpu.VMEM((3, NG, 4, 64, 128), BF16),
+            pltpu.VMEM((3, 32, CLAT, C), BF16),
+            pltpu.VMEM((3, 32, CLAT, C), BF16),
+            pltpu.VMEM((1024, 1024), BF16),
+            dma((3,)), dma((3,)), dma((3,)),
         ],
-        compiler_params=pltpu.CompilerParams(collective_id=1, has_side_effects=True, vmem_limit_bytes=VMEM_LIMIT),
-    )(d_conv, fields, upstream, land, w, shares)
+        compiler_params=pltpu.CompilerParams(vmem_limit_bytes=VMEM_LIMIT),
+    )(place, S, upstream, total)
 
 
 def per_device(fields, land_sea, tile_list, upstream, dw_weight, dw_bias, ln_gain, ln_bias, w_in, b_in, w_out, b_out,
@@ -671,11 +721,13 @@
 
     fours = fields.reshape(24, 4, CLAT, C)
     land = land_sea.T
-    conv = forward_conv(fours, land, dw_weight, row(dw_bias))
+    conv, lon_halo, left_halo, right_halo = forward_conv(fours, land, dw_weight)
     mixed, d_conv, shares = listed_mlp(
-        tile_list.reshape(-1), conv, fours, upstream, land, row(ln_gain), row(ln_bias), w_in, row(b_in), w_out,
+        tile_list.reshape(-1), conv, fours, upstream, land, row(dw_bias), row(ln_gain), row(ln_bias), w_in, row(b_in), w_out,
         row(b_out), row(layer_scale))
-    grad_input, g_win, g_wout, g_dw, g_channel, g_bin = backward_conv(d_conv, fours, upstream, land, dw_weight, shares)
+    grouped, total = backward_conv(d_conv, fours, lon_halo, left_halo, right_halo, land, dw_weight, shares)
+    place = lax.axis_index("lat").astype(jnp.int32).reshape(1)
+    grad_input, g_win, g_wout, g_dw, g_channel, g_bin = finish(place, grouped, upstream, total)
     return mixed, grad_input, g_win.T, g_wout, g_dw.T, g_channel, g_bin.reshape(-1)
 
 

time: 106 us -> 75.2 us (0.71)
  Pallas kernels: 99.6 us -> 70.4 us
  local copies, waits for them, and re-layouts: 5.6 us -> 2.98 us
    pallas_call x2 -> x3, Pallas kernels: 71 us -> 51.6 us  [the longest x1 26.3 us: backward_conv(): pl.pallas_call(grad_kernel, name='backward_conv', out_shape=(pltpu.VMEM((...]
    pallas_call x1, Pallas kernels: 28.6 us -> 18.7 us  [listed_mlp(): pl.pallas_call(mlp_kernel, name='listed_mlp', out_shape=(jax.ShapeDtypeSt...]
    unnamed x16 -> x28, local copies, waits for them, and re-layouts: 5.6 us -> 2.98 us
where the time goes in v3:
time: 75.2 us; the launch traced here: 74.4 us
  Pallas kernels  70.4 us (94%)
  local copies, waits for them, and re-layouts  2.98 us (4%)
  between operations  1.02 us (1%)
    pallas_call x1, Pallas kernels, backward_conv(): pl.pallas_call(grad_kernel, name='backward_conv', out_shape=(pltpu.VMEM((...  26.3 us
    pallas_call x1, Pallas kernels, forward_conv(): pl.pallas_call(conv_kernel, name='forward_conv', out_shape=(pltpu.VMEM((T...  21.2 us
    pallas_call x1, Pallas kernels, listed_mlp(): pl.pallas_call(mlp_kernel, name='listed_mlp', out_shape=(jax.ShapeDtypeSt...  18.7 us
    pallas_call x1, Pallas kernels, finish(): pl.pallas_call(finish_kernel, name='finish', out_shape=(jax.ShapeDtypeStr...  4.1 us
    unnamed x28, local copies, waits for them, and re-layouts  2.98 us

profile of v3, /device:TPU:0, one launch (start us, length us, event | category | flops | bytes accessed | tf_op | source)
XLA Modules:
  0.0 74.4 jit_solution(11874012805286635597)
XLA Ops:
  0.6 0.0 copy-start.8
  0.6 0.0 copy-start.9
  0.7 0.0 copy-start.10
  0.7 0.0 copy-start.7
  0.7 0.0 copy-start
  0.7 1.4 %copy-done = bf16[96,64,128]{2,1,0:T(8,128)(2,1)S(1)} copy-done((bf16[96,64,128]{2,1,0:T(8,128)(2,1)S(1)}, bf16[96,64,128]{2,1,0:T(8,128)(2,1)}, u32[]{:S(2)}) %copy-start) | copy-done | bytes 1572888
  2.1 0.0 copy-start.2
  2.1 0.8 %copy-done.2 = s32[96,64]{0,1:T(8,128)S(1)} copy-done((s32[96,64]{0,1:T(8,128)S(1)}, s32[96,64]{0,1:T(8,128)}, u32[]{:S(2)}) %copy-start.2) | copy-done | bytes 24600
  2.9 0.0 copy-start.5
  2.9 0.7 %copy-done.5 = f32[49,128]{1,0:T(8,128)S(1)} copy-done((f32[49,128]{1,0:T(8,128)S(1)}, f32[49,128]{1,0:T(8,128)}, u32[]{:S(2)}) %copy-start.5) | copy-done | bytes 25112
  3.6 0.0 copy-start.3
  3.6 0.0 copy-start.4
  3.6 0.0 copy-start.11
  3.6 0.0 copy-start.12
  3.6 0.0 copy-start.13
  3.6 21.2 %forward_conv.1 = (bf16[96,64,128]{2,1,0:T(8,128)(2,1)S(1)}, bf16[2,4,64,128]{3,2,1,0:T(8,128)(2,1)S(1)}, bf16[14,32,128]{2,1,0:T(8,128)(2,1)S(1)}, bf16[14,32,128]{2,1,0:T(8,128)(2,1)S(1)}) custom-call(bf16[24,4,64,128]{3,2,1,0:T(8,128)(2,1)S(1)} %bitcast.15, s32[64,96]{1,0:T(8,128)S(1)} %bitcast.16, f32[49,128]{1,0:T(8,128)S(1)} %copy-done.5), custom_call_target="tpu_custom_call" | custom-call | tf_op jit(solution)/shard_map/forward_conv/pallas_call | solution.py:315
  24.9 0.0 copy-done.8
  24.9 0.0 copy-done.9
  24.9 0.0 copy-done.10
  24.9 0.0 copy-done.7
  24.9 0.0 copy-done.3
  24.9 0.0 copy-done.4
  24.9 0.0 copy-done.11
  24.9 0.0 copy-done.12
  24.9 0.0 copy-done.13
  24.9 0.0 copy-start.6
  25.0 18.7 %listed_mlp.1 = (bf16[96,64,128]{2,1,0:T(8,128)(2,1)}, bf16[24,4,64,128]{3,2,1,0:T(8,128)(2,1)S(1)}, bf16[16,80,128]{2,1,0:T(8,128)(2,1)S(1)}) custom-call(s32[72]{0:T(128)S(1)} %bitcast.20, bf16[96,64,128]{2,1,0:T(8,128)(2,1)S(1)} %get-tuple-element.22.conv, bf16[24,4,64,128]{3,2,1,0:T(8,128)(2,1)} %bitcast.13, bf16[96,64,128]{2,1,0:T(8,128)(2,1)} %up.1, ...), custom_call_target="tpu_custom_call" | custom-call | tf_op jit(solution)/shard_map/listed_mlp/pallas_call | solution.py:437
  43.7 0.0 copy-done.6
  43.7 0.0 copy-start.1
  43.7 26.3 %backward_conv.1 = (bf16[8,12,64,128]{3,2,1,0:T(8,128)(2,1)S(1)}, f32[88,128]{1,0:T(8,128)S(1)}) custom-call(bf16[24,4,64,128]{3,2,1,0:T(8,128)(2,1)S(1)} %get-tuple-element.24.d_conv, bf16[24,4,64,128]{3,2,1,0:T(8,128)(2,1)} %bitcast.14, bf16[2,4,64,128]{3,2,1,0:T(8,128)(2,1)S(1)} %get-tuple-element.25.lon_halo, ...), custom_call_target="tpu_custom_call" | custom-call | tf_op jit(solution)/shard_map/backward_conv/pallas_call | solution.py:628
  70.1 0.0 copy-done.1
  70.1 4.1 %finish.1 = (bf16[96,64,128]{2,1,0:T(8,128)(2,1)}, f32[32,128]{1,0:T(8,128)}, f32[32,128]{1,0:T(8,128)}, f32[8,49]{1,0:T(8,128)}, f32[5,8]{1,0:T(8,128)}, /*index=5*/f32[1,32]{1,0:T(1,128)}) custom-call(s32[1]{0:T(128)} %bitcast.9.place, bf16[8,12,64,128]{3,2,1,0:T(8,128)(2,1)S(1)} %get-tuple-element.29.S, bf16[96,64,128]{2,1,0:T(8,128)(2,1)S(1)} %copy-done.1, ...), custom_call_target="tpu_custom_call" | custom-call | tf_op jit(solution)/shard_map/finish/pallas_call | solution.py:693
Async XLA Ops:
  0.6 24.2 %copy-start.8 = (s32[1,1,72]{2,1,0:T(1,128)S(1)}, s32[1,1,72]{2,1,0:T(1,128)}, u32[]{:S(2)}) copy-start(s32[1,1,72]{2,1,0:T(1,128)} %param.15) | copy-start | bytes 868
  0.6 24.2 %copy-start.9 = (f32[128]{0:T(128)S(1)}, f32[128]{0:T(128)}, u32[]{:S(2)}) copy-start(f32[128]{0:T(128)} %param.18) | copy-start | bytes 1540
  0.7 24.2 %copy-start.10 = (f32[128]{0:T(128)S(1)}, f32[128]{0:T(128)}, u32[]{:S(2)}) copy-start(f32[128]{0:T(128)} %param.19) | copy-start | bytes 1540
  0.7 24.2 %copy-start.7 = (f32[512]{0:T(512)S(1)}, f32[512]{0:T(512)}, u32[]{:S(2)}) copy-start(f32[512]{0:T(512)} %param.22) | copy-start | bytes 6148
  0.7 1.4 %copy-start = (bf16[96,64,128]{2,1,0:T(8,128)(2,1)S(1)}, bf16[96,64,128]{2,1,0:T(8,128)(2,1)}, u32[]{:S(2)}) copy-start(bf16[96,64,128]{2,1,0:T(8,128)(2,1)} %param.13) | copy-start | bytes 4718596
  2.1 0.8 %copy-start.2 = (s32[96,64]{0,1:T(8,128)S(1)}, s32[96,64]{0,1:T(8,128)}, u32[]{:S(2)}) copy-start(s32[96,64]{0,1:T(8,128)} %param.14) | copy-start | bytes 73732
  2.9 0.7 %copy-start.5 = (f32[49,128]{1,0:T(8,128)S(1)}, f32[49,128]{1,0:T(8,128)}, u32[]{:S(2)}) copy-start(f32[49,128]{1,0:T(8,128)} %w.3) | copy-start | bytes 75268
  3.6 21.3 %copy-start.3 = (bf16[128,512]{1,0:T(8,128)(2,1)S(1)}, bf16[128,512]{1,0:T(8,128)(2,1)}, u32[]{:S(2)}) copy-start(bf16[128,512]{1,0:T(8,128)(2,1)} %w_in.1) | copy-start | bytes 393220
  3.6 21.3 %copy-start.4 = (bf16[512,128]{1,0:T(8,128)(2,1)S(1)}, bf16[512,128]{1,0:T(8,128)(2,1)}, u32[]{:S(2)}) copy-start(bf16[512,128]{1,0:T(8,128)(2,1)} %w_out.1) | copy-start | bytes 393220
  3.6 21.3 %copy-start.11 = (f32[128]{0:T(128)S(1)}, f32[128]{0:T(128)}, u32[]{:S(2)}) copy-start(f32[128]{0:T(128)} %param.20) | copy-start | bytes 1540
  3.6 21.3 %copy-start.12 = (f32[128]{0:T(128)S(1)}, f32[128]{0:T(128)}, u32[]{:S(2)}) copy-start(f32[128]{0:T(128)} %param.24) | copy-start | bytes 1540
  3.6 21.3 %copy-start.13 = (f32[128]{0:T(128)S(1)}, f32[128]{0:T(128)}, u32[]{:S(2)}) copy-start(f32[128]{0:T(128)} %param.25) | copy-start | bytes 1540
  24.9 18.8 %copy-start.6 = (f32[49,128]{1,0:T(8,128)S(1)}, f32[49,128]{1,0:T(8,128)}, u32[]{:S(2)}) copy-start(f32[49,128]{1,0:T(8,128)} %w.3) | copy-start | bytes 75268
  43.7 26.3 %copy-start.1 = (bf16[96,64,128]{2,1,0:T(8,128)(2,1)S(1)}, bf16[96,64,128]{2,1,0:T(8,128)(2,1)}, u32[]{:S(2)}) copy-start(bf16[96,64,128]{2,1,0:T(8,128)(2,1)} %up.1) | copy-start | bytes 4718596

commit v4 on v3

--- a/solution.py
+++ b/solution.py
@@ -21,9 +21,11 @@
 N_LON, N_LAT = 8, 16
 SHIFTS = (-4, -2, 0, 2)
 GRAD_SCALE = 1.0 / math.sqrt(768 * 1024)
-VMEM_LIMIT = 50 * 1024 * 1024
-ERF_COEFS = (0.7978822019328625, 0.03634471964933557, -4.4922105999092954e-05,
-             -5.0349129465290195e-05, 3.0967343000773035e-06, -6.63025075261232e-08)
+VMEM_LIMIT = 42 * 1024 * 1024
+ERF_COEFS = (0.7978697125817803, 0.03639228534613075, -8.782596074631976e-05, -3.669357312826199e-05,
+             1.4250137713525853e-06)
+PDF_SCALE = -0.5 / math.log(2.0)
+PDF_SHIFT = -0.5 * math.log2(2.0 * math.pi)
 
 
 def iota(shape, dim):
@@ -96,7 +98,7 @@
             for m in range(4):
                 pair = []
                 for i in (2 * m, 2 * m + 1):
-                    cells = X[1 + 2 * n + i // 4, i % 4, 48 * east : 48 * east + 16].astype(F32)
+                    cells = X[2 * n + i // 4, i % 4, 48 * east : 48 * east + 16].astype(F32)
                     pair.append(cells[8 * east : 8 * east + 8])
                 if east:
                     value = jnp.where(low, pltpu.roll(pair[0], 4, axis=0), pair[1])
@@ -111,14 +113,14 @@
     lax.fori_loop(0, NI, block, 0)
 
 
-def halo_copies(X, EL, ER, LH, RH, send, recv, lon, lat):
+def halo_copies(first, last, XH, EL, ER, LH, RH, send, recv, lon, lat):
     up, down = lax.rem(lon + 1, N_LON), lax.rem(lon + N_LON - 1, N_LON)
     east, west = lax.rem(lat + 1, N_LAT), lax.rem(lat + N_LAT - 1, N_LAT)
     plan = (
         (EL, RH.at[pl.ds(1, NI)], (lon, west)),
         (ER, LH.at[pl.ds(1, NI)], (lon, east)),
-        (X.at[1], X.at[25], (down, lat)),
-        (X.at[24], X.at[0], (up, lat)),
+        (first, XH.at[1], (down, lat)),
+        (last, XH.at[0], (up, lat)),
         (EL.at[0, pl.ds(0, 16)], RH.at[13, pl.ds(0, 16)], (down, west)),
         (EL.at[NI - 1, pl.ds(16, 16)], RH.at[0, pl.ds(16, 16)], (up, west)),
         (ER.at[0, pl.ds(0, 16)], LH.at[13, pl.ds(0, 16)], (down, east)),
@@ -157,6 +159,16 @@
     lax.fori_loop(0, NI + 1, block, 0)
 
 
+def padded_cells(X, XH):
+    def cells(k, i):
+        at = 2 * k + i // 4 - 1
+        if at < 0:
+            return XH[0, i]
+        return XH[1, i - 4] if at > 23 else X[at, i % 4]
+
+    return cells
+
+
 def group_blocks(cells, blocks, PM, PS, M):
     lhs = jnp.concatenate([jnp.concatenate([cells(k, i) for k in blocks], axis=0) for i in range(8)], axis=1)
 
@@ -223,14 +235,18 @@
         put(n, jnp.dot(lhs, PM[:, 256 * n : 256 * n + 256], preferred_element_type=F32))
 
 
-def conv_kernel(fields, land, w, conv_out, lon_halo, left_halo, right_halo, X, EL, ER, LH, RH, EH, PS, Z, W, PM, AB, S, M, land_pad, send, recv,
-                load):
+def conv_kernel(fields, upstream, w_in, w_out, land_far, w_far,
+                conv_out, lon_halo, left_halo, right_halo, X, near_up, near_in, near_out,
+                land, w, EX, XH, EL, ER, LH, RH, EH, PS, Z, W, PM, AB, S, M, land_pad, send, recv, load):
     lon, lat = lax.axis_index("lon"), lax.axis_index("lat")
     around = neighbours(lon, lat)
     greet(around)
-    copy_in = pltpu.make_async_copy(fields, X.at[pl.ds(1, 24)], load)
-    copy_in.start()
+    pairs = ((land_far, land), (fields, X), (w_far, w), (upstream, near_up), (w_in, near_in), (w_out, near_out))
+    loads = [pltpu.make_async_copy(far, near, load.at[n]) for n, (far, near) in enumerate(pairs)]
+    for copy in loads:
+        copy.start()
     land_pad[...] = jnp.zeros((CLAT, 128), F32)
+    loads[0].wait()
     land_pad[:, 0:CLON] = land[...].astype(F32)
     land_t = land_pad[...]
     expand_mask(with_ones(land_t), M, NI + 1)
@@ -241,29 +257,27 @@
         turned = pltpu.roll(edge, 4, axis=0)
         edge = jnp.where(low, turned, edge) if east else jnp.where(low, edge, turned)
         masks.append(jnp.where(low, edge, pltpu.roll(edge, 127, axis=1)))
-    copy_in.wait()
+    loads[1].wait()
     pack_edges(X, EL, ER, masks)
-    for at, first in ((1, 0), (24, CLON - 4)):
+    for at, first in ((0, 0), (23, CLON - 4)):
         for i in range(4):
             keep = jnp.broadcast_to(land_t[:, first + i : first + i + 1], (CLAT, C))
-            X[at, i] = (X[at, i].astype(F32) * keep).astype(BF16)
+            EX[at // 23, i] = (X[at, i].astype(F32) * keep).astype(BF16)
     greeted(around)
-    copies = halo_copies(X, EL, ER, LH, RH, send, recv, lon, lat)
+    copies = halo_copies(EX.at[0], EX.at[1], XH, EL, ER, LH, RH, send, recv, lon, lat)
     for copy in copies:
         copy.start()
     build_permutation(PM)
     clear_margins(PS)
-
-    def cells(k, i):
-        return X[2 * k + i // 4, i % 4]
+    cells = padded_cells(X, XH)
 
     for blocks in INNER:
         group_blocks(cells, blocks, PM, PS, M)
+    loads[2].wait()
     build_weights(w, W, False)
     for copy in copies:
         copy.wait()
-    lon_halo[0] = X[0]
-    lon_halo[1] = X[25]
+    lon_halo[...] = XH[...]
     left_halo[...] = LH[...]
     right_halo[...] = RH[...]
     group_blocks(cells, (0, NI), PM, PS, M)
@@ -281,6 +295,8 @@
                     conv_out[(first + m) * NJ + t, 16 * n : 16 * n + 16] = value.astype(BF16)
 
         ungroup(S, PM, range(first, first + 4), put)
+    for copy in loads[3:]:
+        copy.wait()
 
 
 def vmem(n):
@@ -293,7 +309,7 @@
 
 def halo_scratch():
     return [
-        pltpu.VMEM((26, 4, CLAT, C), BF16),
+        pltpu.VMEM((2, 4, CLAT, C), BF16),
         pltpu.VMEM((NI, 32, C), BF16),
         pltpu.VMEM((NI, 32, C), BF16),
         pltpu.VMEM((14, 32, C), BF16),
@@ -310,7 +326,7 @@
     ]
 
 
-def forward_conv(fields, land, w):
+def forward_conv(fields, upstream, w_in, w_out, land, w):
     dma = pltpu.SemaphoreType.DMA
     return pl.pallas_call(
         conv_kernel,
@@ -320,12 +336,22 @@
             pltpu.VMEM((2, 4, CLAT, C), BF16),
             pltpu.VMEM((14, 32, C), BF16),
             pltpu.VMEM((14, 32, C), BF16),
+            pltpu.VMEM((24, 4, CLAT, C), BF16),
+            pltpu.VMEM((CLON, CLAT, C), BF16),
+            pltpu.VMEM((C, FF), BF16),
+            pltpu.VMEM((FF, C), BF16),
         ),
-        in_specs=hbm(1) + vmem(2),
-        out_specs=tuple(vmem(4)),
-        scratch_shapes=halo_scratch() + [dma((8,)), dma((8,)), dma],
+        in_specs=hbm(6),
+        out_specs=tuple(vmem(8)),
+        scratch_shapes=[
+            pltpu.VMEM((CLAT, CLON), jnp.int32),
+            pltpu.VMEM((49, C), F32),
+            pltpu.VMEM((2, 4, CLAT, C), BF16),
+        ]
+        + halo_scratch()
+        + [dma((8,)), dma((8,)), dma((6,))],
         compiler_params=pltpu.CompilerParams(collective_id=0, has_side_effects=True, vmem_limit_bytes=VMEM_LIMIT),
-    )(fields, land, w)
+    )(fields, upstream, w_in, w_out, land, w)
 
 
 def normal_cdf(h, square):
@@ -336,11 +362,9 @@
 
 
 def mlp_kernel(tile_ids, conv, fields, upstream, land, offset, gain, shift, w_in, b_in, w_out, b_out, scale,
-               mixed, d_conv_out, shares, branch, d_conv, w_in_t, w_out_t, g_in, g_out, g_bin, sums, land_tr, own, load):
+               mixed, d_conv_out, shares, branch, d_conv, w_in_t, w_out_t, g_in, g_out, g_bin, sums, land_tr, mixed_part, store):
     slots = 18
     rows = slots * 64
-    copy_in = pltpu.make_async_copy(fields, own, load)
-    copy_in.start()
     land_tr[...] = jnp.zeros((CLAT, 128), F32)
     land_tr[:, 0:CLON] = land[...].astype(F32)
     w_in_t[...] = w_in[...].astype(F32).T.astype(BF16)
@@ -374,9 +398,8 @@
         normed = center * inv_std
         normed_b = (normed * gain_row + shift_row).astype(BF16)
         hidden = jnp.dot(normed_b, w_in[...], preferred_element_type=F32) + b_in[...]
-        bounded = jnp.clip(hidden, -5.0, 5.0)
-        square = bounded * bounded
-        cdf = normal_cdf(bounded, square)
+        square = hidden * hidden
+        cdf = normal_cdf(hidden, square)
         activated = (hidden * cdf).astype(BF16)
         output = jnp.dot(activated, w_out[...], preferred_element_type=F32) + b_out[...]
         gate = active * scale_row
@@ -384,7 +407,7 @@
         d_out = gate * up
         d_out_b = d_out.astype(BF16)
         g_out[...] += lax.dot_general(d_out_b, activated, (((0,), (0,)), ((), ())), preferred_element_type=F32)
-        pdf = jnp.exp(-0.5 * (hidden * hidden)) * (1.0 / math.sqrt(2.0 * math.pi))
+        pdf = jnp.exp2(square * PDF_SCALE + PDF_SHIFT)
         d_hidden = jnp.dot(d_out_b, w_out_t[...], preferred_element_type=F32) * (cdf + hidden * pdf)
         d_hidden_b = d_hidden.astype(BF16)
         g_in[...] += lax.dot_general(normed_b, d_hidden_b, (((0,), (0,)), ((), ())), preferred_element_type=F32)
@@ -399,27 +422,30 @@
         for k, term in enumerate((d_cells, d_norm * normed, d_norm, d_out, active * output * up)):
             sums[k] += jnp.sum(term.reshape(rows // 8, 8, C), axis=0)
         for q in range(slots):
-
-            @pl.when(ids[q] >= 0)
-            def _(q=q):
-                branch[tiles[q]] = branch_rows[64 * q : 64 * q + 64]
-                d_conv[tiles[q]] = d_cells[64 * q : 64 * q + 64]
+            to = jnp.where(ids[q] >= 0, ids[q], TILES)
+            branch[to] = branch_rows[64 * q : 64 * q + 64]
+            d_conv[to] = d_cells[64 * q : 64 * q + 64]
 
         return carry
 
     lax.fori_loop(0, TCAP // slots, step, 0)
 
-    copy_in.wait()
-
-    def mix(n, carry):
-        for i in range(8):
-            rows_i = jnp.concatenate([branch[n * NJ + t, 8 * i : 8 * i + 8] for t in range(NJ)], axis=0)
-            mixed[8 * n + i] = (own[2 * n + i // 4, i % 4].astype(F32) + rows_i).astype(BF16)
-            rows_i = jnp.concatenate([d_conv[n * NJ + t, 8 * i : 8 * i + 8] for t in range(NJ)], axis=0)
-            d_conv_out[2 * n + i // 4, i % 4] = rows_i.astype(BF16)
-        return carry
-
-    lax.fori_loop(0, NI, mix, 0)
+    stores = [
+        pltpu.make_async_copy(mixed_part.at[n], mixed.at[pl.ds(32 * n, 32)], store.at[n]) for n in range(3)
+    ]
+    for chunk in range(3):
+
+        def mix(n, carry, chunk=chunk):
+            for i in range(8):
+                rows_i = jnp.concatenate([branch[n * NJ + t, 8 * i : 8 * i + 8] for t in range(NJ)], axis=0)
+                total = fields[2 * n + i // 4, i % 4].astype(F32) + rows_i
+                mixed_part[chunk, 8 * (n - 4 * chunk) + i] = total.astype(BF16)
+                rows_i = jnp.concatenate([d_conv[n * NJ + t, 8 * i : 8 * i + 8] for t in range(NJ)], axis=0)
+                d_conv_out[2 * n + i // 4, i % 4] = rows_i.astype(BF16)
+            return carry
+
+        lax.fori_loop(4 * chunk, 4 * chunk + 4, mix, 0)
+        stores[chunk].start()
     bin_row = jnp.sum(g_bin[...], axis=0, keepdims=True)
     tail = jnp.concatenate([jnp.sum(sums[k], axis=0, keepdims=True) for k in range(5)], axis=0)
     for n in range(4):
@@ -431,6 +457,8 @@
             shares[q, 32:64] = turned_out[32 * m : 32 * m + 32].astype(BF16)
             rest = [bin_row[:, 128 * n : 128 * n + 128], tail, jnp.zeros((10, 128), F32)]
             shares[q, 64:80] = jnp.concatenate(rest, axis=0).astype(BF16)
+    for copy in stores:
+        copy.wait()
 
 
 def listed_mlp(tile_ids, conv, fields, upstream, land, offset, gain, shift, w_in, b_in, w_out, b_out, scale):
@@ -442,11 +470,11 @@
             pltpu.VMEM((24, 4, CLAT, C), BF16),
             pltpu.VMEM((N_LAT, 80, 128), BF16),
         ),
-        in_specs=[pl.BlockSpec(memory_space=pltpu.SMEM)] + vmem(1) + hbm(1) + vmem(10),
-        out_specs=tuple(vmem(3)),
+        in_specs=[pl.BlockSpec(memory_space=pltpu.SMEM)] + vmem(12),
+        out_specs=tuple(hbm(1) + vmem(2)),
         scratch_shapes=[
-            pltpu.VMEM((TILES, 64, C), F32),
-            pltpu.VMEM((TILES, 64, C), F32),
+            pltpu.VMEM((TILES + 1, 64, C), F32),
+            pltpu.VMEM((TILES + 1, 64, C), F32),
             pltpu.VMEM((FF, C), BF16),
             pltpu.VMEM((C, FF), BF16),
             pltpu.VMEM((C, FF), F32),
@@ -454,8 +482,8 @@
             pltpu.VMEM((8, FF), F32),
             pltpu.VMEM((5, 8, C), F32),
             pltpu.VMEM((CLAT, 128), F32),
-            pltpu.VMEM((24, 4, CLAT, C), BF16),
-            pltpu.SemaphoreType.DMA,
+            pltpu.VMEM((3, 32, CLAT, C), BF16),
+            pltpu.SemaphoreType.DMA((3,)),
         ],
         compiler_params=pltpu.CompilerParams(vmem_limit_bytes=VMEM_LIMIT),
     )(tile_ids, conv, fields, upstream, land, offset, gain, shift, w_in, b_in, w_out, b_out, scale)
@@ -511,27 +539,16 @@
 
 def grad_kernel(d_conv, fields, lon_halo, left_halo, right_halo, land, w, shares,
                 S, total_out,
-                X, EL, ER, LH, RH, EH, PS, Z, W, PM, AB, M, land_pad,
-                own, MP, G, taps, square, tap_shares, parts, tap_parts, mine, whole, tap_mine, tap_whole,
-                send, recv, send_one, recv_one, send_tap, recv_tap, send_two, recv_two, send_last, recv_last, load):
+                XH, EL, ER, LH, RH, EH, PS, Z, W, PM, AB, M, land_pad, MP, G, taps, square, tap_shares, parts, tap_parts, mine, whole, tap_mine, tap_whole,
+                send, recv, send_one, recv_one, send_tap, recv_tap, send_two, recv_two, send_last, recv_last):
     lon, lat = lax.axis_index("lon"), lax.axis_index("lat")
     around = neighbours(lon, lat)
     around += [(lon, lax.rem(lat + d, N_LAT)) for d in range(2, N_LAT - 1)]
     around += [(lax.rem(lon + d, N_LON), lat) for d in range(2, N_LON - 1)]
     greet(around)
-    copy_in = pltpu.make_async_copy(d_conv, X.at[pl.ds(1, 24)], load.at[0])
-    copies_own = [
-        pltpu.make_async_copy(fields, own.at[pl.ds(1, 24)], load.at[1]),
-        pltpu.make_async_copy(lon_halo.at[0], own.at[0], load.at[2]),
-        pltpu.make_async_copy(lon_halo.at[1], own.at[25], load.at[3]),
-    ]
-    copy_in.start()
-    for copy in copies_own:
-        copy.start()
-    copy_in.wait()
-    pack_edges(X, EL, ER, None)
+    pack_edges(d_conv, EL, ER, None)
     greeted(around)
-    copies = halo_copies(X, EL, ER, LH, RH, send, recv, lon, lat)
+    copies = halo_copies(d_conv.at[0], d_conv.at[23], XH, EL, ER, LH, RH, send, recv, lon, lat)
     for copy in copies:
         copy.start()
     share_copies, tap_copies = [], []
@@ -551,16 +568,15 @@
     land_pad[:, 0:CLON] = land[...].astype(F32)
     land_t = land_pad[...]
     expand_mask(with_ones(land_t), M, NI + 1)
-    for copy in copies_own:
-        copy.wait()
+    cells = padded_cells(fields, lon_halo)
     for blocks in INNER + ((0, NI),):
-        group_blocks(lambda k, i: own[2 * k + i // 4, i % 4], blocks, PM, PS, M)
+        group_blocks(cells, blocks, PM, PS, M)
     group_halos(left_halo, right_halo, EH, PM, PS, lat)
     for g in range(NG):
         shift_blocks(PS, Z, g)
     clear_margins(PS)
     for blocks in ((0, 1, 2, 3), (4, 5, 6, 7), (8, 9, 10, 11)):
-        group_blocks(lambda k, i: X[1 + 2 * k + i // 4, i % 4], blocks, PM, PS, None)
+        group_blocks(lambda k, i: d_conv[2 * k + i // 4, i % 4], blocks, PM, PS, None)
     pair_rows(PS, MP)
     for g in range(NG):
         tap_gradients(Z, MP, G, taps, (g,))
@@ -569,10 +585,7 @@
         copy.start()
     build_weights(w, W, True)
     expand_mask(land_t, M, NI)
-
-    def cells(k, i):
-        return X[2 * k + i // 4, i % 4]
-
+    cells = padded_cells(d_conv, XH)
     for blocks in INNER:
         group_blocks(cells, blocks, PM, PS, None)
     for copy in copies:
@@ -629,11 +642,10 @@
         grad_kernel,
         name="backward_conv",
         out_shape=(pltpu.VMEM((NG, NI, 64, 128), BF16), pltpu.VMEM((88, C), F32)),
-        in_specs=hbm(3) + vmem(5),
+        in_specs=vmem(8),
         out_specs=tuple(vmem(2)),
         scratch_shapes=scratch
         + [
-            pltpu.VMEM((26, 4, CLAT, C), BF16),
             pltpu.VMEM((NG, NI, ZR, 256), BF16),
             pltpu.VMEM((2, 2, 256, 512), F32),
             pltpu.VMEM((NG, 56, 128), F32),
@@ -646,23 +658,17 @@
             pltpu.VMEM((8, 128), F32),
             pltpu.VMEM((N_LON, 8, 128), F32),
             dma((8,)), dma((8,)), dma((N_LAT,)), dma((N_LAT,)), dma((N_LAT,)), dma((N_LAT,)),
-            dma((N_LON,)), dma((N_LON,)), dma((N_LON,)), dma((N_LON,)), dma((4,)),
+            dma((N_LON,)), dma((N_LON,)), dma((N_LON,)), dma((N_LON,)),
         ],
         compiler_params=pltpu.CompilerParams(collective_id=1, has_side_effects=True, vmem_limit_bytes=VMEM_LIMIT),
     )(d_conv, fields, lon_halo, left_halo, right_halo, land, w, shares)
 
 
 def finish_kernel(place, S, up, total, grad_input, out_win, out_wout, out_dw, out_channel, out_bin,
-                  S_in, up_in, made, PM, load_s, load_up, store):
-    copies = []
-    for n in range(3):
-        copies.append((
-            pltpu.make_async_copy(S.at[:, pl.ds(4 * n, 4)], S_in.at[n], load_s.at[n]),
-            pltpu.make_async_copy(up.at[pl.ds(32 * n, 32)], up_in.at[n], load_up.at[n]),
-            pltpu.make_async_copy(made.at[n], grad_input.at[pl.ds(32 * n, 32)], store.at[n]),
-        ))
-        copies[n][0].start()
-        copies[n][1].start()
+                  made, PM, store):
+    copies = [
+        pltpu.make_async_copy(made.at[n], grad_input.at[pl.ds(32 * n, 32)], store.at[n]) for n in range(3)
+    ]
     build_permutation(PM)
     lat = place[0]
     out_win[...] = total[0:32]
@@ -672,20 +678,18 @@
     out_channel[...] = pltpu.roll(small, lax.rem(128 - 8 * lat, 128), axis=1)[1:6, 0:8]
     out_dw[...] = total[80:88, 0:49]
     for chunk in range(3):
-        copies[chunk][0].wait()
-        copies[chunk][1].wait()
 
         def put(n, both, chunk=chunk):
             for m in range(4):
                 for h in range(2):
                     at = 8 * m + 2 * n + h
-                    value = up_in[chunk, at].astype(F32) + both[64 * m : 64 * m + 64, 128 * h : 128 * h + 128]
+                    value = up[32 * chunk + at].astype(F32) + both[64 * m : 64 * m + 64, 128 * h : 128 * h + 128]
                     made[chunk, at] = value.astype(BF16)
 
-        ungroup(S_in.at[chunk], PM, range(4), put)
-        copies[chunk][2].start()
-    for chunk in range(3):
-        copies[chunk][2].wait()
+        ungroup(S, PM, range(4 * chunk, 4 * chunk + 4), put)
+        copies[chunk].start()
+    for copy in copies:
+        copy.wait()
 
 
 def finish(place, S, upstream, total):
@@ -701,14 +705,12 @@
             jax.ShapeDtypeStruct((5, 8), F32),
             jax.ShapeDtypeStruct((1, 32), F32),
         ),
-        in_specs=[pl.BlockSpec(memory_space=pltpu.SMEM)] + hbm(2) + vmem(1),
+        in_specs=[pl.BlockSpec(memory_space=pltpu.SMEM)] + vmem(3),
         out_specs=tuple(hbm(1) + vmem(5)),
         scratch_shapes=[
-            pltpu.VMEM((3, NG, 4, 64, 128), BF16),
-            pltpu.VMEM((3, 32, CLAT, C), BF16),
             pltpu.VMEM((3, 32, CLAT, C), BF16),
             pltpu.VMEM((1024, 1024), BF16),
-            dma((3,)), dma((3,)), dma((3,)),
+            dma((3,)),
         ],
         compiler_params=pltpu.CompilerParams(vmem_limit_bytes=VMEM_LIMIT),
     )(place, S, upstream, total)
@@ -721,13 +723,14 @@
 
     fours = fields.reshape(24, 4, CLAT, C)
     land = land_sea.T
-    conv, lon_halo, left_halo, right_halo = forward_conv(fours, land, dw_weight)
+    far = [pltpu.with_memory_space_constraint(v, pltpu.HBM) for v in (fours, upstream, w_in, w_out, land, dw_weight)]
+    conv, lon_halo, left_halo, right_halo, near_fours, near_up, near_in, near_out = forward_conv(*far)
     mixed, d_conv, shares = listed_mlp(
-        tile_list.reshape(-1), conv, fours, upstream, land, row(dw_bias), row(ln_gain), row(ln_bias), w_in, row(b_in), w_out,
+        tile_list.reshape(-1), conv, near_fours, near_up, land, row(dw_bias), row(ln_gain), row(ln_bias), near_in, row(b_in), near_out,
         row(b_out), row(layer_scale))
-    grouped, total = backward_conv(d_conv, fours, lon_halo, left_halo, right_halo, land, dw_weight, shares)
+    grouped, total = backward_conv(d_conv, near_fours, lon_halo, left_halo, right_halo, land, dw_weight, shares)
     place = lax.axis_index("lat").astype(jnp.int32).reshape(1)
-    grad_input, g_win, g_wout, g_dw, g_channel, g_bin = finish(place, grouped, upstream, total)
+    grad_input, g_win, g_wout, g_dw, g_channel, g_bin = finish(place, grouped, near_up, total)
     return mixed, grad_input, g_win.T, g_wout, g_dw.T, g_channel, g_bin.reshape(-1)
 
 

time: 75.2 us -> 67.6 us (0.90)
  Pallas kernels: 70.4 us -> 66 us
  local copies, waits for them, and re-layouts: 2.98 us -> 0.04 us
    pallas_call x1, Pallas kernels: 18.7 us -> 15.1 us  [listed_mlp(): pl.pallas_call(mlp_kernel, name='listed_mlp', out_shape=(jax.ShapeDtypeSt...]
    unnamed x28 -> x18, local copies, waits for them, and re-layouts: 2.98 us -> 0.04 us
where the time goes in v4:
time: 67.6 us; the launch traced here: 67 us
  Pallas kernels  66 us (98%)
  between operations  0.97 us (1%)
    pallas_call x1, Pallas kernels, backward_conv(): pl.pallas_call(grad_kernel, name='backward_conv', out_shape=(pltpu.VMEM((...  26.1 us
    pallas_call x1, Pallas kernels, forward_conv(): pl.pallas_call(conv_kernel, name='forward_conv', out_shape=(pltpu.VMEM((T...  21.3 us
    pallas_call x1, Pallas kernels, listed_mlp(): pl.pallas_call(mlp_kernel, name='listed_mlp', out_shape=(jax.ShapeDtypeSt...  15.1 us
    pallas_call x1, Pallas kernels, finish(): pl.pallas_call(finish_kernel, name='finish', out_shape=(jax.ShapeDtypeStr...  3.42 us

profile of v4, /device:TPU:0, one launch (start us, length us, event | category | flops | bytes accessed | tf_op | source)
XLA Modules:
  0.0 67.0 jit_solution(2198449085585678604)
XLA Ops:
  0.6 0.0 copy-start
  0.6 0.0 copy-start.2
  0.7 0.0 copy-start.3
  0.7 0.0 copy-start.4
  0.7 0.0 copy-start.5
  0.7 0.0 copy-start.6
  0.7 0.0 copy-start.7
  0.7 0.0 copy-start.8
  0.7 21.3 %forward_conv.1 = (bf16[96,64,128]{2,1,0:T(8,128)(2,1)S(1)}, bf16[2,4,64,128]{3,2,1,0:T(8,128)(2,1)S(1)}, bf16[14,32,128]{2,1,0:T(8,128)(2,1)S(1)}, bf16[14,32,1...) custom-call(bf16[24,4,64,128]{3,2,1,0:T(8,128)(2,1)} %bitcast.23, ...), custom_call_target="tpu_custom_call" | custom-call | tf_op jit(solution)/shard_map/forward_conv/pallas_call | solution.py:331
  22.1 0.0 copy-done
  22.1 0.0 copy-done.2
  22.1 0.0 copy-done.3
  22.1 0.0 copy-done.4
  22.1 0.0 copy-done.5
  22.1 0.0 copy-done.6
  22.1 0.0 copy-done.7
  22.1 0.0 copy-done.8
  22.1 0.0 copy-start.1
  22.2 15.1 %listed_mlp.1 = (bf16[96,64,128]{2,1,0:T(8,128)(2,1)}, bf16[24,4,64,128]{3,2,1,0:T(8,128)(2,1)S(1)}, bf16[16,80,128]{2,1,0:T(8,128)(2,1)S(1)}) custom-call(s32[72]{0:T(128)S(1)} %bitcast.17, bf16[96,64,128]{2,1,0:T(8,128)(2,1)S(1)} %get-tuple-element.26.conv, bf16[24,4,64,128]{3,2,1,0:T(8,128)(2,1)S(1)} %get-tuple-element.27.fields, ...), custom_call_target="tpu_custom_call" | custom-call | tf_op jit(solution)/shard_map/listed_mlp/pallas_call | solution.py:465
  37.3 0.0 copy-done.1
  37.3 26.1 %backward_conv.1 = (bf16[8,12,64,128]{3,2,1,0:T(8,128)(2,1)S(1)}, f32[88,128]{1,0:T(8,128)S(1)}) custom-call(bf16[24,4,64,128]{3,2,1,0:T(8,128)(2,1)S(1)} %get-tuple-element.32.d_conv, bf16[24,4,64,128]{3,2,1,0:T(8,128)(2,1)S(1)} %get-tuple-element.27.fields, bf16[2,4,64,128]{3,2,1,0:T(8,128)(2,1)S(1)} %get-tuple-element.33.lon_halo, ...), custom_call_target="tpu_custom_call" | custom-call | tf_op jit(solution)/shard_map/backward_conv/pallas_call | solution.py:641
  63.4 3.4 %finish.1 = (bf16[96,64,128]{2,1,0:T(8,128)(2,1)}, f32[32,128]{1,0:T(8,128)}, f32[32,128]{1,0:T(8,128)}, f32[8,49]{1,0:T(8,128)}, f32[5,8]{1,0:T(8,128)}, /*index=5*/f32[1,32]{1,0:T(1,128)}) custom-call(s32[1]{0:T(128)} %bitcast.9.place, bf16[8,12,64,128]{3,2,1,0:T(8,128)(2,1)S(1)} %get-tuple-element.37.S, ...), custom_call_target="tpu_custom_call" | custom-call | tf_op jit(solution)/shard_map/finish/pallas_call | solution.py:697
Async XLA Ops:
  0.6 21.4 %copy-start = (s32[96,64]{0,1:T(8,128)S(1)}, s32[96,64]{0,1:T(8,128)}, u32[]{:S(2)}) copy-start(s32[96,64]{0,1:T(8,128)} %param.14) | copy-start | bytes 73732
  0.6 21.4 %copy-start.2 = (f32[512]{0:T(512)S(1)}, f32[512]{0:T(512)}, u32[]{:S(2)}) copy-start(f32[512]{0:T(512)} %param.22) | copy-start | bytes 6148
  0.7 21.4 %copy-start.3 = (s32[1,1,72]{2,1,0:T(1,128)S(1)}, s32[1,1,72]{2,1,0:T(1,128)}, u32[]{:S(2)}) copy-start(s32[1,1,72]{2,1,0:T(1,128)} %param.15) | copy-start | bytes 868
  0.7 21.4 %copy-start.4 = (f32[128]{0:T(128)S(1)}, f32[128]{0:T(128)}, u32[]{:S(2)}) copy-start(f32[128]{0:T(128)} %param.18) | copy-start | bytes 1540
  0.7 21.4 %copy-start.5 = (f32[128]{0:T(128)S(1)}, f32[128]{0:T(128)}, u32[]{:S(2)}) copy-start(f32[128]{0:T(128)} %param.19) | copy-start | bytes 1540
  0.7 21.4 %copy-start.6 = (f32[128]{0:T(128)S(1)}, f32[128]{0:T(128)}, u32[]{:S(2)}) copy-start(f32[128]{0:T(128)} %param.20) | copy-start | bytes 1540
  0.7 21.4 %copy-start.7 = (f32[128]{0:T(128)S(1)}, f32[128]{0:T(128)}, u32[]{:S(2)}) copy-start(f32[128]{0:T(128)} %param.24) | copy-start | bytes 1540
  0.7 21.4 %copy-start.8 = (f32[128]{0:T(128)S(1)}, f32[128]{0:T(128)}, u32[]{:S(2)}) copy-start(f32[128]{0:T(128)} %param.25) | copy-start | bytes 1540
  22.1 15.1 %copy-start.1 = (f32[49,128]{1,0:T(8,128)S(1)}, f32[49,128]{1,0:T(8,128)}, u32[]{:S(2)}) copy-start(f32[49,128]{1,0:T(8,128)} %w.1) | copy-start | bytes 75268

commit v5 on v4

--- a/solution.py
+++ b/solution.py
@@ -21,7 +21,7 @@
 N_LON, N_LAT = 8, 16
 SHIFTS = (-4, -2, 0, 2)
 GRAD_SCALE = 1.0 / math.sqrt(768 * 1024)
-VMEM_LIMIT = 42 * 1024 * 1024
+VMEM_LIMIT = 34 * 1024 * 1024
 ERF_COEFS = (0.7978697125817803, 0.03639228534613075, -8.782596074631976e-05, -3.669357312826199e-05,
              1.4250137713525853e-06)
 PDF_SCALE = -0.5 / math.log(2.0)
@@ -236,8 +236,8 @@
 
 
 def conv_kernel(fields, upstream, w_in, w_out, land_far, w_far,
-                conv_out, lon_halo, left_halo, right_halo, X, near_up, near_in, near_out,
-                land, w, EX, XH, EL, ER, LH, RH, EH, PS, Z, W, PM, AB, S, M, land_pad, send, recv, load):
+                conv_out, Z, X, near_up, near_in, near_out,
+                land, w, EX, XH, EL, ER, LH, RH, EH, PS, W, PM, AB, S, M, land_pad, send, recv, load):
     lon, lat = lax.axis_index("lon"), lax.axis_index("lat")
     around = neighbours(lon, lat)
     greet(around)
@@ -277,9 +277,6 @@
     build_weights(w, W, False)
     for copy in copies:
         copy.wait()
-    lon_halo[...] = XH[...]
-    left_halo[...] = LH[...]
-    right_halo[...] = RH[...]
     group_blocks(cells, (0, NI), PM, PS, M)
     group_halos(LH, RH, EH, PM, PS, lat)
     for g in range(NG):
@@ -316,7 +313,6 @@
         pltpu.VMEM((14, 32, C), BF16),
         pltpu.VMEM((7, 16, 1024), BF16),
         pltpu.VMEM((NG, NI + 1, 104, 128), F32),
-        pltpu.VMEM((NG, NI + 1, ZR, 512), BF16),
         pltpu.VMEM((NG, 1024, 256), BF16),
         pltpu.VMEM((1024, 1024), BF16),
         pltpu.VMEM((2, NI * ZR, 128), F32),
@@ -333,16 +329,14 @@
         name="forward_conv",
         out_shape=(
             pltpu.VMEM((TILES, 64, C), BF16),
-            pltpu.VMEM((2, 4, CLAT, C), BF16),
-            pltpu.VMEM((14, 32, C), BF16),
-            pltpu.VMEM((14, 32, C), BF16),
+            pltpu.VMEM((NG, NI + 1, ZR, 512), BF16),
             pltpu.VMEM((24, 4, CLAT, C), BF16),
             pltpu.VMEM((CLON, CLAT, C), BF16),
             pltpu.VMEM((C, FF), BF16),
             pltpu.VMEM((FF, C), BF16),
         ),
         in_specs=hbm(6),
-        out_specs=tuple(vmem(8)),
+        out_specs=tuple(vmem(6)),
         scratch_shapes=[
             pltpu.VMEM((CLAT, CLON), jnp.int32),
             pltpu.VMEM((49, C), F32),
@@ -537,9 +531,10 @@
         tap_shares[q] = turned[8 * q : 8 * q + 8]
 
 
-def grad_kernel(d_conv, fields, lon_halo, left_halo, right_halo, land, w, shares,
+def grad_kernel(d_conv, ZM, land, w, shares,
                 S, total_out,
-                XH, EL, ER, LH, RH, EH, PS, Z, W, PM, AB, M, land_pad, MP, G, taps, square, tap_shares, parts, tap_parts, mine, whole, tap_mine, tap_whole,
+                XH, EL, ER, LH, RH, EH, PS, W, PM, AB, M, land_pad,
+                Z, MP, G, taps, square, tap_shares, parts, tap_parts, mine, whole, tap_mine, tap_whole,
                 send, recv, send_one, recv_one, send_tap, recv_tap, send_two, recv_two, send_last, recv_last):
     lon, lat = lax.axis_index("lon"), lax.axis_index("lat")
     around = neighbours(lon, lat)
@@ -547,6 +542,12 @@
     around += [(lax.rem(lon + d, N_LON), lat) for d in range(2, N_LON - 1)]
     greet(around)
     pack_edges(d_conv, EL, ER, None)
+    build_permutation(PM)
+    clear_margins(PS)
+    build_weights(w, W, True)
+    land_pad[...] = jnp.zeros((CLAT, 128), F32)
+    land_pad[:, 0:CLON] = land[...].astype(F32)
+    expand_mask(land_pad[...], M, NI)
     greeted(around)
     copies = halo_copies(d_conv.at[0], d_conv.at[23], XH, EL, ER, LH, RH, send, recv, lon, lat)
     for copy in copies:
@@ -562,29 +563,14 @@
             device_id=(lon, to), device_id_type=MESH))
     for copy in share_copies:
         copy.start()
-    build_permutation(PM)
-    clear_margins(PS)
-    land_pad[...] = jnp.zeros((CLAT, 128), F32)
-    land_pad[:, 0:CLON] = land[...].astype(F32)
-    land_t = land_pad[...]
-    expand_mask(with_ones(land_t), M, NI + 1)
-    cells = padded_cells(fields, lon_halo)
-    for blocks in INNER + ((0, NI),):
-        group_blocks(cells, blocks, PM, PS, M)
-    group_halos(left_halo, right_halo, EH, PM, PS, lat)
-    for g in range(NG):
-        shift_blocks(PS, Z, g)
-    clear_margins(PS)
     for blocks in ((0, 1, 2, 3), (4, 5, 6, 7), (8, 9, 10, 11)):
         group_blocks(lambda k, i: d_conv[2 * k + i // 4, i % 4], blocks, PM, PS, None)
     pair_rows(PS, MP)
     for g in range(NG):
-        tap_gradients(Z, MP, G, taps, (g,))
+        tap_gradients(ZM, MP, G, taps, (g,))
     gather_taps(taps, square, tap_shares)
     for copy in tap_copies:
         copy.start()
-    build_weights(w, W, True)
-    expand_mask(land_t, M, NI)
     cells = padded_cells(d_conv, XH)
     for blocks in INNER:
         group_blocks(cells, blocks, PM, PS, None)
@@ -611,7 +597,7 @@
         return made
 
     last_copies = spread(mine, whole, send_two, recv_two)
-    for g in range(NG // 2):
+    for g in range(2):
         shift_blocks(PS, Z, g)
         banded_conv(Z, W, AB, S, M, g)
     for copy in tap_copies:
@@ -621,7 +607,7 @@
         total += tap_parts[d]
     tap_mine[...] = total * GRAD_SCALE
     last_copies += spread(tap_mine, tap_whole, send_last, recv_last)
-    for g in range(NG // 2, NG):
+    for g in range(2, NG):
         shift_blocks(PS, Z, g)
         banded_conv(Z, W, AB, S, M, g)
     for copy in last_copies:
@@ -634,18 +620,19 @@
     total_out[80:88] = tap_total
 
 
-def backward_conv(d_conv, fields, lon_halo, left_halo, right_halo, land, w, shares):
+def backward_conv(d_conv, shifted, land, w, shares):
     dma = pltpu.SemaphoreType.DMA
     scratch = halo_scratch()
-    scratch.pop(11)
+    scratch.pop(10)
     return pl.pallas_call(
         grad_kernel,
         name="backward_conv",
         out_shape=(pltpu.VMEM((NG, NI, 64, 128), BF16), pltpu.VMEM((88, C), F32)),
-        in_specs=vmem(8),
+        in_specs=vmem(5),
         out_specs=tuple(vmem(2)),
         scratch_shapes=scratch
         + [
+            pltpu.VMEM((NG, NI + 1, ZR, 512), BF16),
             pltpu.VMEM((NG, NI, ZR, 256), BF16),
             pltpu.VMEM((2, 2, 256, 512), F32),
             pltpu.VMEM((NG, 56, 128), F32),
@@ -661,7 +648,7 @@
             dma((N_LON,)), dma((N_LON,)), dma((N_LON,)), dma((N_LON,)),
         ],
         compiler_params=pltpu.CompilerParams(collective_id=1, has_side_effects=True, vmem_limit_bytes=VMEM_LIMIT),
-    )(d_conv, fields, lon_halo, left_halo, right_halo, land, w, shares)
+    )(d_conv, shifted, land, w, shares)
 
 
 def finish_kernel(place, S, up, total, grad_input, out_win, out_wout, out_dw, out_channel, out_bin,
@@ -724,11 +711,11 @@
     fours = fields.reshape(24, 4, CLAT, C)
     land = land_sea.T
     far = [pltpu.with_memory_space_constraint(v, pltpu.HBM) for v in (fours, upstream, w_in, w_out, land, dw_weight)]
-    conv, lon_halo, left_halo, right_halo, near_fours, near_up, near_in, near_out = forward_conv(*far)
+    conv, shifted, near_fours, near_up, near_in, near_out = forward_conv(*far)
     mixed, d_conv, shares = listed_mlp(
         tile_list.reshape(-1), conv, near_fours, near_up, land, row(dw_bias), row(ln_gain), row(ln_bias), near_in, row(b_in), near_out,
         row(b_out), row(layer_scale))
-    grouped, total = backward_conv(d_conv, near_fours, lon_halo, left_halo, right_halo, land, dw_weight, shares)
+    grouped, total = backward_conv(d_conv, shifted, land, dw_weight, shares)
     place = lax.axis_index("lat").astype(jnp.int32).reshape(1)
     grad_input, g_win, g_wout, g_dw, g_channel, g_bin = finish(place, grouped, near_up, total)
     return mixed, grad_input, g_win.T, g_wout, g_dw.T, g_channel, g_bin.reshape(-1)

time: 67.6 us -> 64.5 us (0.954)
  Pallas kernels: 66 us -> 62.6 us
    pallas_call x1, Pallas kernels: 26.1 us -> 22.8 us  [backward_conv(): pl.pallas_call(grad_kernel, name='backward_conv', out_shape=(pltpu.VMEM((...]
where the time goes in v5:
time: 64.5 us; the launch traced here: 63.6 us
  Pallas kernels  62.6 us (97%)
  between operations  0.99 us (2%)
    pallas_call x1, Pallas kernels, backward_conv(): pl.pallas_call(grad_kernel, name='backward_conv', out_shape=(pltpu.VMEM((...  22.8 us
    pallas_call x1, Pallas kernels, forward_conv(): pl.pallas_call(conv_kernel, name='forward_conv', out_shape=(pltpu.VMEM((T...  21.3 us
    pallas_call x1, Pallas kernels, listed_mlp(): pl.pallas_call(mlp_kernel, name='listed_mlp', out_shape=(jax.ShapeDtypeSt...  15.1 us
    pallas_call x1, Pallas kernels, finish(): pl.pallas_call(finish_kernel, name='finish', out_shape=(jax.ShapeDtypeStr...  3.42 us

profile of v5, /device:TPU:0, one launch (start us, length us, event | category | flops | bytes accessed | tf_op | source)
XLA Modules:
  0.0 63.6 jit_solution(17923117279200491821)
XLA Ops:
  0.6 0.0 copy-start
  0.6 0.0 copy-start.2
  0.7 0.0 copy-start.3
  0.7 0.0 copy-start.4
  0.7 0.0 copy-start.5
  0.7 0.0 copy-start.6
  0.7 0.0 copy-start.7
  0.7 0.0 copy-start.8
  0.7 21.3 %forward_conv.1 = (bf16[96,64,128]{2,1,0:T(8,128)(2,1)S(1)}, bf16[8,13,80,512]{3,2,1,0:T(8,128)(2,1)S(1)}, bf16[24,4,64,128]{3,2,1,0:T(8,128)(2,1)S(1)}, bf16[96...) custom-call(bf16[24,4,64,128]{3,2,1,0:T(8,128)(2,1)} %bitcast.23, ...), custom_call_target="tpu_custom_call" | custom-call | tf_op jit(solution)/shard_map/forward_conv/pallas_call | solution.py:327
  22.0 0.0 copy-done
  22.1 0.0 copy-done.2
  22.1 0.0 copy-done.3
  22.1 0.0 copy-done.4
  22.1 0.0 copy-done.5
  22.1 0.0 copy-done.6
  22.1 0.0 copy-done.7
  22.1 0.0 copy-done.8
  22.1 0.0 copy-start.1
  22.1 15.1 %listed_mlp.1 = (bf16[96,64,128]{2,1,0:T(8,128)(2,1)}, bf16[24,4,64,128]{3,2,1,0:T(8,128)(2,1)S(1)}, bf16[16,80,128]{2,1,0:T(8,128)(2,1)S(1)}) custom-call(s32[72]{0:T(128)S(1)} %bitcast.17, bf16[96,64,128]{2,1,0:T(8,128)(2,1)S(1)} %get-tuple-element.24.conv, bf16[24,4,64,128]{3,2,1,0:T(8,128)(2,1)S(1)} %get-tuple-element.25.fields, ...), custom_call_target="tpu_custom_call" | custom-call | tf_op jit(solution)/shard_map/listed_mlp/pallas_call | solution.py:459
  37.2 0.0 copy-done.1
  37.2 22.8 %backward_conv.1 = (bf16[8,12,64,128]{3,2,1,0:T(8,128)(2,1)S(1)}, f32[88,128]{1,0:T(8,128)S(1)}) custom-call(bf16[24,4,64,128]{3,2,1,0:T(8,128)(2,1)S(1)} %get-tuple-element.30.d_conv, bf16[8,13,80,512]{3,2,1,0:T(8,128)(2,1)S(1)} %get-tuple-element.31.ZM, s32[64,96]{1,0:T(8,128)S(1)} %bitcast.15, f32[49,128]{1,0:T(8,128)S(1)} %copy-done.1, ...), custom_call_target="tpu_custom_call" | custom-call | tf_op jit(solution)/shard_map/backward_conv/pallas_call | solution.py:627
  60.0 3.4 %finish.1 = (bf16[96,64,128]{2,1,0:T(8,128)(2,1)}, f32[32,128]{1,0:T(8,128)}, f32[32,128]{1,0:T(8,128)}, f32[8,49]{1,0:T(8,128)}, f32[5,8]{1,0:T(8,128)}, /*index=5*/f32[1,32]{1,0:T(1,128)}) custom-call(s32[1]{0:T(128)} %bitcast.9.place, bf16[8,12,64,128]{3,2,1,0:T(8,128)(2,1)S(1)} %get-tuple-element.33.S, ...), custom_call_target="tpu_custom_call" | custom-call | tf_op jit(solution)/shard_map/finish/pallas_call | solution.py:684
Async XLA Ops:
  0.6 21.4 %copy-start = (s32[96,64]{0,1:T(8,128)S(1)}, s32[96,64]{0,1:T(8,128)}, u32[]{:S(2)}) copy-start(s32[96,64]{0,1:T(8,128)} %param.14) | copy-start | bytes 73732
  0.6 21.4 %copy-start.2 = (f32[512]{0:T(512)S(1)}, f32[512]{0:T(512)}, u32[]{:S(2)}) copy-start(f32[512]{0:T(512)} %param.22) | copy-start | bytes 6148
  0.7 21.4 %copy-start.3 = (s32[1,1,72]{2,1,0:T(1,128)S(1)}, s32[1,1,72]{2,1,0:T(1,128)}, u32[]{:S(2)}) copy-start(s32[1,1,72]{2,1,0:T(1,128)} %param.15) | copy-start | bytes 868
  0.7 21.4 %copy-start.4 = (f32[128]{0:T(128)S(1)}, f32[128]{0:T(128)}, u32[]{:S(2)}) copy-start(f32[128]{0:T(128)} %param.18) | copy-start | bytes 1540
  0.7 21.4 %copy-start.5 = (f32[128]{0:T(128)S(1)}, f32[128]{0:T(128)}, u32[]{:S(2)}) copy-start(f32[128]{0:T(128)} %param.19) | copy-start | bytes 1540
  0.7 21.4 %copy-start.6 = (f32[128]{0:T(128)S(1)}, f32[128]{0:T(128)}, u32[]{:S(2)}) copy-start(f32[128]{0:T(128)} %param.20) | copy-start | bytes 1540
  0.7 21.4 %copy-start.7 = (f32[128]{0:T(128)S(1)}, f32[128]{0:T(128)}, u32[]{:S(2)}) copy-start(f32[128]{0:T(128)} %param.24) | copy-start | bytes 1540
  0.7 21.4 %copy-start.8 = (f32[128]{0:T(128)S(1)}, f32[128]{0:T(128)}, u32[]{:S(2)}) copy-start(f32[128]{0:T(128)} %param.25) | copy-start | bytes 1540
  22.1 15.1 %copy-start.1 = (f32[49,128]{1,0:T(8,128)S(1)}, f32[49,128]{1,0:T(8,128)}, u32[]{:S(2)}) copy-start(f32[49,128]{1,0:T(8,128)} %w.1) | copy-start | bytes 75268

commit v6 on v5

--- a/solution.py
+++ b/solution.py
@@ -583,7 +583,7 @@
     total = shares[lat].astype(F32)
     for d in range(1, N_LAT):
         total += parts[d].astype(F32)
-    mine[...] = total * GRAD_SCALE
+    mine[...] = (total * GRAD_SCALE).astype(BF16)
 
     def spread(block, parts, send_sem, recv_sem):
         made = [
@@ -612,9 +612,9 @@
         banded_conv(Z, W, AB, S, M, g)
     for copy in last_copies:
         copy.wait()
-    total, tap_total = mine[...], tap_mine[...]
+    total, tap_total = mine[...].astype(F32), tap_mine[...]
     for d in range(1, N_LON):
-        total += whole[d]
+        total += whole[d].astype(F32)
         tap_total += tap_whole[d]
     total_out[0:80] = total
     total_out[80:88] = tap_total
@@ -640,8 +640,8 @@
             pltpu.VMEM((N_LAT, 8, 128), F32),
             pltpu.VMEM((N_LAT, 80, 128), BF16),
             pltpu.VMEM((N_LAT, 8, 128), F32),
-            pltpu.VMEM((80, 128), F32),
-            pltpu.VMEM((N_LON, 80, 128), F32),
+            pltpu.VMEM((80, 128), BF16),
+            pltpu.VMEM((N_LON, 80, 128), BF16),
             pltpu.VMEM((8, 128), F32),
             pltpu.VMEM((N_LON, 8, 128), F32),
             dma((8,)), dma((8,)), dma((N_LAT,)), dma((N_LAT,)), dma((N_LAT,)), dma((N_LAT,)),

time: 64.5 us -> 63.1 us (0.978)
  Pallas kernels: 62.6 us -> 61.8 us
    pallas_call x1, Pallas kernels: 22.8 us -> 21.9 us  [backward_conv(): pl.pallas_call(grad_kernel, name='backward_conv', out_shape=(pltpu.VMEM((...]
where the time goes in v6:
time: 63.1 us; the launch traced here: 62.8 us
  Pallas kernels  61.8 us (98%)
  between operations  0.99 us (2%)
    pallas_call x1, Pallas kernels, backward_conv(): pl.pallas_call(grad_kernel, name='backward_conv', out_shape=(pltpu.VMEM((...  21.9 us
    pallas_call x1, Pallas kernels, forward_conv(): pl.pallas_call(conv_kernel, name='forward_conv', out_shape=(pltpu.VMEM((T...  21.3 us
    pallas_call x1, Pallas kernels, listed_mlp(): pl.pallas_call(mlp_kernel, name='listed_mlp', out_shape=(jax.ShapeDtypeSt...  15.1 us
    pallas_call x1, Pallas kernels, finish(): pl.pallas_call(finish_kernel, name='finish', out_shape=(jax.ShapeDtypeStr...  3.42 us

profile of v6, /device:TPU:0, one launch (start us, length us, event | category | flops | bytes accessed | tf_op | source)
XLA Modules:
  0.0 62.8 jit_solution(16636297079318687672)
XLA Ops:
  0.6 0.0 copy-start
  0.6 0.0 copy-start.2
  0.7 0.0 copy-start.3
  0.7 0.0 copy-start.4
  0.7 0.0 copy-start.5
  0.7 0.0 copy-start.6
  0.7 0.0 copy-start.7
  0.7 0.0 copy-start.8
  0.7 21.3 %forward_conv.1 = (bf16[96,64,128]{2,1,0:T(8,128)(2,1)S(1)}, bf16[8,13,80,512]{3,2,1,0:T(8,128)(2,1)S(1)}, bf16[24,4,64,128]{3,2,1,0:T(8,128)(2,1)S(1)}, bf16[96...) custom-call(bf16[24,4,64,128]{3,2,1,0:T(8,128)(2,1)} %bitcast.23, ...), custom_call_target="tpu_custom_call" | custom-call | tf_op jit(solution)/shard_map/forward_conv/pallas_call | solution.py:327
  22.0 0.0 copy-done
  22.1 0.0 copy-done.2
  22.1 0.0 copy-done.3
  22.1 0.0 copy-done.4
  22.1 0.0 copy-done.5
  22.1 0.0 copy-done.6
  22.1 0.0 copy-done.7
  22.1 0.0 copy-done.8
  22.1 0.0 copy-start.1
  22.1 15.1 %listed_mlp.1 = (bf16[96,64,128]{2,1,0:T(8,128)(2,1)}, bf16[24,4,64,128]{3,2,1,0:T(8,128)(2,1)S(1)}, bf16[16,80,128]{2,1,0:T(8,128)(2,1)S(1)}) custom-call(s32[72]{0:T(128)S(1)} %bitcast.17, bf16[96,64,128]{2,1,0:T(8,128)(2,1)S(1)} %get-tuple-element.24.conv, bf16[24,4,64,128]{3,2,1,0:T(8,128)(2,1)S(1)} %get-tuple-element.25.fields, ...), custom_call_target="tpu_custom_call" | custom-call | tf_op jit(solution)/shard_map/listed_mlp/pallas_call | solution.py:459
  37.2 0.0 copy-done.1
  37.3 21.9 %backward_conv.1 = (bf16[8,12,64,128]{3,2,1,0:T(8,128)(2,1)S(1)}, f32[88,128]{1,0:T(8,128)S(1)}) custom-call(bf16[24,4,64,128]{3,2,1,0:T(8,128)(2,1)S(1)} %get-tuple-element.30.d_conv, bf16[8,13,80,512]{3,2,1,0:T(8,128)(2,1)S(1)} %get-tuple-element.31.ZM, s32[64,96]{1,0:T(8,128)S(1)} %bitcast.15, f32[49,128]{1,0:T(8,128)S(1)} %copy-done.1, ...), custom_call_target="tpu_custom_call" | custom-call | tf_op jit(solution)/shard_map/backward_conv/pallas_call | solution.py:627
  59.2 3.4 %finish.1 = (bf16[96,64,128]{2,1,0:T(8,128)(2,1)}, f32[32,128]{1,0:T(8,128)}, f32[32,128]{1,0:T(8,128)}, f32[8,49]{1,0:T(8,128)}, f32[5,8]{1,0:T(8,128)}, /*index=5*/f32[1,32]{1,0:T(1,128)}) custom-call(s32[1]{0:T(128)} %bitcast.9.place, bf16[8,12,64,128]{3,2,1,0:T(8,128)(2,1)S(1)} %get-tuple-element.33.S, ...), custom_call_target="tpu_custom_call" | custom-call | tf_op jit(solution)/shard_map/finish/pallas_call | solution.py:684
Async XLA Ops:
  0.6 21.4 %copy-start = (s32[96,64]{0,1:T(8,128)S(1)}, s32[96,64]{0,1:T(8,128)}, u32[]{:S(2)}) copy-start(s32[96,64]{0,1:T(8,128)} %param.14) | copy-start | bytes 73732
  0.6 21.4 %copy-start.2 = (f32[512]{0:T(512)S(1)}, f32[512]{0:T(512)}, u32[]{:S(2)}) copy-start(f32[512]{0:T(512)} %param.22) | copy-start | bytes 6148
  0.7 21.4 %copy-start.3 = (s32[1,1,72]{2,1,0:T(1,128)S(1)}, s32[1,1,72]{2,1,0:T(1,128)}, u32[]{:S(2)}) copy-start(s32[1,1,72]{2,1,0:T(1,128)} %param.15) | copy-start | bytes 868
  0.7 21.4 %copy-start.4 = (f32[128]{0:T(128)S(1)}, f32[128]{0:T(128)}, u32[]{:S(2)}) copy-start(f32[128]{0:T(128)} %param.18) | copy-start | bytes 1540
  0.7 21.4 %copy-start.5 = (f32[128]{0:T(128)S(1)}, f32[128]{0:T(128)}, u32[]{:S(2)}) copy-start(f32[128]{0:T(128)} %param.19) | copy-start | bytes 1540
  0.7 21.4 %copy-start.6 = (f32[128]{0:T(128)S(1)}, f32[128]{0:T(128)}, u32[]{:S(2)}) copy-start(f32[128]{0:T(128)} %param.20) | copy-start | bytes 1540
  0.7 21.4 %copy-start.7 = (f32[128]{0:T(128)S(1)}, f32[128]{0:T(128)}, u32[]{:S(2)}) copy-start(f32[128]{0:T(128)} %param.24) | copy-start | bytes 1540
  0.7 21.4 %copy-start.8 = (f32[128]{0:T(128)S(1)}, f32[128]{0:T(128)}, u32[]{:S(2)}) copy-start(f32[128]{0:T(128)} %param.25) | copy-start | bytes 1540
  22.1 15.1 %copy-start.1 = (f32[49,128]{1,0:T(8,128)S(1)}, f32[49,128]{1,0:T(8,128)}, u32[]{:S(2)}) copy-start(f32[49,128]{1,0:T(8,128)} %w.1) | copy-start | bytes 75268
